TPU v7x, 256 devices: a whole 4x4x8 slice. The times are simulated.
256 devices in a mesh: grp: 8 (over y, x_hi), seq: 32 (over x_lo, z, core).
Axes of the slice: x: 4 (x_hi: 2, x_lo: 2; x = x_hi * 2 + x_lo), y: 4, z: 8, core: 2. Of those that a mesh axis runs over, the one named last changes fastest.
Arguments:
- gate_in: bfloat16 [32768, 4096], P(('grp', 'seq')), parts along dimension 0, may hold values from -6 to 6
- value_in: bfloat16 [32768, 4096], P(('grp', 'seq')), parts along dimension 0, may hold values from -6 to 6
- gate_out: bfloat16 [32768, 4096], P(('grp', 'seq')), parts along dimension 0, may hold values from -6 to 6
- cotangent: bfloat16 [32768, 4096], P(('grp', 'seq')), parts along dimension 0, may hold values from -3 to 3
- long_filter: float32 [4096, 4096], P(None, 'seq'), may hold values from -1.1 to 1.1
- short_filters: float32 [3, 3, 4096], replicated, may hold values from -3 to 3
Outputs:
- mixed: bfloat16 [32768, 4096], P(('grp', 'seq')), parts along dimension 0
- grad_gate_in: bfloat16 [32768, 4096], P(('grp', 'seq')), parts along dimension 0
- grad_value: bfloat16 [32768, 4096], P(('grp', 'seq')), parts along dimension 0
- grad_gate_out: bfloat16 [32768, 4096], P(('grp', 'seq')), parts along dimension 0
- grad_long: float32 [32768, 4096], P('grp', 'seq'), parts along dimension 0
- grad_short: float32 [24, 3, 4096], P('grp'), parts along dimension 0
There are 8 independent parts, one for each index of `grp`. A program takes and returns all parts, laid end to end along the dimension named above; an argument that names none is the same for every part. Nothing has to cross between parts.
All inputs are finite; a program needn't handle non-finite values.
Results may differ from a plain program's by a relative error of at most 0.02.
Values may be sent and summed in bfloat16 or wider, within the bound.
No kernel may reach another device: no remote copies, remote signals or barrier semaphores. Data moves between devices by JAX's collectives and lax.ppermute only.
A program may use at most 256 MiB of HBM per device.

v0:
```python
import math

import jax
import jax.numpy as jnp
from jax import lax
from jax.sharding import PartitionSpec as P

exact_dots = lax.Precision.HIGHEST
split_dots = lax.Precision.HIGH


def factor_pair(length):
    second_len = 1
    while length % (second_len * 2) == 0 and second_len * 2 * (second_len * 2) <= 2 * length:
        second_len = second_len * 2
    return (2 * length // second_len, second_len)


def spectrum(source, first_len, second_len, accuracy):
    half_len = first_len // 2
    channels = source.shape[1]
    blocks = source.astype(jnp.float32).reshape(half_len, second_len, channels)
    row_a = lax.broadcasted_iota(jnp.int32, (first_len, half_len), 0)
    col_b = lax.broadcasted_iota(jnp.int32, (first_len, half_len), 1)
    turns = (row_a * col_b % first_len).astype(jnp.float32) * (2.0 * math.pi / first_len)
    first_table = jnp.stack([jnp.cos(turns), -jnp.sin(turns)], axis=1)
    section = jnp.einsum("arb,bnc->arnc", first_table, blocks, precision=accuracy)
    full_len = first_len * second_len
    idx_a = lax.broadcasted_iota(jnp.int32, (first_len, second_len, second_len), 0)
    idx_m = lax.broadcasted_iota(jnp.int32, (first_len, second_len, second_len), 1)
    idx_n = lax.broadcasted_iota(jnp.int32, (first_len, second_len, second_len), 2)
    phase = ((idx_a * idx_n + first_len * idx_m * idx_n) % full_len).astype(jnp.float32) * (
        2.0 * math.pi / full_len
    )
    cos_w = jnp.cos(phase)
    sin_w = jnp.sin(phase)
    mixer = jnp.stack(
        [jnp.stack([cos_w, sin_w], axis=2), jnp.stack([-sin_w, cos_w], axis=2)], axis=1
    )
    return jnp.einsum("asmrn,arnc->asmc", mixer, section, precision=accuracy)


def inverse_spec(spec, first_len, second_len, both_parts):
    half_len = first_len // 2
    channels = spec.shape[3]
    full_len = first_len * second_len
    idx_a = lax.broadcasted_iota(jnp.int32, (first_len, second_len, second_len), 0)
    idx_n = lax.broadcasted_iota(jnp.int32, (first_len, second_len, second_len), 1)
    idx_m = lax.broadcasted_iota(jnp.int32, (first_len, second_len, second_len), 2)
    phase = ((idx_a * idx_n + first_len * idx_m * idx_n) % full_len).astype(jnp.float32) * (
        2.0 * math.pi / full_len
    )
    cos_w = jnp.cos(phase)
    sin_w = jnp.sin(phase)
    mixer = jnp.stack(
        [jnp.stack([cos_w, -sin_w], axis=2), jnp.stack([sin_w, cos_w], axis=2)], axis=1
    )
    section = jnp.einsum("asnrm,armc->asnc", mixer, spec, precision=exact_dots)
    row_b = lax.broadcasted_iota(jnp.int32, (half_len, first_len), 0)
    col_a = lax.broadcasted_iota(jnp.int32, (half_len, first_len), 1)
    turns = (row_b * col_a % first_len).astype(jnp.float32) * (2.0 * math.pi / first_len)
    cos_f = jnp.cos(turns)
    sin_f = jnp.sin(turns)
    real_table = jnp.stack([cos_f, -sin_f], axis=2)
    if both_parts:
        imag_table = jnp.stack([sin_f, cos_f], axis=2)
        tables = jnp.stack([real_table, imag_table], axis=0)
        result = jnp.einsum("sbar,arnc->sbnc", tables, section, precision=exact_dots)
        return (result * (1.0 / full_len)).reshape(2, half_len * second_len, channels)
    result = jnp.einsum("bar,arnc->bnc", real_table, section, precision=exact_dots)
    return (result * (1.0 / full_len)).reshape(half_len * second_len, channels)


def short_causal(extended, taps, count):
    return (
        taps[0] * extended[2 : 2 + count]
        + taps[1] * extended[1 : 1 + count]
        + taps[2] * extended[0:count]
    )


def short_adjoint(extended, taps, count):
    return (
        taps[0] * extended[0:count]
        + taps[1] * extended[1 : 1 + count]
        + taps[2] * extended[2 : 2 + count]
    )


def tap_sums(grad_rows, extended, count):
    return jnp.stack(
        [
            jnp.sum(grad_rows * extended[2 - lag_rows : 2 - lag_rows + count], axis=0)
            for lag_rows in range(3)
        ],
        axis=0,
    )


def gate_inputs(ext_gate, ext_value, ext_out, cotangent, taps, count):
    feat_gate = short_causal(ext_gate, taps[0], count).astype(jnp.bfloat16)
    feat_value = short_causal(ext_value, taps[1], count).astype(jnp.bfloat16)
    feat_out = short_causal(ext_out, taps[2], count).astype(jnp.bfloat16)
    signal = (feat_gate.astype(jnp.float32) * feat_value.astype(jnp.float32)).astype(jnp.bfloat16)
    outer_grad = (feat_out.astype(jnp.float32) * cotangent.astype(jnp.float32)).astype(jnp.bfloat16)
    return ((feat_gate, feat_value, feat_out), signal, outer_grad)


def gate_grads(conv_rows, sig_rows, feats, cotangent):
    feat_gate, feat_value, feat_out = feats
    conv_float = conv_rows.astype(jnp.float32)
    mixed = (feat_out.astype(jnp.float32) * conv_float).astype(jnp.bfloat16)
    out_feat_grad = (cotangent.astype(jnp.float32) * conv_float).astype(jnp.bfloat16)
    sig_float = sig_rows.astype(jnp.float32)
    gate_feat_grad = (sig_float * feat_value.astype(jnp.float32)).astype(jnp.bfloat16)
    value_feat_grad = (sig_float * feat_gate.astype(jnp.float32)).astype(jnp.bfloat16)
    return (mixed, (gate_feat_grad, value_feat_grad, out_feat_grad))


def adjoint_all(feat_grads, heads, extendeds, taps, count):
    results = []
    partials = []
    for which in range(3):
        grad_rows = feat_grads[which].astype(jnp.float32)
        after = jnp.concatenate([grad_rows, heads[which].astype(jnp.float32)], axis=0)
        results.append(short_adjoint(after, taps[which], count).astype(jnp.bfloat16))
        partials.append(tap_sums(grad_rows, extendeds[which], count))
    return (results, jnp.stack(partials, axis=0))


def forward_conv(signal, filter_chan):
    seq_len = signal.shape[0]
    first_len, second_len = factor_pair(seq_len)
    signal_spec = spectrum(signal, first_len, second_len, split_dots)
    filter_spec = spectrum(filter_chan, first_len, second_len, exact_dots)
    sig_re = signal_spec[:, 0]
    sig_im = signal_spec[:, 1]
    fil_re = filter_spec[:, 0]
    fil_im = filter_spec[:, 1]
    conv_spec = jnp.stack(
        [sig_re * fil_re - sig_im * fil_im, sig_re * fil_im + sig_im * fil_re], axis=1
    )
    conv_out = inverse_spec(conv_spec, first_len, second_len, False).astype(jnp.bfloat16)
    return ((signal_spec, filter_spec), conv_out)


def backward_conv(moved_grad, spectra):
    seq_len = moved_grad.shape[0]
    first_len, second_len = factor_pair(seq_len)
    signal_spec, filter_spec = spectra
    grad_spec = spectrum(moved_grad, first_len, second_len, split_dots)
    sig_re = signal_spec[:, 0]
    sig_im = signal_spec[:, 1]
    fil_re = filter_spec[:, 0]
    fil_im = filter_spec[:, 1]
    grd_re = grad_spec[:, 0]
    grd_im = grad_spec[:, 1]
    inner_re = fil_re * grd_re + fil_im * grd_im
    inner_im = fil_re * grd_im - fil_im * grd_re
    outer_re = sig_re * grd_re + sig_im * grd_im
    outer_im = sig_re * grd_im - sig_im * grd_re
    joined = jnp.stack([inner_re - outer_im, inner_im + outer_re], axis=1)
    both = inverse_spec(joined, first_len, second_len, True)
    return (both[0].astype(jnp.bfloat16), both[1])


def local(gate_in, value_in, gate_out, cotangent, long_filter, short_filters):
    channels_here = long_filter.shape[1]
    taps_chan = lax.dynamic_slice_in_dim(
        short_filters, lax.axis_index("seq") * channels_here, channels_here, 2
    )
    moved_gate, moved_value, moved_out, moved_cot = (
        lax.all_to_all(gate_in, "seq", split_axis=1, concat_axis=0, tiled=True),
        lax.all_to_all(value_in, "seq", split_axis=1, concat_axis=0, tiled=True),
        lax.all_to_all(gate_out, "seq", split_axis=1, concat_axis=0, tiled=True),
        lax.all_to_all(cotangent, "seq", split_axis=1, concat_axis=0, tiled=True),
    )
    seq_len = moved_gate.shape[0]
    zero_rows = jnp.zeros((2, channels_here), jnp.float32)
    ext_gate = jnp.concatenate([zero_rows, moved_gate.astype(jnp.float32)], axis=0)
    ext_value = jnp.concatenate([zero_rows, moved_value.astype(jnp.float32)], axis=0)
    ext_out = jnp.concatenate([zero_rows, moved_out.astype(jnp.float32)], axis=0)
    feats, signal, outer_grad = gate_inputs(
        ext_gate, ext_value, ext_out, moved_cot, taps_chan, seq_len
    )
    spectra, conv_out = forward_conv(signal, long_filter)
    back_grad, grad_long = backward_conv(outer_grad, spectra)
    mixed_chan, feat_grads = gate_grads(conv_out, back_grad, feats, moved_cot)
    zero_heads = jnp.zeros((2, channels_here), jnp.bfloat16)
    grads, short_part = adjoint_all(
        feat_grads,
        (zero_heads, zero_heads, zero_heads),
        (ext_gate, ext_value, ext_out),
        taps_chan,
        seq_len,
    )
    mixed, grad_gate_in, grad_value, grad_gate_out = (
        lax.all_to_all(mixed_chan, "seq", split_axis=0, concat_axis=1, tiled=True),
        lax.all_to_all(grads[0], "seq", split_axis=0, concat_axis=1, tiled=True),
        lax.all_to_all(grads[1], "seq", split_axis=0, concat_axis=1, tiled=True),
        lax.all_to_all(grads[2], "seq", split_axis=0, concat_axis=1, tiled=True),
    )
    grad_short = lax.all_gather(short_part, "seq", axis=2, tiled=True)
    return (mixed, grad_gate_in, grad_value, grad_gate_out, grad_long, grad_short)


def solution(mesh):
    placed = (
        P(("grp", "seq"), None),
        P(("grp", "seq"), None),
        P(("grp", "seq"), None),
        P(("grp", "seq"), None),
        P(None, "seq"),
        P(),
    )
    return jax.shard_map(
        local,
        mesh=mesh,
        in_specs=placed,
        out_specs=(
            P(("grp", "seq"), None),
            P(("grp", "seq"), None),
            P(("grp", "seq"), None),
            P(("grp", "seq"), None),
            P("grp", "seq"),
            P("grp", None, None),
        ),
        check_vma=False,
    )
```

profile of v0, /device:TPU:8, one launch (start us, length us, event | category | flops | bytes accessed | tf_op | source)
XLA Modules:
  0.0 478.3 jit_solution(3740904334034919334)
XLA Ops:
  0.7 2.4 copy.21
  3.1 9.8 %all-to-all-start.1 = ((bf16[128,32,128]{0,2,1:T(8,128)(2,1)}), bf16[128,32,128]{0,2,1:T(8,128)(2,1)S(1)}, u32[]{:S(2)}, u32[]{:S(2)}) async-start(bf16[128,32,128]{0,2,1:T(8,128)(2,1)} %bitcast.15), calls=%async_computation.1 | async-start | bytes 2097152 | tf_op jit(solution)/shard_map/all_to_all | solution.py:173
  14.6 26.6 %all-to-all-done.1 = bf16[128,32,128]{0,2,1:T(8,128)(2,1)S(1)} async-done(((bf16[128,32,128]{0,2,1:T(8,128)(2,1)}), bf16[128,32,128]{0,2,1:T(8,128)(2,1)S(1)}, u32[]{:S(2)}, u32[]{:S(2)}) %all-to-all-start.1) | async-done | bytes 1048608 | tf_op jit(solution)/shard_map/all_to_all | solution.py:173
  41.2 4.1 all-to-all-start.2
  46.6 2.3 copy.33
  48.9 11.2 %convolution_bitcast_fusion.2 = f32[128,2,64,128,1]{3,0,2,1,4:T(8,128)} fusion(f32[64,64,128]{2,1,0:T(8,128)} %bitcast.202, f32[128,1,64]{0,2,1:T(8,128)S(1)} %get-tuple-element.57, f32[128,1,64]{0,2,1:T(8,128)S(1)} %get-tuple-element.58), kind=kOutput, calls=%fused_computation.46 | convolution fusion | flops 1610629120 | bytes 10551296 | tf_op jit(solution)/shard_map/arb,bnc->arnc/dot_general | solution.py:27
  60.1 35.2 %fusion.57 = (f32[128,64,1,64]{3,1,2,0:T(8,128)}, f32[128,64,1,64]{3,1,2,0:T(8,128)S(1)}, f32[128,64,1,64]{3,1,2,0:T(8,128)}, f32[128,64,1,64]{3,1,2,0:T(8,128)S...) fusion(s32[64]{0:T(128)S(1)} %iota_multiply_fusion), kind=kLoop, calls=%fused_computation.99 | loop fusion | flops 16777216 | bytes 12583168 | tf_op jit(solution)/shard_map/neg | solution.py:56
  95.4 6.9 %maximum_bitcast_fusion.2 = (f32[128,1,64,2,64]{4,2,3,1,0:T(8,128)}, f32[128,1,64,2,64]{4,2,3,1,0:T(8,128)}) fusion(f32[128,64,1,64]{3,1,2,0:T(8,128)S(1)} %get-tuple-element.54, f32[128,64,1,64]{3,1,2,0:T(8,128)S(1)} %get-tuple-element.55, f32[128,64,1,64]{3,1,2,0:T(8,128)S(1)} %get-tuple-element.52), kind=kLoop, calls=%fused_computation.11 | loop fusion | flops 2097152 | bytes 14680064 | tf_op jit(solution)/shard_map/stack | solution.py:37
  102.3 8.5 %all-to-all-start = ((bf16[128,32,128]{0,2,1:T(8,128)(2,1)}), bf16[128,32,128]{0,2,1:T(8,128)(2,1)S(1)}, u32[]{:S(2)}, u32[]{:S(2)}) async-start(bf16[128,32,128]{0,2,1:T(8,128)(2,1)} %bitcast.1), calls=%async_computation | async-start | bytes 2097152 | tf_op jit(solution)/shard_map/all_to_all | solution.py:175
  111.7 12.7 %maximum_bitcast_fusion = (f32[128,1,64,2,64]{4,2,3,0,1:T(8,128)}, f32[128,1,64,2,64]{4,2,3,0,1:T(8,128)}) fusion(f32[128,64,1,64]{3,1,2,0:T(8,128)} %get-tuple-element.51, f32[128,64,1,64]{3,1,2,0:T(8,128)} %get-tuple-element.56, f32[128,64,1,64]{3,1,2,0:T(8,128)} %get-tuple-element.53), kind=kLoop, calls=%fused_computation.9 | loop fusion | flops 2097152 | bytes 14680064 | tf_op jit(solution)/shard_map/stack | solution.py:55
  124.4 26.1 %fusion.28 = f32[128,2,64,128]{3,2,1,0:T(8,128)} fusion(f32[128,2,64,128,1]{3,0,2,1,4:T(8,128)} %convolution_bitcast_fusion.2, f32[128,1,64,2,64]{4,2,3,1,0:T(8,128)} %get-tuple-element.34, f32[128,1,64,2,64]{4,2,3,1,0:T(8,128)S(1)} %bitcast.179), kind=kOutput, calls=%fused_computation.48 | convolution fusion | flops 3223322624 | bytes 25165824 | tf_op jit(solution)/shard_map/asmrn,arnc->asmc/dot_general | solution.py:40
  150.6 2.8 convert_bitcast_fusion.2
  153.3 2.3 copy.22
  155.7 3.5 convert_bitcast_fusion.1
  159.2 2.9 copy.24
  162.1 8.6 %all-to-all-start.4 = ((bf16[128,32,128]{0,2,1:T(8,128)(2,1)}), bf16[128,32,128]{0,2,1:T(8,128)(2,1)}, u32[]{:S(2)}, u32[]{:S(2)}) async-start(bf16[128,32,128]{0,2,1:T(8,128)(2,1)} %bitcast.192), calls=%async_computation.4 | async-start | bytes 2097152 | tf_op jit(solution)/shard_map/all_to_all | solution.py:176
  172.3 2.9 copy.19
  175.2 5.8 %fusion.49 = (bf16[4096,128]{1,0:T(8,128)(2,1)S(1)}, bf16[4096,128]{1,0:T(8,128)(2,1)}, bf16[4096,128]{1,0:T(8,128)(2,1)}) fusion(f32[128]{0:T(128)S(1)} %get-tuple-element.42, f32[4096,128]{1,0:T(8,128)S(1)} %bitcast.184, f32[128]{0:T(128)S(1)} %get-tuple-element.43, f32[128]{0:T(128)S(1)} %get-tuple-element.44, f32[128]{0:T(128)S(1)} %get-tuple-element.48, ...), kind=kLoop, calls=%fused_computation.64 | loop fusion | flops 8388608 | bytes 7343104 | tf_op jit(solution)/shard_map/convert_element_type | solution.py:104
  181.0 5.7 %convolution_bitcast_fusion.1 = f32[128,2,64,128,1]{3,0,2,1,4:T(8,128)} fusion(bf16[64,64,128]{2,1,0:T(8,128)(2,1)S(1)} %bitcast.196, f32[128,1,64]{0,2,1:T(8,128)S(1)} %get-tuple-element.57, f32[128,1,64]{0,2,1:T(8,128)S(1)} %get-tuple-element.58), kind=kOutput, calls=%fused_computation.45 | convolution fusion | flops 805322752 | bytes 9502720 | tf_op jit(solution)/shard_map/arb,bnc->arnc/dot_general | solution.py:27
  186.7 19.3 %fusion.25 = f32[128,2,64,128]{3,2,1,0:T(8,128)} fusion(f32[128,2,64,128,1]{3,0,2,1,4:T(8,128)} %convolution_bitcast_fusion.1, f32[128,1,64,2,64]{4,2,3,1,0:T(8,128)} %get-tuple-element.34, f32[128,1,64,2,64]{4,2,3,1,0:T(8,128)S(1)} %bitcast.181), kind=kOutput, calls=%fused_computation.47 | convolution fusion | flops 1612709888 | bytes 25165824 | tf_op jit(solution)/shard_map/asmrn,arnc->asmc/dot_general | solution.py:40
  206.0 2.9 convert_bitcast_fusion
  209.0 3.0 copy.34
  212.0 3.5 fusion.47
  215.5 5.7 %convolution_bitcast_fusion = f32[128,2,64,128,1]{3,0,2,1,4:T(8,128)} fusion(bf16[64,64,128]{2,1,0:T(8,128)(2,1)S(1)} %bitcast.195, f32[128,1,64]{0,2,1:T(8,128)S(1)} %get-tuple-element.57, f32[128,1,64]{0,2,1:T(8,128)S(1)} %get-tuple-element.58), kind=kOutput, calls=%fused_computation.44 | convolution fusion | flops 805322752 | bytes 9502720 | tf_op jit(solution)/shard_map/arb,bnc->arnc/dot_general | solution.py:27
  221.2 19.3 %fusion.31 = f32[128,2,64,128]{3,2,1,0:T(8,128)} fusion(f32[128,2,64,128,1]{3,0,2,1,4:T(8,128)} %convolution_bitcast_fusion, f32[128,1,64,2,64]{4,2,3,1,0:T(8,128)} %get-tuple-element.34, f32[128,1,64,2,64]{4,2,3,1,0:T(8,128)S(1)} %bitcast.183), kind=kOutput, calls=%fused_computation.49 | convolution fusion | flops 1612709888 | bytes 25165824 | tf_op jit(solution)/shard_map/asmrn,arnc->asmc/dot_general | solution.py:40
  240.5 15.1 %subtract_subtract_fusion = (f32[128,1,64,128]{3,2,1,0:T(8,128)}, f32[128,1,64,128]{3,2,1,0:T(8,128)}, f32[128,1,64,128]{3,2,1,0:T(8,128)}) fusion(f32[128,2,64,128]{3,2,1,0:T(8,128)} %fusion.31, f32[128,2,64,128]{3,2,1,0:T(8,128)} %fusion.28, f32[128,2,64,128]{3,2,1,0:T(8,128)} %fusion.25), kind=kLoop, calls=%fused_computation.41 | loop fusion | flops 17825792 | bytes 37748736 | tf_op jit(solution)/shard_map/sub | solution.py:162
  255.6 19.4 %fusion.37 = f32[128,2,64,128]{3,2,1,0:T(8,128)S(1)} fusion(f32[128,1,64,128]{3,2,1,0:T(8,128)} %get-tuple-element.29, f32[128,1,64,128]{3,2,1,0:T(8,128)} %get-tuple-element.28, f32[128,1,64,2,64]{4,2,3,0,1:T(8,128)} %get-tuple-element.32, f32[128,1,64,2,64]{4,2,3,0,1:T(8,128)} %get-tuple-element.31), kind=kOutput, calls=%fused_computation.51 | convolution fusion | flops 3225419776 | bytes 25165824 | tf_op jit(solution)/shard_map/asnrm,armc->asnc/dot_general | solution.py:58
  275.0 10.1 %bitcast_multiply_fusion = f32[2,64,64,128]{3,1,2,0:T(8,128)S(1)} fusion(f32[128,2,64,128]{3,2,1,0:T(8,128)S(1)} %fusion.37, f32[1,64,128,2]{2,1,3,0:T(8,128)S(1)} %get-tuple-element.50, f32[1,64,128,2]{2,1,3,0:T(8,128)S(1)} %get-tuple-element.49), kind=kOutput, calls=%fused_computation.39 | convolution fusion | flops 3222306816 | bytes 12713984 | tf_op jit(solution)/shard_map/sbar,arnc->sbnc/dot_general | solution.py:68
  286.7 1.6 copy-done.1
  289.5 2.4 multiply_reduce_fusion.4
  292.0 1.7 add_convert_fusion.1
  293.7 8.2 %all-to-all-start.6 = ((bf16[32,128,128]{2,1,0:T(8,128)(2,1)}), bf16[32,128,128]{2,1,0:T(8,128)(2,1)S(1)}, u32[]{:S(2)}, u32[]{:S(2)}) async-start(bf16[32,128,128]{2,1,0:T(8,128)(2,1)} %bitcast.70), calls=%async_computation.6 | async-start | bytes 2097152 | tf_op jit(solution)/shard_map/all_to_all | solution.py:200
  302.1 10.4 %multiply_add_fusion = f32[128,1,64,128]{3,2,1,0:T(8,128)} fusion(f32[128,2,64,128]{3,2,1,0:T(8,128)} %fusion.28, f32[128,2,64,128]{3,2,1,0:T(8,128)} %fusion.25), kind=kLoop, calls=%fused_computation.42 | loop fusion | flops 3145728 | bytes 20971520 | tf_op jit(solution)/shard_map/add | solution.py:141
  312.4 1.6 add_convert_fusion.2
  314.1 16.2 %all-to-all-done.6 = bf16[32,128,128]{2,1,0:T(8,128)(2,1)S(1)} async-done(((bf16[32,128,128]{2,1,0:T(8,128)(2,1)}), bf16[32,128,128]{2,1,0:T(8,128)(2,1)S(1)}, u32[]{:S(2)}, u32[]{:S(2)}) %all-to-all-start.6) | async-done | bytes 1048608 | tf_op jit(solution)/shard_map/all_to_all | solution.py:200
  330.3 4.7 all-to-all-start.5
  335.0 19.2 %fusion.34 = f32[128,2,64,128]{3,2,1,0:T(8,128)S(1)} fusion(f32[128,1,64,128]{3,2,1,0:T(8,128)} %multiply_add_fusion, f32[128,1,64,128]{3,2,1,0:T(8,128)} %get-tuple-element.30, f32[128,1,64,2,64]{4,2,3,0,1:T(8,128)} %get-tuple-element.32, f32[128,1,64,2,64]{4,2,3,0,1:T(8,128)} %get-tuple-element.31), kind=kOutput, calls=%fused_computation.50 | convolution fusion | flops 3225419776 | bytes 25165824 | tf_op jit(solution)/shard_map/asnrm,armc->asnc/dot_general | solution.py:58
  354.2 9.7 %fusion.59 = f32[64,64,128]{2,0,1:T(8,128)S(1)} fusion(f32[128,2,64,128]{3,2,1,0:T(8,128)S(1)} %fusion.34, f32[64,128,1]{1,0,2:T(8,128)S(1)} %get-tuple-element.60, f32[64,128,1]{1,0,2:T(8,128)S(1)} %get-tuple-element.59), kind=kOutput, calls=%fused_computation.101 | convolution fusion | flops 1612201984 | bytes 10551296 | tf_op jit(solution)/shard_map/bar,arnc->bnc/dot_general | solution.py:70
  366.2 1.8 multiply_reduce_fusion.1
  368.0 1.6 add_convert_fusion
  369.6 37.0 %all_to_all.128 = bf16[32,128,128]{2,1,0:T(8,128)(2,1)} all-to-all(bf16[32,128,128]{2,1,0:T(8,128)(2,1)} %bitcast.194), channel_id=1, replica_groups=mesh['grp'=8,'seq'=32] {'seq'}, dimensions={0} | all-to-all | bytes 2097152 | tf_op jit(solution)/shard_map/all_to_all | solution.py:201
  406.6 4.7 all-to-all-start.3
  411.3 1.8 copy.45
  413.1 2.5 multiply_reduce_fusion.2
  415.6 49.2 %all_gather.3 = f32[3,3,4096]{2,1,0:T(4,128)S(1)} all-gather(f32[3,3,128]{2,1,0:T(4,128)S(1)} %pad_maximum_fusion.13), channel_id=1, replica_groups=mesh['grp'=8,'seq'=32] {'seq'}, dimensions={2}, use_global_device_ids=true | all-gather | bytes 152064 | tf_op jit(solution)/shard_map/all_gather | solution.py:203
  464.8 2.5 copy.43
  469.3 1.6 copy.40
  474.2 1.6 copy.32
  (80 shorter events, 18.1 us)
Async XLA Ops:
  0.6 12.2 %copy-start.15 = (bf16[128,4096]{1,0:T(8,128)(2,1)S(1)}, bf16[128,4096]{1,0:T(8,128)(2,1)}, u32[]{:S(2)}) copy-start(bf16[128,4096]{1,0:T(8,128)(2,1)} %param.7) | copy-start | bytes 3145732
  0.6 44.7 %copy-start.16 = (bf16[128,4096]{1,0:T(8,128)(2,1)S(1)}, bf16[128,4096]{1,0:T(8,128)(2,1)}, u32[]{:S(2)}) copy-start(bf16[128,4096]{1,0:T(8,128)(2,1)} %param.8) | copy-start | bytes 3145732
  3.1 38.2 %all-to-all-start.1 = ((bf16[128,32,128]{0,2,1:T(8,128)(2,1)}), bf16[128,32,128]{0,2,1:T(8,128)(2,1)S(1)}, u32[]{:S(2)}, u32[]{:S(2)}) async-start(bf16[128,32,128]{0,2,1:T(8,128)(2,1)} %bitcast.15), calls=%async_computation.1 | async-start | bytes 2097152 | tf_op jit(solution)/shard_map/all_to_all | solution.py:173
  41.2 18.9 %copy-start.7 = (bf16[128,32,128]{0,2,1:T(8,128)(2,1)}, bf16[128,32,128]{0,2,1:T(8,128)(2,1)S(1)}, u32[]{:S(2)}) copy-start(bf16[128,32,128]{0,2,1:T(8,128)(2,1)S(1)} %all-to-all-done.1) | copy-start | bytes 3145732
  41.2 61.0 %all-to-all-start.2 = ((bf16[128,32,128]{0,2,1:T(8,128)(2,1)}), bf16[128,32,128]{0,2,1:T(8,128)(2,1)S(1)}, u32[]{:S(2)}, u32[]{:S(2)}) async-start(bf16[128,32,128]{0,2,1:T(8,128)(2,1)} %bitcast.21), calls=%async_computation.2 | async-start | bytes 2097152 | tf_op jit(solution)/shard_map/all_to_all | solution.py:174
  102.3 9.5 %copy-start.8 = (bf16[128,32,128]{0,2,1:T(8,128)(2,1)}, bf16[128,32,128]{0,2,1:T(8,128)(2,1)S(1)}, u32[]{:S(2)}) copy-start(bf16[128,32,128]{0,2,1:T(8,128)(2,1)S(1)} %all-to-all-done.2) | copy-start | bytes 3145732
  102.3 59.9 %all-to-all-start = ((bf16[128,32,128]{0,2,1:T(8,128)(2,1)}), bf16[128,32,128]{0,2,1:T(8,128)(2,1)S(1)}, u32[]{:S(2)}, u32[]{:S(2)}) async-start(bf16[128,32,128]{0,2,1:T(8,128)(2,1)} %bitcast.1), calls=%async_computation | async-start | bytes 2097152 | tf_op jit(solution)/shard_map/all_to_all | solution.py:175
  111.7 12.7 %slice-start = ((s8[8388608]{0:T(1024)(128)(4,1)}), s8[4194304]{0:T(1024)(128)(4,1)S(1)}, s32[]{:S(2)}) async-start(s8[8388608]{0:T(1024)(128)(4,1)} %bitcast.178), calls=%async_computation.8 | async-start | bytes 8388608
  111.7 12.7 %slice-start.1 = ((s8[8388608]{0:T(1024)(128)(4,1)}), s8[4194304]{0:T(1024)(128)(4,1)S(1)}, s32[]{:S(2)}) async-start(s8[8388608]{0:T(1024)(128)(4,1)} %bitcast.178), calls=%async_computation.9 | async-start | bytes 8388608
  155.7 19.5 %copy-start = (f32[32,128,128]{2,1,0:T(8,128)}, f32[32,128,128]{2,1,0:T(8,128)S(1)}, u32[]{:S(2)}) copy-start(f32[32,128,128]{2,1,0:T(8,128)S(1)} %copy.22) | copy-start | bytes 6291460
  162.1 43.9 %all-to-all-start.4 = ((bf16[128,32,128]{0,2,1:T(8,128)(2,1)}), bf16[128,32,128]{0,2,1:T(8,128)(2,1)}, u32[]{:S(2)}, u32[]{:S(2)}) async-start(bf16[128,32,128]{0,2,1:T(8,128)(2,1)} %bitcast.192), calls=%async_computation.4 | async-start | bytes 2097152 | tf_op jit(solution)/shard_map/all_to_all | solution.py:176
  175.2 11.5 %slice-start.2 = ((s8[8388608]{0:T(1024)(128)(4,1)}), s8[4194304]{0:T(1024)(128)(4,1)S(1)}, s32[]{:S(2)}) async-start(s8[8388608]{0:T(1024)(128)(4,1)} %bitcast.180), calls=%async_computation.10 | async-start | bytes 8388608
  181.0 5.7 %slice-start.3 = ((s8[8388608]{0:T(1024)(128)(4,1)}), s8[4194304]{0:T(1024)(128)(4,1)S(1)}, s32[]{:S(2)}) async-start(s8[8388608]{0:T(1024)(128)(4,1)} %bitcast.180), calls=%async_computation.11 | async-start | bytes 8388608
  206.0 6.0 %copy-start.3 = (f32[32,128,128]{2,1,0:T(8,128)S(1)}, f32[32,128,128]{2,1,0:T(8,128)}, u32[]{:S(2)}) copy-start(f32[32,128,128]{2,1,0:T(8,128)} %copy.19) | copy-start | bytes 6291460
  212.0 9.2 %slice-start.4 = ((s8[8388608]{0:T(1024)(128)(4,1)}), s8[4194304]{0:T(1024)(128)(4,1)S(1)}, s32[]{:S(2)}) async-start(s8[8388608]{0:T(1024)(128)(4,1)} %bitcast.182), calls=%async_computation.12 | async-start | bytes 8388608
  215.5 5.7 %slice-start.5 = ((s8[8388608]{0:T(1024)(128)(4,1)}), s8[4194304]{0:T(1024)(128)(4,1)S(1)}, s32[]{:S(2)}) async-start(s8[8388608]{0:T(1024)(128)(4,1)} %bitcast.182), calls=%async_computation.13 | async-start | bytes 8388608
  285.1 6.8 %copy-start.6 = (f32[2,64,64,128]{3,1,2,0:T(8,128)}, f32[2,64,64,128]{3,1,2,0:T(8,128)S(1)}, u32[]{:S(2)}) copy-start(f32[2,64,64,128]{3,1,2,0:T(8,128)S(1)} %bitcast_multiply_fusion) | copy-start | bytes 12582916
  285.1 3.1 copy-start.1
  285.2 3.7 copy-start.2
  285.2 4.0 copy-start.13
  285.2 4.3 copy-start.14
  293.7 36.6 %all-to-all-start.6 = ((bf16[32,128,128]{2,1,0:T(8,128)(2,1)}), bf16[32,128,128]{2,1,0:T(8,128)(2,1)S(1)}, u32[]{:S(2)}, u32[]{:S(2)}) async-start(bf16[32,128,128]{2,1,0:T(8,128)(2,1)} %bitcast.70), calls=%async_computation.6 | async-start | bytes 2097152 | tf_op jit(solution)/shard_map/all_to_all | solution.py:200
  330.3 4.7 copy-start.9
  330.3 39.3 %all-to-all-start.5 = ((bf16[32,128,128]{2,1,0:T(8,128)(2,1)}), bf16[32,128,128]{2,1,0:T(8,128)(2,1)}, u32[]{:S(2)}, u32[]{:S(2)}) async-start(bf16[32,128,128]{2,1,0:T(8,128)(2,1)} %bitcast.67), calls=%async_computation.5 | async-start | bytes 2097152 | tf_op jit(solution)/shard_map/all_to_all | solution.py:199
  354.2 11.0 %copy-start.12 = (bf16[4096,128]{1,0:T(8,128)(2,1)S(1)}, bf16[4096,128]{1,0:T(8,128)(2,1)}, u32[]{:S(2)}) copy-start(bf16[4096,128]{1,0:T(8,128)(2,1)} %get-tuple-element.24) | copy-start | bytes 3145732
  363.9 1.6 copy-start.4
  364.0 2.2 copy-start.5
  406.6 67.6 %all-to-all-start.3 = ((bf16[32,128,128]{2,1,0:T(8,128)(2,1)}), bf16[32,128,128]{2,1,0:T(8,128)(2,1)}, u32[]{:S(2)}, u32[]{:S(2)}) async-start(bf16[32,128,128]{2,1,0:T(8,128)(2,1)} %bitcast.201), calls=%async_computation.3 | async-start | bytes 2097152 | tf_op jit(solution)/shard_map/all_to_all | solution.py:198
  413.1 51.7 %slice-start.6 = ((f32[2,64,64,128]{3,1,2,0:T(8,128)}), f32[1,64,64,128]{3,1,2,0:T(8,128)S(1)}, s32[]{:S(2)}) async-start(f32[2,64,64,128]{3,1,2,0:T(8,128)} %copy-done.6), calls=%async_computation.14 | async-start | bytes 4194304 | tf_op jit(solution)/shard_map/slice | solution.py:164
  413.1 54.2 %copy-start.10 = (bf16[32,128,128]{2,1,0:T(8,128)(2,1)S(1)}, bf16[32,128,128]{2,1,0:T(8,128)(2,1)}, u32[]{:S(2)}) copy-start(bf16[32,128,128]{2,1,0:T(8,128)(2,1)} %copy-done.9) | copy-start | bytes 3145732
  467.3 4.9 %copy-start.11 = (bf16[32,128,128]{2,1,0:T(8,128)(2,1)S(1)}, bf16[32,128,128]{2,1,0:T(8,128)(2,1)}, u32[]{:S(2)}) copy-start(bf16[32,128,128]{2,1,0:T(8,128)(2,1)} %all_to_all.128) | copy-start | bytes 3145732
where the time goes:
time: 488 us; the launch traced here: 478 us
  matrix products  146 us (30%)
  other arithmetic  113 us (23%)
  blocking collectives  86.1 us (18%)
  starting transfers between devices  48.5 us (10%)
  waiting for transfers between devices  42.8 us (9%)
  local copies, waits for them, and re-layouts  40.5 us (8%)
    dot_general x3, matrix products, spectrum(): return jnp.einsum('asmrn,arnc->asmc', mixer, section, precision=accuracy)  64.7 us
    all_gather x1, blocking collectives, local(): grad_short = lax.all_gather(short_part, 'seq', axis=2, tiled=True)  49.2 us
    dot_general x2, matrix products, inverse_spec(): section = jnp.einsum('asnrm,armc->asnc', mixer, spec, precision=exact_dots)  38.6 us
    all_to_all x1, blocking collectives, local(): lax.all_to_all(grads[2], 'seq', split_axis=0, concat_axis=1, tiled=True)  37 us
    neg x1, other arithmetic, inverse_spec(): -sin_w  35.2 us
    all_to_all x1, waiting for transfers between devices, local(): lax.all_to_all(gate_in, 'seq', split_axis=1, concat_axis=0, tiled=True)  26.6 us
    dot_general x3, matrix products, spectrum(): jnp.einsum('arb,bnc->arnc', first_table, blocks, precision=accuracy)  22.6 us
    unnamed x55, local copies, waits for them, and re-layouts  17.1 us
  transfers between devices with their start and end apart: 7, of which 2 were waited for; matrix products, arithmetic and copies ran while one was open for 43% of the time, Pallas kernels for 0%

commit v1 on v0

v1 whole, which is shorter than its diff:
```python
import functools

import jax
import jax.numpy as jnp
import ml_dtypes
import numpy as np
from jax import lax
from jax.experimental import pallas as pl
from jax.experimental.pallas import tpu as pltpu
from jax.sharding import PartitionSpec as P

bf16 = jnp.bfloat16
f32 = jnp.float32

TILE = 512
GROUP = 8
PAD = 8


class Sizes:
    def __init__(self, blocks, rows, width):
        self.blocks, self.rows, self.width = blocks, rows, width
        self.half = blocks + 1
        self.parts = -(-2 * self.half // 8) * 8
        self.pitch = rows + PAD
        self.length = 2 * blocks * rows


def tables(z):
    a, b = np.arange(z.half), np.arange(z.blocks)
    turn = 2 * np.pi * ((a[:, None] * b[None, :]) % (2 * z.blocks)) / (2 * z.blocks)
    coarse = np.zeros((z.parts, z.blocks))
    coarse[0 : 2 * z.half : 2] = np.cos(turn)
    coarse[1 : 2 * z.half : 2] = -np.sin(turn)
    weight = np.where((a == 0) | (a == z.blocks), 1.0, 2.0) / z.length
    back = np.zeros((z.blocks, z.parts))
    back[:, 0 : 2 * z.half : 2] = (np.cos(turn) * weight[:, None]).T
    back[:, 1 : 2 * z.half : 2] = (-np.sin(turn) * weight[:, None]).T
    r = np.arange(z.rows)
    phase = ((a[:, None, None] + 2 * z.blocks * r[None, :, None]) * r[None, None, :]) % z.length
    cos_w, sin_w = np.cos(2 * np.pi * phase / z.length), np.sin(2 * np.pi * phase / z.length)
    fine = np.concatenate([np.concatenate([cos_w, sin_w], 2), np.concatenate([-sin_w, cos_w], 2)], 1)
    twice = np.concatenate([coarse, coarse], 1)
    return [t.astype(ml_dtypes.bfloat16) for t in (coarse, twice, fine, fine.transpose(0, 2, 1), back)]


def rows_at(z, block):
    return pl.ds(pl.multiple_of(block * z.pitch, 8), z.rows)


def coarse_forward(z, held, coarse_ref, parts, split):
    coarse = coarse_ref[...]

    def body(step, carry):
        columns = []
        for j in range(GROUP):
            value = held[pl.ds(step * GROUP + j, z.blocks, stride=z.pitch), :]
            high = value.astype(bf16)
            if split:
                high = jnp.concatenate([high, (value - high.astype(f32)).astype(bf16)], axis=0)
            columns.append(high)
        out = jnp.dot(coarse, jnp.concatenate(columns, axis=1), preferred_element_type=f32)
        for j in range(GROUP):
            parts[pl.ds(step * GROUP + j, z.parts, stride=z.pitch), :] = out[:, j * z.width : (j + 1) * z.width]
        return carry

    lax.fori_loop(0, z.rows // GROUP, body, 0)


def coarse_inverse(z, parts, back_ref, held):
    back = back_ref[...]

    def body(step, carry):
        columns = [parts[pl.ds(step * GROUP + j, z.parts, stride=z.pitch), :].astype(bf16) for j in range(GROUP)]
        out = jnp.dot(back, jnp.concatenate(columns, axis=1), preferred_element_type=f32)
        for j in range(GROUP):
            held[pl.ds(step * GROUP + j, z.blocks, stride=z.pitch), :] = out[:, j * z.width : (j + 1) * z.width]
        return carry

    lax.fori_loop(0, z.rows // GROUP, body, 0)


def fine_forward(z, fine_ref, parts, a):
    re = parts[rows_at(z, 2 * a), :].astype(bf16)
    im = parts[rows_at(z, 2 * a + 1), :].astype(bf16)
    return jnp.dot(fine_ref[a], jnp.concatenate([re, im], axis=0), preferred_element_type=f32)


def fine_inverse(z, fine_ref, parts, a, re, im):
    spec = jnp.concatenate([re.astype(bf16), im.astype(bf16)], axis=0)
    out = jnp.dot(fine_ref[a], spec, preferred_element_type=f32)
    parts[rows_at(z, 2 * a), :] = out[: z.rows]
    parts[rows_at(z, 2 * a + 1), :] = out[z.rows :]


def load_blocks(z, block_of, held):
    def body(i, carry):
        held[rows_at(z, i), :] = block_of(i).astype(f32)
        return carry

    lax.fori_loop(0, z.blocks, body, 0, unroll=4)


def filter_kernel(z, filter_ref, twice_ref, fine_ref, spec_ref, held, parts):
    load_blocks(z, lambda i: filter_ref[pl.ds(pl.multiple_of(i * z.rows, 8), z.rows), :], held)
    coarse_forward(z, held, twice_ref, parts, True)

    def body(a, carry):
        spec_ref[a] = fine_forward(z, fine_ref, parts, a).astype(spec_ref.dtype)
        return carry

    lax.fori_loop(0, z.half, body, 0, unroll=3)


def conv_kernel(z, conj, data_ref, filter_ref, coarse_ref, fine_ref, inv_ref, back_ref, spec_ref, out_ref, held, parts):
    load_blocks(z, lambda i: data_ref[i], held)
    coarse_forward(z, held, coarse_ref, parts, False)

    def body(a, carry):
        spec = fine_forward(z, fine_ref, parts, a)
        spec_ref[a] = spec.astype(spec_ref.dtype)
        other = filter_ref[a].astype(f32)
        s_re, s_im, h_re, h_im = spec[: z.rows], spec[z.rows :], other[: z.rows], other[z.rows :]
        if conj:
            re, im = s_re * h_re + s_im * h_im, s_im * h_re - s_re * h_im
        else:
            re, im = s_re * h_re - s_im * h_im, s_re * h_im + s_im * h_re
        fine_inverse(z, inv_ref, parts, a, re, im)
        return carry

    lax.fori_loop(0, z.half, body, 0, unroll=3)
    coarse_inverse(z, parts, back_ref, held)

    def done(i, carry):
        out_ref[i] = held[rows_at(z, i), :].astype(out_ref.dtype)
        return carry

    lax.fori_loop(0, z.blocks, done, 0, unroll=4)


def long_kernel(z, signal_ref, grad_ref, inv_ref, back_ref, out_ref, held, parts):
    spare = (z.parts - 2 * z.half) * z.pitch
    if spare:
        parts[pl.ds(2 * z.half * z.pitch, spare), :] = jnp.zeros((spare, z.width), f32)

    def body(a, carry):
        s, g = signal_ref[a].astype(f32), grad_ref[a].astype(f32)
        s_re, s_im, g_re, g_im = s[: z.rows], s[z.rows :], g[: z.rows], g[z.rows :]
        fine_inverse(z, inv_ref, parts, a, s_re * g_re + s_im * g_im, s_re * g_im - s_im * g_re)
        return carry

    lax.fori_loop(0, z.half, body, 0, unroll=3)
    coarse_inverse(z, parts, back_ref, held)

    def done(i, carry):
        out_ref[pl.ds(pl.multiple_of(i * z.rows, 8), z.rows), :] = held[rows_at(z, i), :]
        return carry

    lax.fori_loop(0, z.blocks, done, 0, unroll=4)


def channel_call(z, kernel, operands, outs, name, cost_us):
    whole = pl.BlockSpec(memory_space=pltpu.VMEM)
    return pl.pallas_call(
        kernel,
        out_shape=outs,
        in_specs=[whole] * len(operands),
        out_specs=[whole] * len(outs),
        scratch_shapes=[
            pltpu.VMEM((z.blocks * z.pitch, z.width), f32),
            pltpu.VMEM((z.parts * z.pitch, z.width), f32),
        ],
        compiler_params=pltpu.CompilerParams(vmem_limit_bytes=40 << 20),
        cost_estimate=pl.CostEstimate(flops=0, bytes_accessed=int(cost_us * 3e6), transcendentals=0),
        name=name,
    )(*operands)


def delayed(rows, before, lag):
    moved = pltpu.roll(rows, lag, 0)
    index = lax.broadcasted_iota(jnp.int32, rows.shape, 0)
    for i in range(lag):
        moved = jnp.where(index == i, before[2 - lag + i : 3 - lag + i], moved)
    return moved


def feature(source, halo, which, taps_ref):
    rows = source.astype(f32)
    before = halo[2 * which : 2 * which + 2]
    one, two = delayed(rows, before, 1), delayed(rows, before, 2)
    taps = taps_ref[which]
    feat = taps[0:1] * rows + taps[1:2] * one + taps[2:3] * two
    return feat.astype(bf16).astype(f32), (rows, one, two)


def outward(out_ref, value):
    for j in range(value.shape[1] // out_ref.shape[2]):
        width = out_ref.shape[2]
        out_ref[j] = value[:, j * width : (j + 1) * width].astype(out_ref.dtype)


def inward(in_ref):
    return jnp.concatenate([in_ref[j] for j in range(in_ref.shape[0])], axis=1).astype(f32)


def outer_kernel(out_ref, cot_ref, halo_ref, taps_ref, outer_ref):
    halo = halo_ref[...].astype(f32)
    feat_out, _ = feature(out_ref[...], halo, 2, taps_ref)
    outward(outer_ref, feat_out * cot_ref[...].astype(f32))


def signal_kernel(gate_ref, value_ref, halo_ref, taps_ref, signal_ref):
    halo = halo_ref[...].astype(f32)
    feat_gate, _ = feature(gate_ref[...], halo, 0, taps_ref)
    feat_value, _ = feature(value_ref[...], halo, 1, taps_ref)
    outward(signal_ref, feat_gate * feat_value)


def adjoint(grad, taps):
    count = grad.shape[0]
    return taps[0:1] * grad + taps[1:2] * pltpu.roll(grad, count - 1, 0) + taps[2:3] * pltpu.roll(grad, count - 2, 0)


def collect(pieces, rows, dtype):
    made = jnp.concatenate(pieces, axis=0)
    spare = rows - made.shape[0]
    if spare:
        made = jnp.concatenate([made, jnp.zeros((spare, made.shape[1]), made.dtype)], axis=0)
    return made.astype(dtype)


def lag_sums(grad, lags):
    return [jnp.sum(grad * lag, axis=0, keepdims=True) for lag in lags]


def input_grads_kernel(
    sig_ref, gate_ref, value_ref, halo_ref, taps_ref, grad_gate_ref, grad_value_ref, sums_ref, head_ref, tail_ref
):
    halo = halo_ref[...].astype(f32)
    sig = inward(sig_ref)
    feat_gate, gate_lags = feature(gate_ref[...], halo, 0, taps_ref)
    feat_value, value_lags = feature(value_ref[...], halo, 1, taps_ref)
    gate_grad = (sig * feat_value).astype(bf16).astype(f32)
    value_grad = (sig * feat_gate).astype(bf16).astype(f32)
    grad_gate_ref[...] = adjoint(gate_grad, taps_ref[0]).astype(bf16)
    grad_value_ref[...] = adjoint(value_grad, taps_ref[1]).astype(bf16)
    sums_ref[...] = collect(lag_sums(gate_grad, gate_lags) + lag_sums(value_grad, value_lags), 8, f32)
    count = sig.shape[0]
    head_ref[...] = collect([gate_grad[0:2], value_grad[0:2]], 8, bf16)
    tail_ref[...] = collect([gate_grad[count - 2 :], value_grad[count - 2 :]], 8, bf16)


def output_grads_kernel(
    conv_ref, out_ref, cot_ref, halo_ref, taps_ref, mixed_ref, grad_out_ref, sums_ref, head_ref, tail_ref
):
    halo = halo_ref[...].astype(f32)
    conv = inward(conv_ref)
    feat_out, out_lags = feature(out_ref[...], halo, 2, taps_ref)
    mixed_ref[...] = (feat_out * conv).astype(bf16)
    out_grad = (cot_ref[...].astype(f32) * conv).astype(bf16).astype(f32)
    grad_out_ref[...] = adjoint(out_grad, taps_ref[2]).astype(bf16)
    sums_ref[...] = collect(lag_sums(out_grad, out_lags), 8, f32)
    count = conv.shape[0]
    head_ref[...] = collect([out_grad[0:2]], 8, bf16)
    tail_ref[...] = collect([out_grad[count - 2 :]], 8, bf16)


def finish_kernel(first, count, *refs):
    ins, head_ref, tail_ref, taps_ref = refs[:count], refs[count], refs[count + 1], refs[count + 2]
    outs = refs[count + 3 :]
    head, tail = head_ref[...].astype(f32), tail_ref[...].astype(f32)
    for k in range(count):
        taps = taps_ref[first + k]
        h0, h1 = head[2 * k : 2 * k + 1], head[2 * k + 1 : 2 * k + 2]
        t0, t1 = tail[2 * k : 2 * k + 1], tail[2 * k + 1 : 2 * k + 2]
        old = ins[k][...].astype(f32)
        index = lax.broadcasted_iota(jnp.int32, old.shape, 0)
        last = old.shape[0] - 1
        new = jnp.where(index == last - 1, taps[0:1] * t0 + taps[1:2] * t1 + taps[2:3] * h0, old)
        new = jnp.where(index == last, taps[0:1] * t1 + taps[1:2] * h0 + taps[2:3] * h1, new)
        outs[k][...] = new.astype(bf16)


def position_call(z, kernel, operands, kinds, out_kinds, channels, name, cost_us, aliases=None):
    tile = TILE if channels % TILE == 0 else z.width

    def spec(kind):
        return {
            "rows": pl.BlockSpec((z.rows, tile), lambda i: (0, i)),
            "moved": pl.BlockSpec((tile // z.width, z.rows, z.width), lambda i: (i, 0, 0)),
            "edge": pl.BlockSpec((8, tile), lambda i: (0, i)),
            "sums": pl.BlockSpec((8, tile), lambda i: (0, i)),
            "taps": pl.BlockSpec((3, 3, tile), lambda i: (0, 0, i)),
            "last": pl.BlockSpec((16, tile), lambda i: (z.rows // 16 - 1, i)),
        }[kind]

    shapes = {
        "rows": jax.ShapeDtypeStruct((z.rows, channels), bf16),
        "last": jax.ShapeDtypeStruct((z.rows, channels), bf16),
        "moved": jax.ShapeDtypeStruct((channels // z.width, z.rows, z.width), bf16),
        "edge": jax.ShapeDtypeStruct((8, channels), bf16),
        "sums": jax.ShapeDtypeStruct((8, channels), f32),
    }
    return pl.pallas_call(
        kernel,
        grid=(channels // tile,),
        out_shape=[shapes[k] for k in out_kinds],
        in_specs=[spec(k) for k in kinds],
        out_specs=[spec(k) for k in out_kinds],
        input_output_aliases=aliases or {},
        compiler_params=pltpu.CompilerParams(vmem_limit_bytes=32 << 20),
        cost_estimate=pl.CostEstimate(flops=0, bytes_accessed=int(cost_us * 3e6), transcendentals=0),
        name=name,
    )(*operands)


def sum_over(value, size):
    bit = 1
    while bit < size:
        value = value + lax.ppermute(value, "seq", [(i, i ^ bit) for i in range(size)])
        bit = 2 * bit
    return value


def exchange(value):
    return lax.all_to_all(value, "seq", split_axis=0, concat_axis=0, tiled=True)


def local(size, gate_in, value_in, gate_out, cotangent, long_filter, short_filters):
    rows, channels = gate_in.shape
    z = Sizes(size, rows, long_filter.shape[1])
    coarse, twice, fine, inv, back = [jnp.asarray(t) for t in tables(z)]
    spec_shape = jax.ShapeDtypeStruct((z.half, 2 * z.rows, z.width), bf16)
    moved_shape = jax.ShapeDtypeStruct((z.blocks, z.rows, z.width), bf16)
    onward = [(i, i + 1) for i in range(size - 1)]
    backward = [(i + 1, i) for i in range(size - 1)]

    edges = jnp.concatenate(
        [gate_in[rows - 2 :], value_in[rows - 2 :], gate_out[rows - 2 :], jnp.zeros((2, channels), bf16)], axis=0
    )
    halo = lax.ppermute(edges, "seq", onward)

    def position(kernel, operands, kinds, outs, name, cost_us, aliases=None):
        return position_call(z, kernel, operands, kinds, outs, channels, name, cost_us, aliases)

    (outer,) = position(
        outer_kernel, (gate_out, cotangent, halo, short_filters), ("rows", "rows", "edge", "taps"), ("moved",), "outer", 4
    )
    (signal,) = position(
        signal_kernel, (gate_in, value_in, halo, short_filters), ("rows", "rows", "edge", "taps"), ("moved",), "signal", 4
    )
    outer_moved = exchange(outer)
    (filter_spec,) = channel_call(
        z, functools.partial(filter_kernel, z), (long_filter, twice, fine), (spec_shape,), "filter_spec", 8
    )
    signal_moved = exchange(signal)
    outer_spec, sig_grad = channel_call(
        z,
        functools.partial(conv_kernel, z, True),
        (outer_moved, filter_spec, coarse, fine, inv, back),
        (spec_shape, moved_shape),
        "signal_grad",
        16,
    )
    sig_rows = exchange(sig_grad)
    signal_spec, conv_out = channel_call(
        z,
        functools.partial(conv_kernel, z, False),
        (signal_moved, filter_spec, coarse, fine, inv, back),
        (spec_shape, moved_shape),
        "conv_out",
        16,
    )
    conv_rows = exchange(conv_out)
    (grad_long,) = channel_call(
        z,
        functools.partial(long_kernel, z),
        (signal_spec, outer_spec, inv, back),
        (jax.ShapeDtypeStruct((z.blocks * z.rows, z.width), f32),),
        "grad_long",
        10,
    )

    grad_gate, grad_value, in_sums, in_head, in_tail = position(
        input_grads_kernel,
        (sig_rows, gate_in, value_in, halo, short_filters),
        ("moved", "rows", "rows", "edge", "taps"),
        ("rows", "rows", "sums", "edge", "edge"),
        "input_grads",
        6,
    )
    in_next = lax.ppermute(in_head, "seq", backward)
    grad_gate, grad_value = position(
        functools.partial(finish_kernel, 0, 2),
        (grad_gate, grad_value, in_next, in_tail, short_filters),
        ("last", "last", "edge", "edge", "taps"),
        ("last", "last"),
        "finish_input_grads",
        2,
        {0: 0, 1: 1},
    )
    in_sums = sum_over(in_sums, size)

    mixed, grad_out, out_sums, out_head, out_tail = position(
        output_grads_kernel,
        (conv_rows, gate_out, cotangent, halo, short_filters),
        ("moved", "rows", "rows", "edge", "taps"),
        ("rows", "rows", "sums", "edge", "edge"),
        "output_grads",
        5,
    )
    out_next = lax.ppermute(out_head, "seq", backward)
    (grad_out,) = position(
        functools.partial(finish_kernel, 2, 1),
        (grad_out, out_next, out_tail, short_filters),
        ("last", "edge", "edge", "taps"),
        ("last",),
        "finish_output_grad",
        2,
        {0: 0},
    )
    out_sums = sum_over(out_sums, size)
    grad_short = jnp.concatenate([in_sums[:6], out_sums[:3]], axis=0).reshape(3, 3, channels)
    return (mixed, grad_gate, grad_value, grad_out, grad_long, grad_short)


def solution(mesh):
    spread = P(("grp", "seq"), None)
    return jax.shard_map(
        functools.partial(local, mesh.shape["seq"]),
        mesh=mesh,
        in_specs=(spread, spread, spread, spread, P(None, "seq"), P()),
        out_specs=(spread, spread, spread, spread, P("grp", "seq"), P("grp", None, None)),
        check_vma=False,
    )
```

time: 488 us -> 232 us (0.48); the launches traced: 478 us -> 229 us
  matrix products: 146 us -> 0 us
  other arithmetic: 113 us -> 0.28 us
  blocking collectives: 86.1 us -> 0 us
  Pallas kernels: 0 us -> 71.5 us
  waiting for transfers between devices: 42.8 us -> 85.4 us
  local copies, waits for them, and re-layouts: 40.5 us -> 25.5 us
    dot_general x10 -> x0, matrix products: 146 us -> none  [the longest x3 64.7 us: spectrum(): return jnp.einsum('asmrn,arnc->asmc', mixer, section, precision=accuracy)]
    pallas_call x0 -> x10, Pallas kernels: none -> 71.5 us  [the longest x4 41.9 us: channel_call(): pl.pallas_call(kernel, out_shape=outs, in_specs=[whole] * len(operands),...]
    all_gather x1 -> x0, blocking collectives: 49.2 us -> none  [local(): grad_short = lax.all_gather(short_part, 'seq', axis=2, tiled=True)]
    all_to_all x1 -> x0, blocking collectives: 37 us -> none  [local(): lax.all_to_all(grads[2], 'seq', split_axis=0, concat_axis=1, tiled=True)]
    neg x2 -> x0, other arithmetic: 35.4 us -> none  [the longest x1 35.2 us: inverse_spec(): -sin_w]
    ppermute x0 -> x13, waiting for transfers between devices: none -> 32.1 us  [the longest x10 31.2 us: sum_over(): lax.ppermute(value, 'seq', [(i, i ^ bit) for i in range(size)])]
    convert_element_type x12 -> x0, other arithmetic: 25.6 us -> none  [the longest x1 5.81 us: gate_inputs(): (feat_gate.astype(jnp.float32) * feat_value.astype(jnp.float32)).astype(j...]
    another operation x7 -> x0, other arithmetic: 19.6 us -> none  [the longest x1 12.7 us: inverse_spec(): jnp.stack([jnp.stack([cos_w, -sin_w], axis=2), jnp.stack([sin_w, cos_w],...]
  transfers between devices with their start and end apart: 7 -> 17, of which waited for: 2 -> 11; matrix products, arithmetic and copies ran while one was open for 43% -> 0% of each run, Pallas kernels for 0% -> 30%
where the time goes in v1:
time: 232 us; the launch traced here: 229 us
  waiting for transfers between devices  85.4 us (37%)
  Pallas kernels  71.5 us (31%)
  starting transfers between devices  45.3 us (20%)
  local copies, waits for them, and re-layouts  25.5 us (11%)
    all_to_all x4, waiting for transfers between devices, exchange(): return lax.all_to_all(value, 'seq', split_axis=0, concat_axis=0, tiled=True)  53.3 us
    pallas_call x4, Pallas kernels, channel_call(): pl.pallas_call(kernel, out_shape=outs, in_specs=[whole] * len(operands),...  41.9 us
    ppermute x10, waiting for transfers between devices, sum_over(): lax.ppermute(value, 'seq', [(i, i ^ bit) for i in range(size)])  31.2 us
    all_to_all x4, starting transfers between devices, exchange(): return lax.all_to_all(value, 'seq', split_axis=0, concat_axis=0, tiled=True)  30.3 us
    pallas_call x6, Pallas kernels, position_call(): pl.pallas_call(kernel, grid=(channels // tile,), out_shape=[shapes[k] for...  29.5 us
    unnamed x66, local copies, waits for them, and re-layouts  22.1 us
    ppermute x10, starting transfers between devices, sum_over(): lax.ppermute(value, 'seq', [(i, i ^ bit) for i in range(size)])  10.7 us
  transfers between devices with their start and end apart: 17, of which 11 were waited for; matrix products, arithmetic and copies ran while one was open for 0% of the time, Pallas kernels for 30%

profile of v1, /device:TPU:8, one launch (start us, length us, event | category | flops | bytes accessed | tf_op | source)
XLA Modules:
  0.0 228.9 jit_solution(11101792379211634155)
XLA Ops:
  0.6 0.9 slice.15
  1.5 0.9 slice.16
  2.4 0.9 slice.17
  3.4 1.7 collective-permute-start
  5.1 0.9 collective-permute-done.halo_ref
  6.0 0.9 copy-done.3
  6.9 1.2 copy-done.8
  8.2 1.2 copy-done.10
  9.4 3.4 %outer.1 = bf16[32,128,128]{2,1,0:T(8,128)(2,1)} custom-call(bf16[128,4096]{1,0:T(8,128)(2,1)S(1)} %copy-done.8, bf16[128,4096]{1,0:T(8,128)(2,1)S(1)} %copy-done.10, bf16[8,4096]{1,0:T(8,128)(2,1)S(1)} %collective-permute-done.halo_ref, f32[3,3,4096]{2,1,0:T(4,128)S(1)} %copy-done.3), custom_call_target="tpu_custom_call" | custom-call | bytes 12000000 | tf_op jit(solution)/shard_map/outer/pallas_call | solution.py:304
  12.8 13.9 %all-to-all-start.2 = ((bf16[32,128,128]{2,1,0:T(8,128)(2,1)}), bf16[32,128,128]{2,1,0:T(8,128)(2,1)S(1)}, u32[]{:S(2)}, u32[]{:S(2)}) async-start(bf16[32,128,128]{2,1,0:T(8,128)(2,1)} %outer.1), calls=%async_computation.2 | async-start | bytes 2097152 | tf_op jit(solution)/shard_map/all_to_all | solution.py:326
  26.8 3.9 %signal.1 = bf16[32,128,128]{2,1,0:T(8,128)(2,1)} custom-call(bf16[128,4096]{1,0:T(8,128)(2,1)S(1)} %copy-done.5, bf16[128,4096]{1,0:T(8,128)(2,1)S(1)} %copy-done.6, bf16[8,4096]{1,0:T(8,128)(2,1)S(1)} %collective-permute-done.halo_ref, f32[3,3,4096]{2,1,0:T(4,128)S(1)} %copy-done.4), custom_call_target="tpu_custom_call" | custom-call | bytes 12000000 | tf_op jit(solution)/shard_map/signal/pallas_call | solution.py:304
  30.7 24.4 %all-to-all-done.2.data_ref = bf16[32,128,128]{2,1,0:T(8,128)(2,1)S(1)} async-done(((bf16[32,128,128]{2,1,0:T(8,128)(2,1)}), bf16[32,128,128]{2,1,0:T(8,128)(2,1)S(1)}, u32[]{:S(2)}, u32[]{:S(2)}) %all-to-all-start.2) | async-done | bytes 1048608 | tf_op jit(solution)/shard_map/all_to_all | solution.py:326
  55.2 1.0 copy-done.12
  56.1 4.7 %all-to-all-start = ((bf16[32,128,128]{2,1,0:T(8,128)(2,1)}), bf16[32,128,128]{2,1,0:T(8,128)(2,1)}, u32[]{:S(2)}, u32[]{:S(2)}) async-start(bf16[32,128,128]{2,1,0:T(8,128)(2,1)} %signal.1), calls=%async_computation | async-start | bytes 2097152 | tf_op jit(solution)/shard_map/all_to_all | solution.py:326
  60.8 2.2 copy-done.1
  63.0 1.6 copy-done.18
  65.4 6.0 %filter_spec.1.filter_ref = bf16[33,256,128]{2,1,0:T(8,128)(2,1)S(1)} custom-call(f32[4096,128]{1,0:T(8,128)S(1)} %copy-done.18, bf16[72,64]{1,0:T(8,128)(2,1)S(1)} %copy-done.28, bf16[33,256,256]{2,1,0:T(8,128)(2,1)S(1)} %copy-done.1), custom_call_target="tpu_custom_call" | custom-call | bytes 24000000 | tf_op jit(solution)/shard_map/filter_spec/pallas_call | solution.py:164
  71.4 14.0 %signal_grad.1 = (bf16[33,256,128]{2,1,0:T(8,128)(2,1)S(1)}, bf16[32,128,128]{2,1,0:T(8,128)(2,1)S(1)}) custom-call(bf16[32,128,128]{2,1,0:T(8,128)(2,1)S(1)} %copy-done.13, bf16[33,256,128]{2,1,0:T(8,128)(2,1)S(1)} %filter_spec.1.filter_ref, bf16[72,32]{1,0:T(8,128)(2,1)S(1)} %copy-done.23, bf16[33,256,256]{2,1,0:T(8,128)(2,1)S(1)} %bitcast.1, ...), custom_call_target="tpu_custom_call" | custom-call | bytes 48000000 | tf_op jit(solution)/shard_map/signal_grad/pallas_call | solution.py:164
  85.4 1.4 copy-done.14
  86.8 1.0 copy-done.20
  87.8 1.4 all-to-all-done.data_ref
  89.1 7.0 %all-to-all-start.3 = ((bf16[32,128,128]{2,1,0:T(8,128)(2,1)}), bf16[32,128,128]{2,1,0:T(8,128)(2,1)}, u32[]{:S(2)}, u32[]{:S(2)}) async-start(bf16[32,128,128]{2,1,0:T(8,128)(2,1)} %copy-done.20), calls=%async_computation.3 | async-start | bytes 2097152 | tf_op jit(solution)/shard_map/all_to_all | solution.py:326
  96.1 2.2 copy-done.2
  99.1 14.3 %conv_out.1 = (bf16[33,256,128]{2,1,0:T(8,128)(2,1)S(1)}, bf16[32,128,128]{2,1,0:T(8,128)(2,1)S(1)}) custom-call(bf16[32,128,128]{2,1,0:T(8,128)(2,1)} %all-to-all-done.data_ref, bf16[33,256,128]{2,1,0:T(8,128)(2,1)S(1)} %filter_spec.1.filter_ref, bf16[72,32]{1,0:T(8,128)(2,1)S(1)} %copy-done.24, bf16[33,256,256]{2,1,0:T(8,128)(2,1)S(1)} %copy-done.2, ...), custom_call_target="tpu_custom_call" | custom-call | bytes 48000000 | tf_op jit(solution)/shard_map/conv_out/pallas_call | solution.py:164
  113.4 1.4 copy-done.16
  114.8 1.0 copy-done.19
  115.8 8.7 %all-to-all-done.3.sig_ref = bf16[32,128,128]{2,1,0:T(8,128)(2,1)} async-done(((bf16[32,128,128]{2,1,0:T(8,128)(2,1)}), bf16[32,128,128]{2,1,0:T(8,128)(2,1)}, u32[]{:S(2)}, u32[]{:S(2)}) %all-to-all-start.3) | async-done | bytes 1048608 | tf_op jit(solution)/shard_map/all_to_all | solution.py:326
  124.5 4.7 %all-to-all-start.1 = ((bf16[32,128,128]{2,1,0:T(8,128)(2,1)}), bf16[32,128,128]{2,1,0:T(8,128)(2,1)}, u32[]{:S(2)}, u32[]{:S(2)}) async-start(bf16[32,128,128]{2,1,0:T(8,128)(2,1)} %copy-done.19), calls=%async_computation.1 | async-start | bytes 2097152 | tf_op jit(solution)/shard_map/all_to_all | solution.py:326
  129.2 0.8 copy-done.22
  130.0 7.4 %input_grads.1 = (bf16[128,4096]{1,0:T(8,128)(2,1)}, bf16[128,4096]{1,0:T(8,128)(2,1)}, f32[8,4096]{1,0:T(8,128)S(1)}, bf16[8,4096]{1,0:T(8,128)(2,1)S(1)}, bf16[8,4096]{1,0:T(8,128)(2,1)S(1)}) custom-call(bf16[32,128,128]{2,1,0:T(8,128)(2,1)} %all-to-all-done.3.sig_ref, bf16[128,4096]{1,0:T(8,128)(2,1)S(1)} %copy-done.5, bf16[128,4096]{1,0:T(8,128)(2,1)S(1)} %copy-done.7, ...), custom_call_target="tpu_custom_call" | custom-call | bytes 18000000 | tf_op jit(solution)/shard_map/input_grads/pallas_call | solution.py:304
  138.8 18.7 %all-to-all-done.1.conv_ref = bf16[32,128,128]{2,1,0:T(8,128)(2,1)} async-done(((bf16[32,128,128]{2,1,0:T(8,128)(2,1)}), bf16[32,128,128]{2,1,0:T(8,128)(2,1)}, u32[]{:S(2)}, u32[]{:S(2)}) %all-to-all-start.1) | async-done | bytes 1048608 | tf_op jit(solution)/shard_map/all_to_all | solution.py:326
  157.5 1.2 copy-done.11
  158.7 6.3 %output_grads.1 = (bf16[128,4096]{1,0:T(8,128)(2,1)}, bf16[128,4096]{1,0:T(8,128)(2,1)}, f32[8,4096]{1,0:T(8,128)S(1)}, bf16[8,4096]{1,0:T(8,128)(2,1)S(1)}, bf16[8,4096]{1,0:T(8,128)(2,1)S(1)}) custom-call(bf16[32,128,128]{2,1,0:T(8,128)(2,1)} %all-to-all-done.1.conv_ref, bf16[128,4096]{1,0:T(8,128)(2,1)S(1)} %copy-done.9, ...), custom_call_target="tpu_custom_call" | custom-call | bytes 15000000 | tf_op jit(solution)/shard_map/output_grads/pallas_call | solution.py:304
  165.2 2.5 %collective-permute-start.4 = (f32[8,4096]{1,0:T(8,128)S(1)}, f32[8,4096]{1,0:T(8,128)S(1)}, u32[]{:S(2)}, u32[]{:S(2)}) collective-permute-start(f32[8,4096]{1,0:T(8,128)S(1)} %add.30), channel_id=1, source_target_pairs={{0,2},{1,3},{2,0},{3,1},{4,6},{5,7},{6,4},{7,5},{8,10},{9,11},{10,... | collective-permute-start | bytes 393224 | tf_op jit(solution)/shard_map/ppermute | solution.py:320
  167.7 1.3 collective-permute-start.9
  169.0 3.0 %collective-permute-done.4 = f32[8,4096]{1,0:T(8,128)S(1)} collective-permute-done((f32[8,4096]{1,0:T(8,128)S(1)}, f32[8,4096]{1,0:T(8,128)S(1)}, u32[]{:S(2)}, u32[]{:S(2)}) %collective-permute-start.4) | collective-permute-done | bytes 131104 | tf_op jit(solution)/shard_map/ppermute | solution.py:320
  172.8 1.8 collective-permute-done.9
  175.2 9.8 %collective-permute-done.5 = f32[8,4096]{1,0:T(8,128)S(1)} collective-permute-done((f32[8,4096]{1,0:T(8,128)S(1)}, f32[8,4096]{1,0:T(8,128)S(1)}, u32[]{:S(2)}, u32[]{:S(2)}) %collective-permute-start.5) | collective-permute-done | bytes 131104 | tf_op jit(solution)/shard_map/ppermute | solution.py:320
  185.5 12.3 %collective-permute-done.10 = f32[8,4096]{1,0:T(8,128)S(1)} collective-permute-done((f32[8,4096]{1,0:T(8,128)S(1)}, f32[8,4096]{1,0:T(8,128)S(1)}, u32[]{:S(2)}, u32[]{:S(2)}) %collective-permute-start.10) | collective-permute-done | bytes 131104 | tf_op jit(solution)/shard_map/ppermute | solution.py:320
  198.1 1.8 collective-permute-start.7
  199.9 1.3 collective-permute-start.2
  201.2 1.3 collective-permute-start.1
  202.5 2.2 copy-done
  204.7 7.6 %grad_long.1 = f32[4096,128]{1,0:T(8,128)} custom-call(bf16[33,256,128]{2,1,0:T(8,128)(2,1)S(1)} %copy-done.17, bf16[33,256,128]{2,1,0:T(8,128)(2,1)S(1)} %copy-done.15, bf16[33,256,256]{2,1,0:T(8,128)(2,1)S(1)} %copy-done, bf16[32,72]{1,0:T(8,128)(2,1)S(1)} %copy-done.25), custom_call_target="tpu_custom_call" | custom-call | bytes 30000000 | tf_op jit(solution)/shard_map/grad_long/pallas_call | solution.py:164
  212.3 4.2 %finish_output_grad.1 = bf16[128,4096]{1,0:T(8,128)(2,1)} custom-call(bf16[128,4096]{1,0:T(8,128)(2,1)} %get-tuple-element.31.refs_0_, bf16[8,4096]{1,0:T(8,128)(2,1)S(1)} %collective-permute-done.2.refs_1_, bf16[8,4096]{1,0:T(8,128)(2,1)S(1)} %get-tuple-element.33.refs_2_, f32[3,3,4096]{2,1,0:T(4,128)S(1)} %copy-done.4), custom_call_target="tpu_custom_call", output_to_operand_aliasing={{}: (0, {})} | custom-call | bytes 6000000 | tf_op jit(solution)/shard_map/finish_output_grad/pallas_call | solution.py:304
  216.5 4.3 %finish_input_grads.1 = (bf16[128,4096]{1,0:T(8,128)(2,1)}, bf16[128,4096]{1,0:T(8,128)(2,1)}) custom-call(bf16[128,4096]{1,0:T(8,128)(2,1)} %get-tuple-element.25.refs_0_, bf16[128,4096]{1,0:T(8,128)(2,1)} %get-tuple-element.26.refs_1_, bf16[8,4096]{1,0:T(8,128)(2,1)S(1)} %collective-permute-done.1.refs_2_, ...), custom_call_target="tpu_custom_call", output_to_operand_aliasing={{0}: (0, {}), {1}: (1, {})} | custom-call | bytes 6000000 | tf_op jit(solution)/shard_map/finish_input_grads/pallas_call | solution.py:304
  220.8 3.1 %collective-permute-start.12 = (f32[8,4096]{1,0:T(8,128)S(1)}, f32[8,4096]{1,0:T(8,128)S(1)}, u32[]{:S(2)}, u32[]{:S(2)}) collective-permute-start(f32[8,4096]{1,0:T(8,128)S(1)} %add.38), channel_id=1, source_target_pairs={{0,16},{1,17},{2,18},{3,19},{4,20},{5,21},{6,22},{7,23},{8,24},{9,... | collective-permute-start | bytes 393224 | tf_op jit(solution)/shard_map/ppermute | solution.py:320
  223.9 4.1 %collective-permute-done.12 = f32[8,4096]{1,0:T(8,128)S(1)} collective-permute-done((f32[8,4096]{1,0:T(8,128)S(1)}, f32[8,4096]{1,0:T(8,128)S(1)}, u32[]{:S(2)}, u32[]{:S(2)}) %collective-permute-start.12) | collective-permute-done | bytes 131104 | tf_op jit(solution)/shard_map/ppermute | solution.py:320
  (81 shorter events, 6.1 us)
Async XLA Ops:
  3.4 2.6 %collective-permute-start = (bf16[8,4096]{1,0:T(8,128)(2,1)S(1)}, bf16[8,4096]{1,0:T(8,128)(2,1)S(1)}, u32[]{:S(2)}, u32[]{:S(2)}) collective-permute-start(bf16[8,4096]{1,0:T(8,128)(2,1)S(1)} %maximum_maximum_fusion), channel_id=1, source_target_pairs={{0,1},{1,2},{2,3},{3,4},{4,5},{5,6},{6,7},{7,8},{8,9},{9,10},{10,1... | collective-permute-start | bytes 196616 | tf_op jit(solution)/shard_map/ppermute | solution.py:341
  6.0 0.9 copy-start.3
  6.9 1.2 copy-start.8
  8.2 1.2 copy-start.10
  9.4 17.4 %copy-start.21 = (bf16[8,4096]{1,0:T(8,128)(2,1)}, bf16[8,4096]{1,0:T(8,128)(2,1)S(1)}, u32[]{:S(2)}) copy-start(bf16[8,4096]{1,0:T(8,128)(2,1)S(1)} %collective-permute-done.halo_ref) | copy-start | bytes 196612
  9.4 17.4 %copy-start.4 = (f32[3,3,4096]{2,1,0:T(4,128)S(1)}, f32[3,3,4096]{2,1,0:T(4,128)}, u32[]{:S(2)}) copy-start(f32[3,3,4096]{2,1,0:T(4,128)} %refs_3_.1) | copy-start | bytes 442372
  9.4 17.4 %copy-start.5 = (bf16[128,4096]{1,0:T(8,128)(2,1)S(1)}, bf16[128,4096]{1,0:T(8,128)(2,1)}, u32[]{:S(2)}) copy-start(bf16[128,4096]{1,0:T(8,128)(2,1)} %gate_ref.3) | copy-start | bytes 3145732
  9.4 17.4 %copy-start.6 = (bf16[128,4096]{1,0:T(8,128)(2,1)S(1)}, bf16[128,4096]{1,0:T(8,128)(2,1)}, u32[]{:S(2)}) copy-start(bf16[128,4096]{1,0:T(8,128)(2,1)} %value_ref.3) | copy-start | bytes 3145732
  12.8 42.3 %all-to-all-start.2 = ((bf16[32,128,128]{2,1,0:T(8,128)(2,1)}), bf16[32,128,128]{2,1,0:T(8,128)(2,1)S(1)}, u32[]{:S(2)}, u32[]{:S(2)}) async-start(bf16[32,128,128]{2,1,0:T(8,128)(2,1)} %outer.1), calls=%async_computation.2 | async-start | bytes 2097152 | tf_op jit(solution)/shard_map/all_to_all | solution.py:326
  55.2 1.0 copy-start.12
  55.2 16.2 %slice-start = ((s8[4325376]{0:T(1024)(128)(4,1)}), s8[131072]{0:T(1024)(128)(4,1)S(1)}, s32[]{:S(2)}) async-start(s8[4325376]{0:T(1024)(128)(4,1)} %bitcast), calls=%async_computation.4 | async-start | bytes 262144
  56.1 33.0 %all-to-all-start = ((bf16[32,128,128]{2,1,0:T(8,128)(2,1)}), bf16[32,128,128]{2,1,0:T(8,128)(2,1)}, u32[]{:S(2)}, u32[]{:S(2)}) async-start(bf16[32,128,128]{2,1,0:T(8,128)(2,1)} %signal.1), calls=%async_computation | async-start | bytes 2097152 | tf_op jit(solution)/shard_map/all_to_all | solution.py:326
  60.8 2.2 copy-start.1
  63.0 1.6 copy-start.18
  64.6 0.7 copy-start.28
  65.3 6.0 %slice-start.1 = ((s8[4325376]{0:T(1024)(128)(4,1)}), s8[4194304]{0:T(1024)(128)(4,1)S(1)}, s32[]{:S(2)}) async-start(s8[4325376]{0:T(1024)(128)(4,1)} %bitcast), calls=%async_computation.5 | async-start | bytes 8388608
  65.3 6.0 %copy-start.13 = (bf16[32,128,128]{2,1,0:T(8,128)(2,1)S(1)}, bf16[32,128,128]{2,1,0:T(8,128)(2,1)}, u32[]{:S(2)}) copy-start(bf16[32,128,128]{2,1,0:T(8,128)(2,1)} %copy-done.12) | copy-start | bytes 3145732
  65.3 6.0 %copy-start.23 = (bf16[72,32]{1,0:T(8,128)(2,1)S(1)}, bf16[72,32]{1,0:T(8,128)(2,1)}, u32[]{:S(2)}) copy-start(bf16[72,32]{1,0:T(8,128)(2,1)} %constant.12.clone.coarse_ref) | copy-start | bytes 13828
  65.4 6.0 %copy-start.25 = (bf16[32,72]{1,0:T(8,128)(2,1)S(1)}, bf16[32,72]{1,0:T(8,128)(2,1)}, u32[]{:S(2)}) copy-start(bf16[32,72]{1,0:T(8,128)(2,1)} %constant.16.clone.back_ref) | copy-start | bytes 13828
  85.4 1.4 copy-start.14
  86.8 1.0 copy-start.20
  89.1 35.3 %all-to-all-start.3 = ((bf16[32,128,128]{2,1,0:T(8,128)(2,1)}), bf16[32,128,128]{2,1,0:T(8,128)(2,1)}, u32[]{:S(2)}, u32[]{:S(2)}) async-start(bf16[32,128,128]{2,1,0:T(8,128)(2,1)} %copy-done.20), calls=%async_computation.3 | async-start | bytes 2097152 | tf_op jit(solution)/shard_map/all_to_all | solution.py:326
  96.1 2.2 copy-start.2
  98.4 0.7 copy-start.24
  113.4 1.4 copy-start.16
  114.8 1.0 copy-start.19
  115.8 13.4 %copy-start.7 = (bf16[128,4096]{1,0:T(8,128)(2,1)S(1)}, bf16[128,4096]{1,0:T(8,128)(2,1)}, u32[]{:S(2)}) copy-start(bf16[128,4096]{1,0:T(8,128)(2,1)} %value_ref.3) | copy-start | bytes 3145732
  124.5 33.0 %all-to-all-start.1 = ((bf16[32,128,128]{2,1,0:T(8,128)(2,1)}), bf16[32,128,128]{2,1,0:T(8,128)(2,1)}, u32[]{:S(2)}, u32[]{:S(2)}) async-start(bf16[32,128,128]{2,1,0:T(8,128)(2,1)} %copy-done.19), calls=%async_computation.1 | async-start | bytes 2097152 | tf_op jit(solution)/shard_map/all_to_all | solution.py:326
  129.2 0.8 copy-start.22
  130.0 27.5 %copy-start.9 = (bf16[128,4096]{1,0:T(8,128)(2,1)S(1)}, bf16[128,4096]{1,0:T(8,128)(2,1)}, u32[]{:S(2)}) copy-start(bf16[128,4096]{1,0:T(8,128)(2,1)} %out_ref.3) | copy-start | bytes 3145732
  138.7 26.4 %collective-permute-start.3 = (f32[8,4096]{1,0:T(8,128)S(1)}, f32[8,4096]{1,0:T(8,128)S(1)}, u32[]{:S(2)}, u32[]{:S(2)}) collective-permute-start(f32[8,4096]{1,0:T(8,128)S(1)} %get-tuple-element.36), channel_id=1, source_target_pairs={{0,1},{1,0},{2,3},{3,2},{4,5},{5,4},{6,7},{7,6},{8,9},{9,8},{10,11... | collective-permute-start | bytes 393224 | tf_op jit(solution)/shard_map/ppermute | solution.py:320
  157.5 1.2 copy-start.11
  158.7 43.7 %copy-start.17 = (bf16[33,256,128]{2,1,0:T(8,128)(2,1)S(1)}, bf16[33,256,128]{2,1,0:T(8,128)(2,1)}, u32[]{:S(2)}) copy-start(bf16[33,256,128]{2,1,0:T(8,128)(2,1)} %copy-done.16) | copy-start | bytes 6488068
  165.1 36.1 %copy-start.30 = (bf16[8,4096]{1,0:T(8,128)(2,1)S(1)}, bf16[8,4096]{1,0:T(8,128)(2,1)}, u32[]{:S(2)}) copy-start(bf16[8,4096]{1,0:T(8,128)(2,1)} %copy-done.29) | copy-start | bytes 196612
  165.1 37.4 %copy-start.15 = (bf16[33,256,128]{2,1,0:T(8,128)(2,1)S(1)}, bf16[33,256,128]{2,1,0:T(8,128)(2,1)}, u32[]{:S(2)}) copy-start(bf16[33,256,128]{2,1,0:T(8,128)(2,1)} %copy-done.14) | copy-start | bytes 6488068
  165.1 2.6 %collective-permute-start.8 = (f32[8,4096]{1,0:T(8,128)S(1)}, f32[8,4096]{1,0:T(8,128)S(1)}, u32[]{:S(2)}, u32[]{:S(2)}) collective-permute-start(f32[8,4096]{1,0:T(8,128)S(1)} %get-tuple-element.37), channel_id=1, source_target_pairs={{0,1},{1,0},{2,3},{3,2},{4,5},{5,4},{6,7},{7,6},{8,9},{9,8},{10,11... | collective-permute-start | bytes 393224 | tf_op jit(solution)/shard_map/ppermute | solution.py:320
  165.2 6.9 %collective-permute-start.4 = (f32[8,4096]{1,0:T(8,128)S(1)}, f32[8,4096]{1,0:T(8,128)S(1)}, u32[]{:S(2)}, u32[]{:S(2)}) collective-permute-start(f32[8,4096]{1,0:T(8,128)S(1)} %add.30), channel_id=1, source_target_pairs={{0,2},{1,3},{2,0},{3,1},{4,6},{5,7},{6,4},{7,5},{8,10},{9,11},{10,... | collective-permute-start | bytes 393224 | tf_op jit(solution)/shard_map/ppermute | solution.py:320
  167.7 6.9 %collective-permute-start.9 = (f32[8,4096]{1,0:T(8,128)S(1)}, f32[8,4096]{1,0:T(8,128)S(1)}, u32[]{:S(2)}, u32[]{:S(2)}) collective-permute-start(f32[8,4096]{1,0:T(8,128)S(1)} %add.35), channel_id=1, source_target_pairs={{0,2},{1,3},{2,0},{3,1},{4,6},{5,7},{6,4},{7,5},{8,10},{9,11},{10,... | collective-permute-start | bytes 393224 | tf_op jit(solution)/shard_map/ppermute | solution.py:320
  172.0 12.9 %collective-permute-start.5 = (f32[8,4096]{1,0:T(8,128)S(1)}, f32[8,4096]{1,0:T(8,128)S(1)}, u32[]{:S(2)}, u32[]{:S(2)}) collective-permute-start(f32[8,4096]{1,0:T(8,128)S(1)} %add.31), channel_id=1, source_target_pairs={{0,4},{1,5},{2,6},{3,7},{4,0},{5,1},{6,2},{7,3},{8,12},{9,13},{10,... | collective-permute-start | bytes 393224 | tf_op jit(solution)/shard_map/ppermute | solution.py:320
  174.6 23.2 %collective-permute-start.10 = (f32[8,4096]{1,0:T(8,128)S(1)}, f32[8,4096]{1,0:T(8,128)S(1)}, u32[]{:S(2)}, u32[]{:S(2)}) collective-permute-start(f32[8,4096]{1,0:T(8,128)S(1)} %add.36), channel_id=1, source_target_pairs={{0,4},{1,5},{2,6},{3,7},{4,0},{5,1},{6,2},{7,3},{8,12},{9,13},{10,... | collective-permute-start | bytes 393224 | tf_op jit(solution)/shard_map/ppermute | solution.py:320
  185.0 13.1 %collective-permute-start.6 = (f32[8,4096]{1,0:T(8,128)S(1)}, f32[8,4096]{1,0:T(8,128)S(1)}, u32[]{:S(2)}, u32[]{:S(2)}) collective-permute-start(f32[8,4096]{1,0:T(8,128)S(1)} %add.32), channel_id=1, source_target_pairs={{0,8},{1,9},{2,10},{3,11},{4,12},{5,13},{6,14},{7,15},{8,0},{9,1},... | collective-permute-start | bytes 393224 | tf_op jit(solution)/shard_map/ppermute | solution.py:320
  197.8 23.0 %collective-permute-start.11 = (f32[8,4096]{1,0:T(8,128)S(1)}, f32[8,4096]{1,0:T(8,128)S(1)}, u32[]{:S(2)}, u32[]{:S(2)}) collective-permute-start(f32[8,4096]{1,0:T(8,128)S(1)} %add.37), channel_id=1, source_target_pairs={{0,8},{1,9},{2,10},{3,11},{4,12},{5,13},{6,14},{7,15},{8,0},{9,1},... | collective-permute-start | bytes 393224 | tf_op jit(solution)/shard_map/ppermute | solution.py:320
  198.1 25.9 %collective-permute-start.7 = (f32[8,4096]{1,0:T(8,128)S(1)}, f32[8,4096]{1,0:T(8,128)S(1)}, u32[]{:S(2)}, u32[]{:S(2)}) collective-permute-start(f32[8,4096]{1,0:T(8,128)S(1)} %add.33), channel_id=1, source_target_pairs={{0,16},{1,17},{2,18},{3,19},{4,20},{5,21},{6,22},{7,23},{8,24},{9,... | collective-permute-start | bytes 393224 | tf_op jit(solution)/shard_map/ppermute | solution.py:320
  199.9 12.5 %collective-permute-start.2 = (bf16[8,4096]{1,0:T(8,128)(2,1)S(1)}, bf16[8,4096]{1,0:T(8,128)(2,1)S(1)}, u32[]{:S(2)}, u32[]{:S(2)}) collective-permute-start(bf16[8,4096]{1,0:T(8,128)(2,1)S(1)} %get-tuple-element.32), channel_id=1, source_target_pairs={{1,0},{2,1},{3,2},{4,3},{5,4},{6,5},{7,6},{8,7},{9,8},{10,9},{11,1... | collective-permute-start | bytes 196616 | tf_op jit(solution)/shard_map/ppermute | solution.py:412
  201.2 15.4 %collective-permute-start.1 = (bf16[8,4096]{1,0:T(8,128)(2,1)S(1)}, bf16[8,4096]{1,0:T(8,128)(2,1)S(1)}, u32[]{:S(2)}, u32[]{:S(2)}) collective-permute-start(bf16[8,4096]{1,0:T(8,128)(2,1)S(1)} %copy-done.30), channel_id=1, source_target_pairs={{1,0},{2,1},{3,2},{4,3},{5,4},{6,5},{7,6},{8,7},{9,8},{10,9},{11,1... | collective-permute-start | bytes 196616 | tf_op jit(solution)/shard_map/ppermute | solution.py:392
  202.5 2.2 copy-start
  212.3 4.2 %copy-start.27 = (bf16[8,4096]{1,0:T(8,128)(2,1)S(1)}, bf16[8,4096]{1,0:T(8,128)(2,1)}, u32[]{:S(2)}) copy-start(bf16[8,4096]{1,0:T(8,128)(2,1)} %copy-done.26) | copy-start | bytes 196612
  220.8 7.2 %collective-permute-start.12 = (f32[8,4096]{1,0:T(8,128)S(1)}, f32[8,4096]{1,0:T(8,128)S(1)}, u32[]{:S(2)}, u32[]{:S(2)}) collective-permute-start(f32[8,4096]{1,0:T(8,128)S(1)} %add.38), channel_id=1, source_target_pairs={{0,16},{1,17},{2,18},{3,19},{4,20},{5,21},{6,22},{7,23},{8,24},{9,... | collective-permute-start | bytes 393224 | tf_op jit(solution)/shard_map/ppermute | solution.py:320
  (2 other events, 1.3 us)

commit v2 on v1

v2 whole, which is shorter than its diff:
```python
import functools

import jax
import jax.numpy as jnp
import ml_dtypes
import numpy as np
from jax import lax
from jax.experimental import pallas as pl
from jax.experimental.pallas import tpu as pltpu
from jax.sharding import PartitionSpec as P

bf16 = jnp.bfloat16
f32 = jnp.float32

TILE = 2048
GROUP = 8
PAD = 8


class Sizes:
    def __init__(self, blocks, rows, width):
        self.blocks, self.rows, self.width = blocks, rows, width
        self.half = blocks + 1
        self.parts = -(-2 * self.half // 8) * 8
        self.pitch = rows + PAD
        self.length = 2 * blocks * rows


def tables(z):
    a, b = np.arange(z.half), np.arange(z.blocks)
    turn = 2 * np.pi * ((a[:, None] * b[None, :]) % (2 * z.blocks)) / (2 * z.blocks)
    coarse = np.zeros((z.parts, z.blocks))
    coarse[0 : 2 * z.half : 2] = np.cos(turn)
    coarse[1 : 2 * z.half : 2] = -np.sin(turn)
    weight = np.where((a == 0) | (a == z.blocks), 1.0, 2.0) / z.length
    back = np.zeros((z.blocks, z.parts))
    back[:, 0 : 2 * z.half : 2] = (np.cos(turn) * weight[:, None]).T
    back[:, 1 : 2 * z.half : 2] = (-np.sin(turn) * weight[:, None]).T
    r = np.arange(z.rows)
    phase = ((a[:, None, None] + 2 * z.blocks * r[None, :, None]) * r[None, None, :]) % z.length
    cos_w, sin_w = np.cos(2 * np.pi * phase / z.length), np.sin(2 * np.pi * phase / z.length)
    fine = np.concatenate([np.concatenate([cos_w, sin_w], 2), np.concatenate([-sin_w, cos_w], 2)], 1)
    twice = np.concatenate([coarse, coarse], 1)
    return [t.astype(ml_dtypes.bfloat16) for t in (coarse, twice, fine, fine.transpose(0, 2, 1), back)]


def rows_at(z, block):
    return pl.ds(pl.multiple_of(block * z.pitch, 8), z.rows)


def coarse_forward(z, held, coarse_ref, parts, split):
    coarse = coarse_ref[...]

    def body(step, carry):
        columns = []
        for j in range(GROUP):
            value = held[pl.ds(step * GROUP + j, z.blocks, stride=z.pitch), :]
            high = value.astype(bf16)
            if split:
                high = jnp.concatenate([high, (value - high.astype(f32)).astype(bf16)], axis=0)
            columns.append(high)
        out = jnp.dot(coarse, jnp.concatenate(columns, axis=1), preferred_element_type=f32)
        for j in range(GROUP):
            parts[pl.ds(step * GROUP + j, z.parts, stride=z.pitch), :] = out[:, j * z.width : (j + 1) * z.width]
        return carry

    lax.fori_loop(0, z.rows // GROUP, body, 0)


def coarse_inverse(z, parts, back_ref, held):
    back = back_ref[...]

    def body(step, carry):
        columns = [parts[pl.ds(step * GROUP + j, z.parts, stride=z.pitch), :].astype(bf16) for j in range(GROUP)]
        out = jnp.dot(back, jnp.concatenate(columns, axis=1), preferred_element_type=f32)
        for j in range(GROUP):
            held[pl.ds(step * GROUP + j, z.blocks, stride=z.pitch), :] = out[:, j * z.width : (j + 1) * z.width]
        return carry

    lax.fori_loop(0, z.rows // GROUP, body, 0)


def fine_forward(z, fine_ref, parts, a):
    re = parts[rows_at(z, 2 * a), :].astype(bf16)
    im = parts[rows_at(z, 2 * a + 1), :].astype(bf16)
    return jnp.dot(fine_ref[a], jnp.concatenate([re, im], axis=0), preferred_element_type=f32)


def fine_inverse(z, fine_ref, targets, a, pairs):
    specs = [jnp.concatenate([re.astype(bf16), im.astype(bf16)], axis=0) for re, im in pairs]
    out = jnp.dot(fine_ref[a], jnp.concatenate(specs, axis=1), preferred_element_type=f32)
    for j, parts in enumerate(targets):
        parts[rows_at(z, 2 * a), :] = out[: z.rows, j * z.width : (j + 1) * z.width]
        parts[rows_at(z, 2 * a + 1), :] = out[z.rows :, j * z.width : (j + 1) * z.width]


def load_blocks(z, block_of, held):
    def body(i, carry):
        held[rows_at(z, i), :] = block_of(i).astype(f32)
        return carry

    lax.fori_loop(0, z.blocks, body, 0, unroll=4)


def store_blocks(z, held, out_ref):
    def body(i, carry):
        out_ref[i] = held[rows_at(z, i), :].astype(out_ref.dtype)
        return carry

    lax.fori_loop(0, z.blocks, body, 0, unroll=4)


def filter_kernel(z, filter_ref, twice_ref, fine_ref, spec_ref, held, parts):
    load_blocks(z, lambda i: filter_ref[pl.ds(pl.multiple_of(i * z.rows, 8), z.rows), :], held)
    coarse_forward(z, held, twice_ref, parts, True)

    def body(a, carry):
        spec_ref[a] = fine_forward(z, fine_ref, parts, a).astype(spec_ref.dtype)
        return carry

    lax.fori_loop(0, z.half, body, 0, unroll=3)


def times(spec, other, rows, conj):
    s_re, s_im, h_re, h_im = spec[:rows], spec[rows:], other[:rows], other[rows:]
    if conj:
        return s_re * h_re + s_im * h_im, s_im * h_re - s_re * h_im
    return s_re * h_re - s_im * h_im, s_re * h_im + s_im * h_re


def signal_grad_kernel(
    z, data_ref, filter_ref, coarse_ref, fine_ref, inv_ref, back_ref, spec_ref, out_ref, held, parts
):
    load_blocks(z, lambda i: data_ref[i], held)
    coarse_forward(z, held, coarse_ref, parts, False)

    def body(a, carry):
        spec = fine_forward(z, fine_ref, parts, a)
        spec_ref[a] = spec.astype(spec_ref.dtype)
        fine_inverse(z, inv_ref, (parts,), a, (times(spec, filter_ref[a].astype(f32), z.rows, True),))
        return carry

    lax.fori_loop(0, z.half, body, 0, unroll=3)
    coarse_inverse(z, parts, back_ref, held)
    store_blocks(z, held, out_ref)


def conv_out_kernel(
    z, data_ref, filter_ref, grad_ref, coarse_ref, fine_ref, inv_ref, back_ref, out_ref, long_ref, held, parts, more
):
    load_blocks(z, lambda i: data_ref[i], held)
    coarse_forward(z, held, coarse_ref, parts, False)
    spare = (z.parts - 2 * z.half) * z.pitch
    if spare:
        more[pl.ds(2 * z.half * z.pitch, spare), :] = jnp.zeros((spare, z.width), f32)

    def body(a, carry):
        spec = fine_forward(z, fine_ref, parts, a)
        conv = times(spec, filter_ref[a].astype(f32), z.rows, False)
        long = times(grad_ref[a].astype(f32), spec, z.rows, True)
        fine_inverse(z, inv_ref, (parts, more), a, (conv, long))
        return carry

    lax.fori_loop(0, z.half, body, 0, unroll=3)
    coarse_inverse(z, parts, back_ref, held)
    store_blocks(z, held, out_ref)
    coarse_inverse(z, more, back_ref, held)

    def done(i, carry):
        long_ref[pl.ds(pl.multiple_of(i * z.rows, 8), z.rows), :] = held[rows_at(z, i), :]
        return carry

    lax.fori_loop(0, z.blocks, done, 0, unroll=4)


def channel_call(z, kernel, operands, outs, name, cost_us, arrays=1):
    whole = pl.BlockSpec(memory_space=pltpu.VMEM)
    return pl.pallas_call(
        kernel,
        out_shape=outs,
        in_specs=[whole] * len(operands),
        out_specs=[whole] * len(outs),
        scratch_shapes=[
            pltpu.VMEM((z.blocks * z.pitch, z.width), f32),
        ]
        + [pltpu.VMEM((z.parts * z.pitch, z.width), f32)] * arrays,
        compiler_params=pltpu.CompilerParams(vmem_limit_bytes=(20 + 8 * arrays) << 20),
        cost_estimate=pl.CostEstimate(flops=0, bytes_accessed=int(cost_us * 3e6), transcendentals=0),
        name=name,
    )(*operands)


def delayed(rows, before, lag):
    moved = pltpu.roll(rows, lag, 0)
    index = lax.broadcasted_iota(jnp.int32, rows.shape, 0)
    for i in range(lag):
        moved = jnp.where(index == i, before[2 - lag + i : 3 - lag + i], moved)
    return moved


def feature(source, halo, which, taps_ref):
    rows = source.astype(f32)
    before = halo[2 * which : 2 * which + 2]
    one, two = delayed(rows, before, 1), delayed(rows, before, 2)
    taps = taps_ref[which]
    feat = taps[0:1] * rows + taps[1:2] * one + taps[2:3] * two
    return feat.astype(bf16).astype(f32), (rows, one, two)


def outward(out_ref, value):
    for j in range(value.shape[1] // out_ref.shape[2]):
        width = out_ref.shape[2]
        out_ref[j] = value[:, j * width : (j + 1) * width].astype(out_ref.dtype)


def inward(in_ref):
    return jnp.concatenate([in_ref[j] for j in range(in_ref.shape[0])], axis=1).astype(f32)


def outer_kernel(out_ref, cot_ref, taps_ref, outer_ref):
    feat_out, _ = feature(out_ref[...], jnp.zeros((8, out_ref.shape[1]), f32), 2, taps_ref)
    outward(outer_ref, feat_out * cot_ref[...].astype(f32))


def outer_head_kernel(old_ref, out_ref, cot_ref, halo_ref, taps_ref, outer_ref):
    feat_out, _ = feature(out_ref[...], halo_ref[...].astype(f32), 2, taps_ref)
    outward(outer_ref, feat_out * cot_ref[...].astype(f32))


def signal_kernel(gate_ref, value_ref, halo_ref, taps_ref, signal_ref):
    halo = halo_ref[...].astype(f32)
    feat_gate, _ = feature(gate_ref[...], halo, 0, taps_ref)
    feat_value, _ = feature(value_ref[...], halo, 1, taps_ref)
    outward(signal_ref, feat_gate * feat_value)


def edges_kernel(gate_ref, value_ref, out_ref, edge_ref):
    rows = [ref[...].astype(f32)[ref.shape[0] - 2 :] for ref in (gate_ref, value_ref, out_ref)]
    edge_ref[...] = collect(rows, 8, bf16)


def adjoint(grad, after, taps):
    index = lax.broadcasted_iota(jnp.int32, grad.shape, 0)
    last = grad.shape[0] - 1
    one = jnp.where(index == last, after[0:1], pltpu.roll(grad, last, 0))
    two = pltpu.roll(grad, last - 1, 0)
    two = jnp.where(index == last - 1, after[0:1], jnp.where(index == last, after[1:2], two))
    return (taps[0:1] * grad + taps[1:2] * one + taps[2:3] * two).astype(bf16)


def collect(pieces, rows, dtype):
    made = jnp.concatenate(pieces, axis=0)
    spare = rows - made.shape[0]
    if spare:
        made = jnp.concatenate([made, jnp.zeros((spare, made.shape[1]), made.dtype)], axis=0)
    return made.astype(dtype)


def lag_sums(grad, lags):
    return [jnp.sum(grad * lag, axis=0, keepdims=True) for lag in lags]


def store_sums(sums_ref, sums):
    made, width = jnp.concatenate(sums, axis=0), sums_ref.shape[2]
    for j in range(sums_ref.shape[0]):
        sums_ref[j] = made[:, j * width : (j + 1) * width]


def input_grads_kernel(
    sig_ref, gate_ref, value_ref, halo_ref, taps_ref, sums_ref, head_ref, tail_ref, grad_gate_ref, grad_value_ref
):
    halo = halo_ref[...].astype(f32)
    sig = inward(sig_ref)
    feat_gate, gate_lags = feature(gate_ref[...], halo, 0, taps_ref)
    feat_value, value_lags = feature(value_ref[...], halo, 1, taps_ref)
    gate_grad = (sig * feat_value).astype(bf16).astype(f32)
    value_grad = (sig * feat_gate).astype(bf16).astype(f32)
    store_sums(sums_ref, lag_sums(gate_grad, gate_lags) + lag_sums(value_grad, value_lags))
    count = sig.shape[0]
    head_ref[...] = collect([gate_grad[0:2], value_grad[0:2]], 8, bf16)
    tail_ref[...] = collect([gate_grad[count - 2 :], value_grad[count - 2 :]], 8, bf16)
    none = jnp.zeros((2, sig.shape[1]), f32)
    grad_gate_ref[...] = adjoint(gate_grad, none, taps_ref[0])
    grad_value_ref[...] = adjoint(value_grad, none, taps_ref[1])


def finish_kernel(gate_ref, value_ref, next_ref, tail_ref, taps_ref, grad_gate_ref, grad_value_ref):
    head, tail = next_ref[...].astype(f32), tail_ref[...].astype(f32)
    for k, (old_ref, new_ref) in enumerate(((gate_ref, grad_gate_ref), (value_ref, grad_value_ref))):
        taps = taps_ref[k]
        t0, t1 = tail[2 * k : 2 * k + 1], tail[2 * k + 1 : 2 * k + 2]
        h0, h1 = head[2 * k : 2 * k + 1], head[2 * k + 1 : 2 * k + 2]
        old = old_ref[...].astype(f32)
        index = lax.broadcasted_iota(jnp.int32, old.shape, 0)
        last = old.shape[0] - 1
        new = jnp.where(index == last - 1, taps[0:1] * t0 + taps[1:2] * t1 + taps[2:3] * h0, old)
        new = jnp.where(index == last, taps[0:1] * t1 + taps[1:2] * h0 + taps[2:3] * h1, new)
        new_ref[...] = new.astype(bf16)


def output_sums_kernel(conv_ref, out_ref, cot_ref, halo_ref, in_head_ref, sums_ref, head_ref):
    before = halo_ref[...].astype(f32)[4:6]
    out_grad = (cot_ref[...].astype(f32) * inward(conv_ref)).astype(bf16).astype(f32)
    rows = out_ref[...].astype(f32)
    lags = (rows, delayed(rows, before, 1), delayed(rows, before, 2))
    store_sums(sums_ref, lag_sums(out_grad, lags))
    head_ref[...] = collect([in_head_ref[...].astype(f32)[0:4], out_grad[0:2]], 8, bf16)


def mixed_kernel(conv_ref, out_ref, halo_ref, taps_ref, mixed_ref):
    feat_out, _ = feature(out_ref[...], halo_ref[...].astype(f32), 2, taps_ref)
    mixed_ref[...] = (feat_out * inward(conv_ref)).astype(bf16)


def output_grad_kernel(conv_ref, cot_ref, next_ref, taps_ref, grad_ref):
    out_grad = (cot_ref[...].astype(f32) * inward(conv_ref)).astype(bf16).astype(f32)
    grad_ref[...] = adjoint(out_grad, next_ref[...].astype(f32)[4:6], taps_ref[2])


def position_call(z, kernel, operands, kinds, out_kinds, channels, name, cost_us, tile=TILE, aliases=None, vmem=14):

    quarter = channels // 4

    def spec(kind):
        return {
            "rows": pl.BlockSpec((z.rows, tile), lambda i: (0, i)),
            "moved": pl.BlockSpec((tile // z.width, z.rows, z.width), lambda i: (i, 0, 0)),
            "edge": pl.BlockSpec((8, tile), lambda i: (0, i)),
            "six": pl.BlockSpec((tile // quarter, 6, quarter), lambda i: (i, 0, 0)),
            "three": pl.BlockSpec((tile // quarter, 3, quarter), lambda i: (i, 0, 0)),
            "taps": pl.BlockSpec((3, 3, tile), lambda i: (0, 0, i)),
            "first": pl.BlockSpec((16, tile), lambda i: (0, i)),
            "moved_first": pl.BlockSpec((tile // z.width, 16, z.width), lambda i: (i, 0, 0)),
            "last": pl.BlockSpec((16, tile), lambda i: (z.rows // 16 - 1, i)),
        }[kind]

    shapes = {
        "rows": jax.ShapeDtypeStruct((z.rows, channels), bf16),
        "last": jax.ShapeDtypeStruct((z.rows, channels), bf16),
        "moved": jax.ShapeDtypeStruct((channels // z.width, z.rows, z.width), bf16),
        "moved_first": jax.ShapeDtypeStruct((channels // z.width, z.rows, z.width), bf16),
        "edge": jax.ShapeDtypeStruct((8, channels), bf16),
        "six": jax.ShapeDtypeStruct((4, 6, quarter), f32),
        "three": jax.ShapeDtypeStruct((4, 3, quarter), f32),
    }
    return pl.pallas_call(
        kernel,
        grid=(channels // tile,),
        out_shape=[shapes[k] for k in out_kinds],
        in_specs=[spec(k) for k in kinds],
        out_specs=[spec(k) for k in out_kinds],
        input_output_aliases=aliases or {},
        compiler_params=pltpu.CompilerParams(vmem_limit_bytes=int(vmem * 2**20)),
        cost_estimate=pl.CostEstimate(flops=0, bytes_accessed=int(cost_us * 3e6), transcendentals=0),
        name=name,
    )(*operands)


class Sums:
    def __init__(self, size):
        self.size, self.depth, self.offsets = size, size // 4, (1, size // 2, size // 2 + 1)
        me = lax.axis_index("seq")
        self.quarter = me % 2 + 2 * (me // (size // 2))

    def swap(self, value, bits):
        return lax.ppermute(value, "seq", [(i, i ^ bits) for i in range(self.size)])

    def piece(self, value, which):
        return lax.dynamic_index_in_dim(value, which, 0, keepdims=False)

    def near(self, value):
        arrived = [self.swap(self.piece(value, self.quarter ^ (k + 1)), bits) for k, bits in enumerate(self.offsets)]
        return (self.piece(value, self.quarter) + arrived[0]) + (arrived[1] + arrived[2])

    def far(self, value):
        lines = [[self.size // 2 * x + 2 * z + core for z in range(self.depth)] for x in range(2) for core in range(2)]
        copies = jnp.broadcast_to(value[None], (self.depth, *value.shape))
        parts = lax.all_to_all(copies, "seq", split_axis=0, concat_axis=0, tiled=True, axis_index_groups=lines)
        return jnp.sum(parts, axis=0)

    def gather(self, value):
        held = jnp.stack([value] + [self.swap(value, bits) for bits in self.offsets])
        return jnp.stack([self.piece(held, self.quarter ^ j) for j in range(4)], axis=1)


def exchange(value):
    return lax.all_to_all(value, "seq", split_axis=0, concat_axis=0, tiled=True)


def local(size, gate_in, value_in, gate_out, cotangent, long_filter, short_filters):
    rows, channels = gate_in.shape
    z = Sizes(size, rows, long_filter.shape[1])
    coarse, twice, fine, inv, back = [jnp.asarray(t) for t in tables(z)]
    spec_shape = jax.ShapeDtypeStruct((z.half, 2 * z.rows, z.width), bf16)
    moved_shape = jax.ShapeDtypeStruct((z.blocks, z.rows, z.width), bf16)
    onward = [(i, i + 1) for i in range(size - 1)]
    backward = [(i + 1, i) for i in range(size - 1)]

    def position(kernel, operands, kinds, outs, name, cost_us, **more):
        return position_call(z, kernel, operands, kinds, outs, channels, name, cost_us, **more)

    (edges,) = position(edges_kernel, (gate_in, value_in, gate_out), ("last",) * 3, ("edge",), "edges", 1, tile=channels, vmem=60)
    halo = lax.ppermute(edges, "seq", onward)

    (outer,) = position(
        outer_kernel,
        (gate_out, cotangent, short_filters),
        ("rows", "rows", "taps"),
        ("moved",),
        "outer",
        4,
        vmem=59.5,
    )
    (outer,) = position(
        outer_head_kernel,
        (outer, gate_out, cotangent, halo, short_filters),
        ("moved_first", "first", "first", "edge", "taps"),
        ("moved_first",),
        "outer_head",
        1,
        tile=channels,
        aliases={0: 0},
        vmem=59.5,
    )
    (signal,) = position(
        signal_kernel, (gate_in, value_in, halo, short_filters), ("rows", "rows", "edge", "taps"), ("moved",), "signal", 4
    )
    outer_moved = exchange(outer)
    (filter_spec,) = channel_call(
        z, functools.partial(filter_kernel, z), (long_filter, twice, fine), (spec_shape,), "filter_spec", 8
    )
    signal, filter_spec = lax.optimization_barrier((signal, filter_spec))
    signal_moved = exchange(signal)
    outer_spec, sig_grad = channel_call(
        z,
        functools.partial(signal_grad_kernel, z),
        (outer_moved, filter_spec, coarse, fine, inv, back),
        (spec_shape, moved_shape),
        "signal_grad",
        16,
    )
    sig_rows = exchange(sig_grad)
    conv_out, grad_long = channel_call(
        z,
        functools.partial(conv_out_kernel, z),
        (signal_moved, filter_spec, outer_spec, coarse, fine, inv, back),
        (moved_shape, jax.ShapeDtypeStruct((z.blocks * z.rows, z.width), f32)),
        "conv_out",
        22,
        arrays=2,
    )
    conv_rows = exchange(conv_out)
    in_sums, in_head, in_tail, grad_gate, grad_value = position(
        input_grads_kernel,
        (sig_rows, gate_in, value_in, halo, short_filters),
        ("moved", "rows", "rows", "edge", "taps"),
        ("six", "edge", "edge", "rows", "rows"),
        "input_grads",
        6,
    )
    sums = Sums(size)
    conv_rows, grad_gate, grad_value, in_sums = lax.optimization_barrier(
        (conv_rows, grad_gate, grad_value, sums.near(in_sums))
    )
    out_sums, out_head = position(
        output_sums_kernel,
        (conv_rows, gate_out, cotangent, halo, in_head),
        ("moved", "rows", "rows", "edge", "edge"),
        ("three", "edge"),
        "output_sums",
        3,
    )
    out_sums, out_head = lax.optimization_barrier((sums.near(out_sums), out_head))
    after = lax.ppermute(out_head, "seq", backward)
    (mixed,) = position(
        mixed_kernel,
        (conv_rows, gate_out, halo, short_filters),
        ("moved", "rows", "edge", "taps"),
        ("rows",),
        "mixed",
        3,
    )
    both = jnp.concatenate([in_sums, out_sums], axis=0).reshape(9, -1, z.width)
    (grad_out,) = position(
        output_grad_kernel,
        (conv_rows, cotangent, after, short_filters),
        ("moved", "rows", "edge", "taps"),
        ("rows",),
        "output_grad",
        3,
    )
    both, grad_out = lax.optimization_barrier((sums.far(both), grad_out))
    grad_gate, grad_value = position(
        finish_kernel,
        (grad_gate, grad_value, after, in_tail, short_filters),
        ("last", "last", "edge", "edge", "taps"),
        ("last", "last"),
        "finish_input_grads",
        2,
        tile=channels,
        aliases={0: 0, 1: 1},
    )
    grad_short = sums.gather(both).reshape(3, 3, channels)
    return (mixed, grad_gate, grad_value, grad_out, grad_long, grad_short)


def solution(mesh):
    spread = P(("grp", "seq"), None)
    return jax.shard_map(
        functools.partial(local, mesh.shape["seq"]),
        mesh=mesh,
        in_specs=(spread, spread, spread, spread, P(None, "seq"), P()),
        out_specs=(spread, spread, spread, spread, P("grp", "seq"), P("grp", None, None)),
        check_vma=False,
    )
```

time: 232 us -> 184 us (0.79)
  waiting for transfers between devices: 85.4 us -> 53.7 us
  Pallas kernels: 71.5 us -> 59.2 us
  starting transfers between devices: 45.3 us -> 39.1 us
    ppermute x12 -> x10, waiting for transfers between devices: 31.2 us -> 9.05 us  [the longest x9 7.21 us: swap(): return lax.ppermute(value, 'seq', [(i, i ^ bits) for i in range(self.size)])]
    all_to_all x4, waiting for transfers between devices: 53.3 us -> 36.7 us  [exchange(): return lax.all_to_all(value, 'seq', split_axis=0, concat_axis=0, tiled=True)]
    all_to_all x0 -> x1, waiting for transfers between devices: none -> 7.92 us  [far(): lax.all_to_all(copies, 'seq', split_axis=0, concat_axis=0, tiled=True, ax...]
    pallas_call x6 -> x9, Pallas kernels: 29.5 us -> 22.6 us  [position_call(): pl.pallas_call(kernel, grid=(channels // tile,), out_shape=[shapes[k] for...]
    ppermute x12 -> x10, starting transfers between devices: 13.3 us -> 7.15 us  [the longest x9 5.86 us: swap(): return lax.ppermute(value, 'seq', [(i, i ^ bits) for i in range(self.size)])]
    pallas_call x4 -> x3, Pallas kernels: 41.9 us -> 36.7 us  [channel_call(): pl.pallas_call(kernel, out_shape=outs, in_specs=[whole] * len(operands),...]
    all_to_all x4, starting transfers between devices: 30.3 us -> 26.1 us  [exchange(): return lax.all_to_all(value, 'seq', split_axis=0, concat_axis=0, tiled=True)]
    all_to_all x0 -> x1, starting transfers between devices: none -> 4.06 us  [far(): lax.all_to_all(copies, 'seq', split_axis=0, concat_axis=0, tiled=True, ax...]
  transfers between devices with their start and end apart: 17 -> 16, of which waited for: 11 -> 10; matrix products, arithmetic and copies ran while one was open for 0% -> 1% of each run, Pallas kernels for 30% -> 30%
where the time goes in v2:
time: 184 us; the launch traced here: 182 us
  Pallas kernels  59.2 us (32%)
  waiting for transfers between devices  53.7 us (29%)
  starting transfers between devices  39.1 us (21%)
  local copies, waits for them, and re-layouts  26.1 us (14%)
  other arithmetic  2.45 us (1%)
    pallas_call x3, Pallas kernels, channel_call(): pl.pallas_call(kernel, out_shape=outs, in_specs=[whole] * len(operands),...  36.7 us
    all_to_all x4, waiting for transfers between devices, exchange(): return lax.all_to_all(value, 'seq', split_axis=0, concat_axis=0, tiled=True)  36.7 us
    all_to_all x4, starting transfers between devices, exchange(): return lax.all_to_all(value, 'seq', split_axis=0, concat_axis=0, tiled=True)  26.1 us
    unnamed x57, local copies, waits for them, and re-layouts  23.9 us
    pallas_call x9, Pallas kernels, position_call(): pl.pallas_call(kernel, grid=(channels // tile,), out_shape=[shapes[k] for...  22.6 us
    all_to_all x1, waiting for transfers between devices, far(): lax.all_to_all(copies, 'seq', split_axis=0, concat_axis=0, tiled=True, ax...  7.92 us
    ppermute x9, waiting for transfers between devices, swap(): return lax.ppermute(value, 'seq', [(i, i ^ bits) for i in range(self.size)])  7.21 us
    ppermute x9, starting transfers between devices, swap(): return lax.ppermute(value, 'seq', [(i, i ^ bits) for i in range(self.size)])  5.86 us
  transfers between devices with their start and end apart: 16, of which 10 were waited for; matrix products, arithmetic and copies ran while one was open for 1% of the time, Pallas kernels for 30%

profile of v2, /device:TPU:8, one launch (start us, length us, event | category | flops | bytes accessed | tf_op | source)
XLA Modules:
  0.0 181.5 jit_solution(9743403003481607501)
XLA Ops:
  0.6 1.7 edges.1
  2.3 1.7 collective-permute-start
  4.1 3.0 %outer.1.old_ref = bf16[32,128,128]{2,1,0:T(8,128)(2,1)} custom-call(bf16[128,4096]{1,0:T(8,128)(2,1)} %out_ref.9, bf16[128,4096]{1,0:T(8,128)(2,1)} %cot_ref.7, f32[3,3,4096]{2,1,0:T(4,128)} %taps_ref.13), custom_call_target="tpu_custom_call" | custom-call | bytes 12000000 | tf_op jit(solution)/shard_map/outer/pallas_call | solution.py:346
  7.7 2.0 %outer_head.1 = bf16[32,128,128]{2,1,0:T(8,128)(2,1)} custom-call(bf16[32,128,128]{2,1,0:T(8,128)(2,1)} %outer.1.old_ref, bf16[128,4096]{1,0:T(8,128)(2,1)} %out_ref.9, bf16[128,4096]{1,0:T(8,128)(2,1)} %cot_ref.7, bf16[8,4096]{1,0:T(8,128)(2,1)} %copy-done.16, f32[3,3,4096]{2,1,0:T(4,128)} %taps_ref.13), custom_call_target="tpu_custom_call", output_to_operand_aliasing={{}: (0, {})} | custom-call | bytes 3000000 | tf_op jit(solution)/shard_map/outer_head/pallas_call | solution.py:346
  9.7 12.1 %all-to-all-start.1 = ((bf16[32,128,128]{2,1,0:T(8,128)(2,1)}), bf16[32,128,128]{2,1,0:T(8,128)(2,1)}, u32[]{:S(2)}, u32[]{:S(2)}) async-start(bf16[32,128,128]{2,1,0:T(8,128)(2,1)} %outer_head.1), calls=%async_computation.1 | async-start | bytes 2097152 | tf_op jit(solution)/shard_map/all_to_all | solution.py:387
  21.9 2.2 %copy-done = bf16[33,256,256]{2,1,0:T(8,128)(2,1)S(1)} copy-done((bf16[33,256,256]{2,1,0:T(8,128)(2,1)S(1)}, bf16[33,256,256]{2,1,0:T(8,128)(2,1)}, u32[]{:S(2)}) %copy-start) | copy-done | bytes 4325400
  24.1 1.6 copy-done.15
  25.7 6.0 %filter_spec.1.filter_ref = bf16[33,256,128]{2,1,0:T(8,128)(2,1)S(1)} custom-call(f32[4096,128]{1,0:T(8,128)S(1)} %copy-done.15, bf16[72,64]{1,0:T(8,128)(2,1)S(1)} %copy-done.26, bf16[33,256,256]{2,1,0:T(8,128)(2,1)S(1)} %copy-done), custom_call_target="tpu_custom_call" | custom-call | bytes 24000000 | tf_op jit(solution)/shard_map/filter_spec/pallas_call | solution.py:178
  31.7 1.9 %signal.1 = bf16[32,128,128]{2,1,0:T(8,128)(2,1)S(1)} custom-call(bf16[128,4096]{1,0:T(8,128)(2,1)S(1)} %copy-done.8, bf16[128,4096]{1,0:T(8,128)(2,1)S(1)} %copy-done.10, bf16[8,4096]{1,0:T(8,128)(2,1)S(1)} %copy-done.17, f32[3,3,4096]{2,1,0:T(4,128)S(1)} %copy-done.7), custom_call_target="tpu_custom_call" | custom-call | bytes 12000000 | tf_op jit(solution)/shard_map/signal/pallas_call | solution.py:346
  33.7 1.0 copy-done.12
  34.6 15.5 %all-to-all-done.1.data_ref = bf16[32,128,128]{2,1,0:T(8,128)(2,1)} async-done(((bf16[32,128,128]{2,1,0:T(8,128)(2,1)}), bf16[32,128,128]{2,1,0:T(8,128)(2,1)}, u32[]{:S(2)}, u32[]{:S(2)}) %all-to-all-start.1) | async-done | bytes 1048608 | tf_op jit(solution)/shard_map/all_to_all | solution.py:387
  50.2 4.7 %all-to-all-start = ((bf16[32,128,128]{2,1,0:T(8,128)(2,1)}), bf16[32,128,128]{2,1,0:T(8,128)(2,1)}, u32[]{:S(2)}, u32[]{:S(2)}) async-start(bf16[32,128,128]{2,1,0:T(8,128)(2,1)} %copy-done.12), calls=%async_computation | async-start | bytes 2097152 | tf_op jit(solution)/shard_map/all_to_all | solution.py:387
  54.9 2.2 %copy-done.1 = bf16[33,256,256]{2,1,0:T(8,128)(2,1)S(1)} copy-done((bf16[33,256,256]{2,1,0:T(8,128)(2,1)S(1)}, bf16[33,256,256]{2,1,0:T(8,128)(2,1)}, u32[]{:S(2)}) %copy-start.1) | copy-done | bytes 4325400
  57.1 2.2 %copy-done.4 = bf16[33,256,256]{2,1,0:T(8,128)(2,1)S(1)} copy-done((bf16[33,256,256]{2,1,0:T(8,128)(2,1)S(1)}, bf16[33,256,256]{2,1,0:T(8,128)(2,1)}, u32[]{:S(2)}) %copy-start.4) | copy-done | bytes 4325400
  59.3 13.0 %signal_grad.1 = (bf16[33,256,128]{2,1,0:T(8,128)(2,1)S(1)}, bf16[32,128,128]{2,1,0:T(8,128)(2,1)S(1)}) custom-call(bf16[32,128,128]{2,1,0:T(8,128)(2,1)} %all-to-all-done.1.data_ref, bf16[33,256,128]{2,1,0:T(8,128)(2,1)S(1)} %filter_spec.1.filter_ref, bf16[72,32]{1,0:T(8,128)(2,1)S(1)} %copy-done.20, bf16[33,256,256]{2,1,0:T(8,128)(2,1)S(1)} %copy-done.1, ...), custom_call_target="tpu_custom_call" | custom-call | bytes 48000000 | tf_op jit(solution)/shard_map/signal_grad/pallas_call | solution.py:178
  72.4 1.4 copy-done.13
  73.7 1.0 copy-done.19
  74.7 8.5 %all-to-all-done.data_ref = bf16[32,128,128]{2,1,0:T(8,128)(2,1)} async-done(((bf16[32,128,128]{2,1,0:T(8,128)(2,1)}), bf16[32,128,128]{2,1,0:T(8,128)(2,1)}, u32[]{:S(2)}, u32[]{:S(2)}) %all-to-all-start) | async-done | bytes 1048608 | tf_op jit(solution)/shard_map/all_to_all | solution.py:387
  83.2 4.7 %all-to-all-start.3 = ((bf16[32,128,128]{2,1,0:T(8,128)(2,1)}), bf16[32,128,128]{2,1,0:T(8,128)(2,1)}, u32[]{:S(2)}, u32[]{:S(2)}) async-start(bf16[32,128,128]{2,1,0:T(8,128)(2,1)} %copy-done.19), calls=%async_computation.3 | async-start | bytes 2097152 | tf_op jit(solution)/shard_map/all_to_all | solution.py:387
  87.9 2.2 %copy-done.2 = bf16[33,256,256]{2,1,0:T(8,128)(2,1)S(1)} copy-done((bf16[33,256,256]{2,1,0:T(8,128)(2,1)S(1)}, bf16[33,256,256]{2,1,0:T(8,128)(2,1)}, u32[]{:S(2)}) %copy-start.2) | copy-done | bytes 4325400
  90.1 2.2 %copy-done.5 = bf16[33,256,256]{2,1,0:T(8,128)(2,1)S(1)} copy-done((bf16[33,256,256]{2,1,0:T(8,128)(2,1)S(1)}, bf16[33,256,256]{2,1,0:T(8,128)(2,1)}, u32[]{:S(2)}) %copy-start.5) | copy-done | bytes 4325400
  92.3 1.6 copy-done.14
  93.9 17.7 %conv_out.1 = (bf16[32,128,128]{2,1,0:T(8,128)(2,1)S(1)}, f32[4096,128]{1,0:T(8,128)}) custom-call(bf16[32,128,128]{2,1,0:T(8,128)(2,1)} %all-to-all-done.data_ref, bf16[33,256,128]{2,1,0:T(8,128)(2,1)S(1)} %filter_spec.1.filter_ref, bf16[33,256,128]{2,1,0:T(8,128)(2,1)S(1)} %copy-done.14, bf16[72,32]{1,0:T(8,128)(2,1)S(1)} %copy-done.20, ...), custom_call_target="tpu_custom_call" | custom-call | bytes 66000000 | tf_op jit(solution)/shard_map/conv_out/pallas_call | solution.py:178
  111.7 1.0 copy-done.18
  112.6 3.6 %all-to-all-done.3.sig_ref = bf16[32,128,128]{2,1,0:T(8,128)(2,1)} async-done(((bf16[32,128,128]{2,1,0:T(8,128)(2,1)}), bf16[32,128,128]{2,1,0:T(8,128)(2,1)}, u32[]{:S(2)}, u32[]{:S(2)}) %all-to-all-start.3) | async-done | bytes 1048608 | tf_op jit(solution)/shard_map/all_to_all | solution.py:387
  116.2 4.6 %all-to-all-start.2 = ((bf16[32,128,128]{2,1,0:T(8,128)(2,1)}), bf16[32,128,128]{2,1,0:T(8,128)(2,1)S(1)}, u32[]{:S(2)}, u32[]{:S(2)}) async-start(bf16[32,128,128]{2,1,0:T(8,128)(2,1)} %copy-done.18), calls=%async_computation.2 | async-start | bytes 2097152 | tf_op jit(solution)/shard_map/all_to_all | solution.py:387
  120.9 1.4 copy-done.9
  122.3 1.2 copy-done.11
  123.5 6.7 %input_grads.1 = (f32[4,6,1024]{2,1,0:T(8,128)S(1)}, bf16[8,4096]{1,0:T(8,128)(2,1)S(1)}, bf16[8,4096]{1,0:T(8,128)(2,1)S(1)}, bf16[128,4096]{1,0:T(8,128)(2,1)}, bf16[128,4096]{1,0:T(8,128)(2,1)}) custom-call(bf16[32,128,128]{2,1,0:T(8,128)(2,1)} %all-to-all-done.3.sig_ref, bf16[128,4096]{1,0:T(8,128)(2,1)S(1)} %copy-done.9, ...), custom_call_target="tpu_custom_call" | custom-call | bytes 18000000 | tf_op jit(solution)/shard_map/input_grads/pallas_call | solution.py:346
  132.3 1.7 collective-permute-start.2
  134.0 2.6 %collective-permute-done.2 = f32[6,1024]{1,0:T(8,128)} collective-permute-done((f32[6,1024]{1,0:T(8,128)}, f32[6,1024]{1,0:T(8,128)}, u32[]{:S(2)}, u32[]{:S(2)}) %collective-permute-start.2) | collective-permute-done | bytes 24608 | tf_op jit(solution)/shard_map/ppermute | solution.py:366
  136.7 2.1 %collective-permute-done.3 = f32[6,1024]{1,0:T(8,128)} collective-permute-done((f32[6,1024]{1,0:T(8,128)}, f32[6,1024]{1,0:T(8,128)}, u32[]{:S(2)}, u32[]{:S(2)}) %collective-permute-start.3) | collective-permute-done | bytes 24608 | tf_op jit(solution)/shard_map/ppermute | solution.py:366
  138.8 1.4 fusion
  140.2 9.0 %all-to-all-done.2.conv_ref = bf16[32,128,128]{2,1,0:T(8,128)(2,1)S(1)} async-done(((bf16[32,128,128]{2,1,0:T(8,128)(2,1)}), bf16[32,128,128]{2,1,0:T(8,128)(2,1)S(1)}, u32[]{:S(2)}, u32[]{:S(2)}) %all-to-all-start.2) | async-done | bytes 1048608 | tf_op jit(solution)/shard_map/all_to_all | solution.py:387
  149.3 0.8 copy-done.24
  150.1 1.5 output_sums.1
  151.7 1.0 collective-permute-start.5
  152.7 0.9 collective-permute-start.6
  153.6 2.2 %collective-permute-done.5 = f32[3,1024]{1,0:T(4,128)S(1)} collective-permute-done((f32[3,1024]{1,0:T(4,128)S(1)}, f32[3,1024]{1,0:T(4,128)S(1)}, u32[]{:S(2)}, u32[]{:S(2)}) %collective-permute-start.5) | collective-permute-done | bytes 12320 | tf_op jit(solution)/shard_map/ppermute | solution.py:366
  156.8 4.1 %all-to-all-start.4 = ((f32[8,9,8,128]{3,2,1,0:T(8,128)}), f32[8,9,8,128]{3,2,1,0:T(8,128)}, u32[]{:S(2)}, u32[]{:S(2)}) async-start(f32[8,9,8,128]{3,2,1,0:T(8,128)} %broadcast_in_dim.8), calls=%async_computation.4 | async-start | bytes 589824 | tf_op jit(solution)/shard_map/all_to_all | solution.py:378
  160.9 1.3 collective-permute-start.7
  162.2 1.8 %collective-permute-done.7.next_ref = bf16[8,4096]{1,0:T(8,128)(2,1)S(1)} collective-permute-done((bf16[8,4096]{1,0:T(8,128)(2,1)S(1)}, bf16[8,4096]{1,0:T(8,128)(2,1)S(1)}, u32[]{:S(2)}, u32[]{:S(2)}) %collective-permute-start.7) | collective-permute-done | bytes 65568 | tf_op jit(solution)/shard_map/ppermute | solution.py:474
  164.0 2.1 %output_grad.1 = bf16[128,4096]{1,0:T(8,128)(2,1)} custom-call(bf16[32,128,128]{2,1,0:T(8,128)(2,1)S(1)} %all-to-all-done.2.conv_ref, bf16[128,4096]{1,0:T(8,128)(2,1)S(1)} %copy-done.6, bf16[8,4096]{1,0:T(8,128)(2,1)S(1)} %collective-permute-done.7.next_ref, f32[3,3,4096]{2,1,0:T(4,128)S(1)} %copy-done.7), custom_call_target="tpu_custom_call" | custom-call | bytes 9000000 | tf_op jit(solution)/shard_map/output_grad/pallas_call | solution.py:346
  166.1 7.9 %all-to-all-done.4 = f32[8,9,8,128]{3,2,1,0:T(8,128)} async-done(((f32[8,9,8,128]{3,2,1,0:T(8,128)}), f32[8,9,8,128]{3,2,1,0:T(8,128)}, u32[]{:S(2)}, u32[]{:S(2)}) %all-to-all-start.4) | async-done | bytes 294944 | tf_op jit(solution)/shard_map/all_to_all | solution.py:378
  174.0 1.0 reduce_sum.9
  175.0 1.0 collective-permute-start.10
  177.0 2.0 %mixed.1 = bf16[128,4096]{1,0:T(8,128)(2,1)} custom-call(bf16[32,128,128]{2,1,0:T(8,128)(2,1)S(1)} %all-to-all-done.2.conv_ref, bf16[128,4096]{1,0:T(8,128)(2,1)S(1)} %copy-done.3, bf16[8,4096]{1,0:T(8,128)(2,1)S(1)} %copy-done.17, f32[3,3,4096]{2,1,0:T(4,128)S(1)} %copy-done.7), custom_call_target="tpu_custom_call" | custom-call | bytes 9000000 | tf_op jit(solution)/shard_map/mixed/pallas_call | solution.py:346
  178.9 1.8 finish_input_grads.1
  (65 shorter events, 5.8 us)
Async XLA Ops:
  2.3 4.8 %collective-permute-start = (bf16[8,4096]{1,0:T(8,128)(2,1)}, bf16[8,4096]{1,0:T(8,128)(2,1)S(1)}, u32[]{:S(2)}, u32[]{:S(2)}) collective-permute-start(bf16[8,4096]{1,0:T(8,128)(2,1)} %edges.1), channel_id=1, source_target_pairs={{0,1},{1,2},{2,3},{3,4},{4,5},{5,6},{6,7},{7,8},{8,9},{9,10},{10,1... | collective-permute-start | bytes 196616 | tf_op jit(solution)/shard_map/ppermute | solution.py:403
  7.1 14.7 %copy-start.26 = (bf16[72,64]{1,0:T(8,128)(2,1)S(1)}, bf16[72,64]{1,0:T(8,128)(2,1)}, u32[]{:S(2)}) copy-start(bf16[72,64]{1,0:T(8,128)(2,1)} %constant.77.clone.twice_ref) | copy-start | bytes 27652
  7.1 0.6 copy-start.16
  9.7 40.5 %all-to-all-start.1 = ((bf16[32,128,128]{2,1,0:T(8,128)(2,1)}), bf16[32,128,128]{2,1,0:T(8,128)(2,1)}, u32[]{:S(2)}, u32[]{:S(2)}) async-start(bf16[32,128,128]{2,1,0:T(8,128)(2,1)} %outer_head.1), calls=%async_computation.1 | async-start | bytes 2097152 | tf_op jit(solution)/shard_map/all_to_all | solution.py:387
  21.8 2.2 %copy-start = (bf16[33,256,256]{2,1,0:T(8,128)(2,1)S(1)}, bf16[33,256,256]{2,1,0:T(8,128)(2,1)}, u32[]{:S(2)}) copy-start(bf16[33,256,256]{2,1,0:T(8,128)(2,1)} %constant.78.clone.fine_ref) | copy-start | bytes 12976132
  24.1 1.6 copy-start.15
  25.7 6.0 %copy-start.7 = (f32[3,3,4096]{2,1,0:T(4,128)S(1)}, f32[3,3,4096]{2,1,0:T(4,128)}, u32[]{:S(2)}) copy-start(f32[3,3,4096]{2,1,0:T(4,128)} %taps_ref.13) | copy-start | bytes 442372
  25.7 6.0 %copy-start.8 = (bf16[128,4096]{1,0:T(8,128)(2,1)S(1)}, bf16[128,4096]{1,0:T(8,128)(2,1)}, u32[]{:S(2)}) copy-start(bf16[128,4096]{1,0:T(8,128)(2,1)} %gate_ref.5) | copy-start | bytes 3145732
  25.7 6.0 %copy-start.10 = (bf16[128,4096]{1,0:T(8,128)(2,1)S(1)}, bf16[128,4096]{1,0:T(8,128)(2,1)}, u32[]{:S(2)}) copy-start(bf16[128,4096]{1,0:T(8,128)(2,1)} %value_ref.5) | copy-start | bytes 3145732
  25.7 6.0 %copy-start.17 = (bf16[8,4096]{1,0:T(8,128)(2,1)S(1)}, bf16[8,4096]{1,0:T(8,128)(2,1)}, u32[]{:S(2)}) copy-start(bf16[8,4096]{1,0:T(8,128)(2,1)} %copy-done.16) | copy-start | bytes 196612
  31.7 23.2 %copy-start.20 = (bf16[72,32]{1,0:T(8,128)(2,1)S(1)}, bf16[72,32]{1,0:T(8,128)(2,1)}, u32[]{:S(2)}) copy-start(bf16[72,32]{1,0:T(8,128)(2,1)} %constant.76.clone.coarse_ref) | copy-start | bytes 13828
  31.7 23.2 %copy-start.25 = (bf16[32,72]{1,0:T(8,128)(2,1)S(1)}, bf16[32,72]{1,0:T(8,128)(2,1)}, u32[]{:S(2)}) copy-start(bf16[32,72]{1,0:T(8,128)(2,1)} %constant.80.clone.back_ref) | copy-start | bytes 13828
  33.7 1.0 copy-start.12
  50.2 33.0 %all-to-all-start = ((bf16[32,128,128]{2,1,0:T(8,128)(2,1)}), bf16[32,128,128]{2,1,0:T(8,128)(2,1)}, u32[]{:S(2)}, u32[]{:S(2)}) async-start(bf16[32,128,128]{2,1,0:T(8,128)(2,1)} %copy-done.12), calls=%async_computation | async-start | bytes 2097152 | tf_op jit(solution)/shard_map/all_to_all | solution.py:387
  54.9 2.2 %copy-start.1 = (bf16[33,256,256]{2,1,0:T(8,128)(2,1)S(1)}, bf16[33,256,256]{2,1,0:T(8,128)(2,1)}, u32[]{:S(2)}) copy-start(bf16[33,256,256]{2,1,0:T(8,128)(2,1)} %constant.78.clone.fine_ref) | copy-start | bytes 12976132
  57.1 2.2 %copy-start.4 = (bf16[33,256,256]{2,1,0:T(8,128)(2,1)S(1)}, bf16[33,256,256]{2,1,0:T(8,128)(2,1)}, u32[]{:S(2)}) copy-start(bf16[33,256,256]{2,1,0:T(8,128)(2,1)} %constant.79.clone.inv_ref) | copy-start | bytes 12976132
  72.4 1.4 copy-start.13
  73.7 1.0 copy-start.19
  83.2 33.0 %all-to-all-start.3 = ((bf16[32,128,128]{2,1,0:T(8,128)(2,1)}), bf16[32,128,128]{2,1,0:T(8,128)(2,1)}, u32[]{:S(2)}, u32[]{:S(2)}) async-start(bf16[32,128,128]{2,1,0:T(8,128)(2,1)} %copy-done.19), calls=%async_computation.3 | async-start | bytes 2097152 | tf_op jit(solution)/shard_map/all_to_all | solution.py:387
  87.9 2.2 %copy-start.2 = (bf16[33,256,256]{2,1,0:T(8,128)(2,1)S(1)}, bf16[33,256,256]{2,1,0:T(8,128)(2,1)}, u32[]{:S(2)}) copy-start(bf16[33,256,256]{2,1,0:T(8,128)(2,1)} %constant.78.clone.fine_ref) | copy-start | bytes 12976132
  90.1 2.2 %copy-start.5 = (bf16[33,256,256]{2,1,0:T(8,128)(2,1)S(1)}, bf16[33,256,256]{2,1,0:T(8,128)(2,1)}, u32[]{:S(2)}) copy-start(bf16[33,256,256]{2,1,0:T(8,128)(2,1)} %constant.79.clone.inv_ref) | copy-start | bytes 12976132
  92.3 1.6 copy-start.14
  111.7 1.0 copy-start.18
  116.2 33.0 %all-to-all-start.2 = ((bf16[32,128,128]{2,1,0:T(8,128)(2,1)}), bf16[32,128,128]{2,1,0:T(8,128)(2,1)S(1)}, u32[]{:S(2)}, u32[]{:S(2)}) async-start(bf16[32,128,128]{2,1,0:T(8,128)(2,1)} %copy-done.18), calls=%async_computation.2 | async-start | bytes 2097152 | tf_op jit(solution)/shard_map/all_to_all | solution.py:387
  120.9 28.4 %copy-start.3 = (bf16[128,4096]{1,0:T(8,128)(2,1)S(1)}, bf16[128,4096]{1,0:T(8,128)(2,1)}, u32[]{:S(2)}) copy-start(bf16[128,4096]{1,0:T(8,128)(2,1)} %out_ref.9) | copy-start | bytes 3145732
  120.9 28.4 %copy-start.6 = (bf16[128,4096]{1,0:T(8,128)(2,1)S(1)}, bf16[128,4096]{1,0:T(8,128)(2,1)}, u32[]{:S(2)}) copy-start(bf16[128,4096]{1,0:T(8,128)(2,1)} %cot_ref.7) | copy-start | bytes 3145732
  120.9 1.4 copy-start.9
  122.3 1.2 copy-start.11
  130.2 0.6 copy-start.21
  130.8 0.6 copy-start.23
  132.1 2.0 %collective-permute-start.1 = (f32[6,1024]{1,0:T(8,128)}, f32[6,1024]{1,0:T(8,128)}, u32[]{:S(2)}, u32[]{:S(2)}) collective-permute-start(f32[6,1024]{1,0:T(8,128)} %get-tuple-element.58), channel_id=1, source_target_pairs={{0,1},{1,0},{2,3},{3,2},{4,5},{5,4},{6,7},{7,6},{8,9},{9,8},{10,11... | collective-permute-start | bytes 73736 | tf_op jit(solution)/shard_map/ppermute | solution.py:366
  132.3 4.3 %collective-permute-start.2 = (f32[6,1024]{1,0:T(8,128)}, f32[6,1024]{1,0:T(8,128)}, u32[]{:S(2)}, u32[]{:S(2)}) collective-permute-start(f32[6,1024]{1,0:T(8,128)} %get-tuple-element.57), channel_id=1, source_target_pairs={{0,16},{1,17},{2,18},{3,19},{4,20},{5,21},{6,22},{7,23},{8,24},{9,... | collective-permute-start | bytes 73736 | tf_op jit(solution)/shard_map/ppermute | solution.py:366
  134.0 4.8 %collective-permute-start.3 = (f32[6,1024]{1,0:T(8,128)}, f32[6,1024]{1,0:T(8,128)}, u32[]{:S(2)}, u32[]{:S(2)}) collective-permute-start(f32[6,1024]{1,0:T(8,128)} %get-tuple-element.56), channel_id=1, source_target_pairs={{0,17},{1,16},{2,19},{3,18},{4,21},{5,20},{6,23},{7,22},{8,25},{9,... | collective-permute-start | bytes 73736 | tf_op jit(solution)/shard_map/ppermute | solution.py:366
  149.2 0.8 copy-start.24
  150.1 5.9 %copy-start.27 = (f32[6,1024]{1,0:T(8,128)S(1)}, f32[6,1024]{1,0:T(8,128)}, u32[]{:S(2)}) copy-start(f32[6,1024]{1,0:T(8,128)} %fusion) | copy-start | bytes 73732
  151.6 2.0 %collective-permute-start.4 = (f32[3,1024]{1,0:T(4,128)S(1)}, f32[3,1024]{1,0:T(4,128)S(1)}, u32[]{:S(2)}, u32[]{:S(2)}) collective-permute-start(f32[3,1024]{1,0:T(4,128)S(1)} %get-tuple-element.61), channel_id=1, source_target_pairs={{0,1},{1,0},{2,3},{3,2},{4,5},{5,4},{6,7},{7,6},{8,9},{9,8},{10,11... | collective-permute-start | bytes 36872 | tf_op jit(solution)/shard_map/ppermute | solution.py:366
  151.7 4.1 %collective-permute-start.5 = (f32[3,1024]{1,0:T(4,128)S(1)}, f32[3,1024]{1,0:T(4,128)S(1)}, u32[]{:S(2)}, u32[]{:S(2)}) collective-permute-start(f32[3,1024]{1,0:T(4,128)S(1)} %get-tuple-element.60), channel_id=1, source_target_pairs={{0,16},{1,17},{2,18},{3,19},{4,20},{5,21},{6,22},{7,23},{8,24},{9,... | collective-permute-start | bytes 36872 | tf_op jit(solution)/shard_map/ppermute | solution.py:366
  152.7 3.3 %collective-permute-start.6 = (f32[3,1024]{1,0:T(4,128)S(1)}, f32[3,1024]{1,0:T(4,128)S(1)}, u32[]{:S(2)}, u32[]{:S(2)}) collective-permute-start(f32[3,1024]{1,0:T(4,128)S(1)} %get-tuple-element.59), channel_id=1, source_target_pairs={{0,17},{1,16},{2,19},{3,18},{4,21},{5,20},{6,23},{7,22},{8,25},{9,... | collective-permute-start | bytes 36872 | tf_op jit(solution)/shard_map/ppermute | solution.py:366
  156.8 17.2 %all-to-all-start.4 = ((f32[8,9,8,128]{3,2,1,0:T(8,128)}), f32[8,9,8,128]{3,2,1,0:T(8,128)}, u32[]{:S(2)}, u32[]{:S(2)}) async-start(f32[8,9,8,128]{3,2,1,0:T(8,128)} %broadcast_in_dim.8), calls=%async_computation.4 | async-start | bytes 589824 | tf_op jit(solution)/shard_map/all_to_all | solution.py:378
  160.9 3.1 %collective-permute-start.7 = (bf16[8,4096]{1,0:T(8,128)(2,1)S(1)}, bf16[8,4096]{1,0:T(8,128)(2,1)S(1)}, u32[]{:S(2)}, u32[]{:S(2)}) collective-permute-start(bf16[8,4096]{1,0:T(8,128)(2,1)S(1)} %get-tuple-element.43), channel_id=1, source_target_pairs={{1,0},{2,1},{3,2},{4,3},{5,4},{6,5},{7,6},{8,7},{9,8},{10,9},{11,1... | collective-permute-start | bytes 196616 | tf_op jit(solution)/shard_map/ppermute | solution.py:474
  166.1 12.8 %copy-start.22 = (bf16[8,4096]{1,0:T(8,128)(2,1)S(1)}, bf16[8,4096]{1,0:T(8,128)(2,1)}, u32[]{:S(2)}) copy-start(bf16[8,4096]{1,0:T(8,128)(2,1)} %copy-done.21) | copy-start | bytes 196612
  175.0 5.7 %collective-permute-start.10 = (f32[9,8,128]{2,1,0:T(8,128)S(1)}, f32[9,8,128]{2,1,0:T(8,128)S(1)}, u32[]{:S(2)}, u32[]{:S(2)}) collective-permute-start(f32[9,8,128]{2,1,0:T(8,128)S(1)} %reduce_sum.9), channel_id=1, source_target_pairs={{0,17},{1,16},{2,19},{3,18},{4,21},{5,20},{6,23},{7,22},{8,25},{9,... | collective-permute-start | bytes 110600 | tf_op jit(solution)/shard_map/ppermute | solution.py:366
  176.0 4.7 %collective-permute-start.9 = (f32[9,8,128]{2,1,0:T(8,128)S(1)}, f32[9,8,128]{2,1,0:T(8,128)S(1)}, u32[]{:S(2)}, u32[]{:S(2)}) collective-permute-start(f32[9,8,128]{2,1,0:T(8,128)S(1)} %reduce_sum.9), channel_id=1, source_target_pairs={{0,16},{1,17},{2,18},{3,19},{4,20},{5,21},{6,22},{7,23},{8,24},{9,... | collective-permute-start | bytes 110600 | tf_op jit(solution)/shard_map/ppermute | solution.py:366
  176.8 3.9 %collective-permute-start.8 = (f32[9,8,128]{2,1,0:T(8,128)S(1)}, f32[9,8,128]{2,1,0:T(8,128)S(1)}, u32[]{:S(2)}, u32[]{:S(2)}) collective-permute-start(f32[9,8,128]{2,1,0:T(8,128)S(1)} %reduce_sum.9), channel_id=1, source_target_pairs={{0,1},{1,0},{2,3},{3,2},{4,5},{5,4},{6,7},{7,6},{8,9},{9,8},{10,11... | collective-permute-start | bytes 110600 | tf_op jit(solution)/shard_map/ppermute | solution.py:366

commit v3 on v2

--- a/solution.py
+++ b/solution.py
@@ -13,7 +13,7 @@
 f32 = jnp.float32
 
 TILE = 2048
-GROUP = 8
+GROUP = 32
 PAD = 8
 
 
@@ -24,6 +24,8 @@
         self.parts = -(-2 * self.half // 8) * 8
         self.pitch = rows + PAD
         self.length = 2 * blocks * rows
+        self.halves = blocks // 16
+        self.pack = -(-18 * self.halves // 8) * 8
 
 
 def tables(z):
@@ -118,7 +120,7 @@
         spec_ref[a] = fine_forward(z, fine_ref, parts, a).astype(spec_ref.dtype)
         return carry
 
-    lax.fori_loop(0, z.half, body, 0, unroll=3)
+    lax.fori_loop(0, z.half, body, 0, unroll=11)
 
 
 def times(spec, other, rows, conj):
@@ -140,7 +142,7 @@
         fine_inverse(z, inv_ref, (parts,), a, (times(spec, filter_ref[a].astype(f32), z.rows, True),))
         return carry
 
-    lax.fori_loop(0, z.half, body, 0, unroll=3)
+    lax.fori_loop(0, z.half, body, 0, unroll=11)
     coarse_inverse(z, parts, back_ref, held)
     store_blocks(z, held, out_ref)
 
@@ -161,7 +163,7 @@
         fine_inverse(z, inv_ref, (parts, more), a, (conv, long))
         return carry
 
-    lax.fori_loop(0, z.half, body, 0, unroll=3)
+    lax.fori_loop(0, z.half, body, 0, unroll=11)
     coarse_inverse(z, parts, back_ref, held)
     store_blocks(z, held, out_ref)
     coarse_inverse(z, more, back_ref, held)
@@ -298,13 +300,56 @@
         new_ref[...] = new.astype(bf16)
 
 
-def output_sums_kernel(conv_ref, out_ref, cot_ref, halo_ref, in_head_ref, sums_ref, head_ref):
+def output_sums_kernel(conv_ref, out_ref, cot_ref, halo_ref, in_sums_ref, packet_ref, head_ref):
     before = halo_ref[...].astype(f32)[4:6]
     out_grad = (cot_ref[...].astype(f32) * inward(conv_ref)).astype(bf16).astype(f32)
     rows = out_ref[...].astype(f32)
     lags = (rows, delayed(rows, before, 1), delayed(rows, before, 2))
-    store_sums(sums_ref, lag_sums(out_grad, lags))
-    head_ref[...] = collect([in_head_ref[...].astype(f32)[0:4], out_grad[0:2]], 8, bf16)
+    sums, ins = jnp.concatenate(lag_sums(out_grad, lags), axis=0), in_sums_ref[...]
+    head_ref[...] = collect([out_grad[0:2]], 8, bf16)
+    count, pack, width = packet_ref.shape
+    quarter = sums.shape[1] // 4
+    part = quarter // 4
+    for n in range(4):
+        pieces = [
+            sums[:, q * quarter + n * part + h : q * quarter + n * part + h + width]
+            for q in range(4)
+            for h in range(0, part, width)
+        ]
+        pieces += [ins[:, n * part + h : n * part + h + width] for h in range(0, part, width)]
+        packet = collect(pieces, pack, bf16)
+        for depth in range(count // 4):
+            packet_ref[(n // 2) * (count // 2) + 2 * depth + n % 2] = packet
+
+
+def packet_sums_kernel(packet_ref, total_ref):
+    count, _, width = packet_ref.shape
+    halves = total_ref.shape[0] // 36
+    outs = 12 * halves
+    packets = [packet_ref[d].astype(f32) for d in range(count)]
+    near = [
+        functools.reduce(jnp.add, [packets[(q // 2) * (count // 2) + 2 * depth + q % 2] for depth in range(count // 4)])
+        for q in range(4)
+    ]
+    whole = (near[0] + near[1]) + (near[2] + near[3])
+    pieces = [whole[:outs]] + [part[outs : outs + 6 * halves] for part in near]
+    total_ref[...] = jnp.concatenate(pieces, axis=0)
+
+
+def short_kernel(me_ref, held_ref, short_ref):
+    quarter = short_ref.shape[2] // 4
+    part, width = quarter // 4, held_ref.shape[2]
+    halves = part // width
+    for n in range(4):
+        held = held_ref[me_ref[0] ^ n]
+        for q in range(4):
+            for h in range(halves):
+                start = q * quarter + n * part + h * width
+                out_row = (q * halves + h) * 3
+                in_row = 12 * halves + (q * halves + h) * 6
+                short_ref[0, :, start : start + width] = held[in_row : in_row + 3]
+                short_ref[1, :, start : start + width] = held[in_row + 3 : in_row + 6]
+                short_ref[2, :, start : start + width] = held[out_row : out_row + 3]
 
 
 def mixed_kernel(conv_ref, out_ref, halo_ref, taps_ref, mixed_ref):
@@ -314,7 +359,7 @@
 
 def output_grad_kernel(conv_ref, cot_ref, next_ref, taps_ref, grad_ref):
     out_grad = (cot_ref[...].astype(f32) * inward(conv_ref)).astype(bf16).astype(f32)
-    grad_ref[...] = adjoint(out_grad, next_ref[...].astype(f32)[4:6], taps_ref[2])
+    grad_ref[...] = adjoint(out_grad, next_ref[...].astype(f32)[0:2], taps_ref[2])
 
 
 def position_call(z, kernel, operands, kinds, out_kinds, channels, name, cost_us, tile=TILE, aliases=None, vmem=14):
@@ -327,8 +372,11 @@
             "moved": pl.BlockSpec((tile // z.width, z.rows, z.width), lambda i: (i, 0, 0)),
             "edge": pl.BlockSpec((8, tile), lambda i: (0, i)),
             "six": pl.BlockSpec((tile // quarter, 6, quarter), lambda i: (i, 0, 0)),
-            "three": pl.BlockSpec((tile // quarter, 3, quarter), lambda i: (i, 0, 0)),
+            "near": pl.BlockSpec((6, quarter), lambda i: (0, 0)),
             "taps": pl.BlockSpec((3, 3, tile), lambda i: (0, 0, i)),
+            "left": pl.BlockSpec(memory_space=pl.ANY),
+            "whole": pl.BlockSpec(memory_space=pltpu.VMEM),
+            "packet": pl.BlockSpec((z.blocks, z.pack, z.width), lambda i: (0, 0, 0)),
             "first": pl.BlockSpec((16, tile), lambda i: (0, i)),
             "moved_first": pl.BlockSpec((tile // z.width, 16, z.width), lambda i: (i, 0, 0)),
             "last": pl.BlockSpec((16, tile), lambda i: (z.rows // 16 - 1, i)),
@@ -339,9 +387,9 @@
         "last": jax.ShapeDtypeStruct((z.rows, channels), bf16),
         "moved": jax.ShapeDtypeStruct((channels // z.width, z.rows, z.width), bf16),
         "moved_first": jax.ShapeDtypeStruct((channels // z.width, z.rows, z.width), bf16),
+        "packet": jax.ShapeDtypeStruct((z.blocks, z.pack, z.width), bf16),
         "edge": jax.ShapeDtypeStruct((8, channels), bf16),
         "six": jax.ShapeDtypeStruct((4, 6, quarter), f32),
-        "three": jax.ShapeDtypeStruct((4, 3, quarter), f32),
     }
     return pl.pallas_call(
         kernel,
@@ -356,9 +404,22 @@
     )(*operands)
 
 
-class Sums:
+def small_call(kernel, operands, out, name, scalars=0):
+    spaces = [pltpu.SMEM] * scalars + [pltpu.VMEM] * (len(operands) - scalars)
+    return pl.pallas_call(
+        kernel,
+        out_shape=[out],
+        in_specs=[pl.BlockSpec(memory_space=space) for space in spaces],
+        out_specs=[pl.BlockSpec(memory_space=pltpu.VMEM)],
+        compiler_params=pltpu.CompilerParams(vmem_limit_bytes=8 << 20),
+        cost_estimate=pl.CostEstimate(flops=0, bytes_accessed=3000000, transcendentals=0),
+        name=name,
+    )(*operands)
+
+
+class Near:
     def __init__(self, size):
-        self.size, self.depth, self.offsets = size, size // 4, (1, size // 2, size // 2 + 1)
+        self.size, self.offsets = size, (1, size // 2, size // 2 + 1)
         me = lax.axis_index("seq")
         self.quarter = me % 2 + 2 * (me // (size // 2))
 
@@ -368,19 +429,12 @@
     def piece(self, value, which):
         return lax.dynamic_index_in_dim(value, which, 0, keepdims=False)
 
-    def near(self, value):
+    def scatter(self, value):
         arrived = [self.swap(self.piece(value, self.quarter ^ (k + 1)), bits) for k, bits in enumerate(self.offsets)]
         return (self.piece(value, self.quarter) + arrived[0]) + (arrived[1] + arrived[2])
 
-    def far(self, value):
-        lines = [[self.size // 2 * x + 2 * z + core for z in range(self.depth)] for x in range(2) for core in range(2)]
-        copies = jnp.broadcast_to(value[None], (self.depth, *value.shape))
-        parts = lax.all_to_all(copies, "seq", split_axis=0, concat_axis=0, tiled=True, axis_index_groups=lines)
-        return jnp.sum(parts, axis=0)
-
     def gather(self, value):
-        held = jnp.stack([value] + [self.swap(value, bits) for bits in self.offsets])
-        return jnp.stack([self.piece(held, self.quarter ^ j) for j in range(4)], axis=1)
+        return jnp.stack([value] + [self.swap(value, bits) for bits in self.offsets])
 
 
 def exchange(value):
@@ -414,7 +468,7 @@
     (outer,) = position(
         outer_head_kernel,
         (outer, gate_out, cotangent, halo, short_filters),
-        ("moved_first", "first", "first", "edge", "taps"),
+        ("left", "first", "first", "whole", "taps"),
         ("moved_first",),
         "outer_head",
         1,
@@ -458,20 +512,20 @@
         "input_grads",
         6,
     )
-    sums = Sums(size)
-    conv_rows, grad_gate, grad_value, in_sums = lax.optimization_barrier(
-        (conv_rows, grad_gate, grad_value, sums.near(in_sums))
-    )
-    out_sums, out_head = position(
+    near = Near(size)
+    in_sums = near.scatter(in_sums)
+    in_after = lax.ppermute(in_head, "seq", backward)
+    packets, out_head = position(
         output_sums_kernel,
-        (conv_rows, gate_out, cotangent, halo, in_head),
-        ("moved", "rows", "rows", "edge", "edge"),
-        ("three", "edge"),
+        (conv_rows, gate_out, cotangent, halo, in_sums),
+        ("moved", "rows", "rows", "edge", "near"),
+        ("packet", "edge"),
         "output_sums",
         3,
-    )
-    out_sums, out_head = lax.optimization_barrier((sums.near(out_sums), out_head))
+        tile=channels,
+    )
     after = lax.ppermute(out_head, "seq", backward)
+    packets = exchange(packets)
     (mixed,) = position(
         mixed_kernel,
         (conv_rows, gate_out, halo, short_filters),
@@ -480,7 +534,6 @@
         "mixed",
         3,
     )
-    both = jnp.concatenate([in_sums, out_sums], axis=0).reshape(9, -1, z.width)
     (grad_out,) = position(
         output_grad_kernel,
         (conv_rows, cotangent, after, short_filters),
@@ -489,10 +542,9 @@
         "output_grad",
         3,
     )
-    both, grad_out = lax.optimization_barrier((sums.far(both), grad_out))
     grad_gate, grad_value = position(
         finish_kernel,
-        (grad_gate, grad_value, after, in_tail, short_filters),
+        (grad_gate, grad_value, in_after, in_tail, short_filters),
         ("last", "last", "edge", "edge", "taps"),
         ("last", "last"),
         "finish_input_grads",
@@ -500,7 +552,17 @@
         tile=channels,
         aliases={0: 0, 1: 1},
     )
-    grad_short = sums.gather(both).reshape(3, 3, channels)
+    packets, mixed, grad_out, grad_gate, grad_value = lax.optimization_barrier(
+        (packets, mixed, grad_out, grad_gate, grad_value)
+    )
+    (total,) = small_call(
+        packet_sums_kernel, (packets,), jax.ShapeDtypeStruct((36 * z.halves, z.width), f32), "packet_sums"
+    )
+    held = near.gather(total)
+    quarter = near.quarter.astype(jnp.int32).reshape(1)
+    (grad_short,) = small_call(
+        short_kernel, (quarter, held), jax.ShapeDtypeStruct((3, 3, channels), f32), "grad_short", scalars=1
+    )
     return (mixed, grad_gate, grad_value, grad_out, grad_long, grad_short)
 
 

time: 184 us -> 179 us (0.973)
  Pallas kernels: 59.2 us -> 45.2 us
  waiting for transfers between devices: 53.7 us -> 66.9 us
    all_to_all x4 -> x5, waiting for transfers between devices: 36.7 us -> 60.4 us  [exchange(): return lax.all_to_all(value, 'seq', split_axis=0, concat_axis=0, tiled=True)]
    pallas_call x3, Pallas kernels: 36.7 us -> 21.1 us  [channel_call(): pl.pallas_call(kernel, out_shape=outs, in_specs=[whole] * len(operands),...]
    all_to_all x1 -> x0, waiting for transfers between devices: 7.92 us -> none  [far(): lax.all_to_all(copies, 'seq', split_axis=0, concat_axis=0, tiled=True, ax...]
    all_to_all x1 -> x0, starting transfers between devices: 4.06 us -> none  [far(): lax.all_to_all(copies, 'seq', split_axis=0, concat_axis=0, tiled=True, ax...]
    all_to_all x4 -> x5, starting transfers between devices: 26.1 us -> 30.2 us  [exchange(): return lax.all_to_all(value, 'seq', split_axis=0, concat_axis=0, tiled=True)]
    ppermute x9 -> x6, starting transfers between devices: 5.86 us -> 3.92 us  [swap(): return lax.ppermute(value, 'seq', [(i, i ^ bits) for i in range(self.size)])]
    ppermute x1, waiting for transfers between devices: 1.85 us -> 0.01 us  [local(): after = lax.ppermute(out_head, 'seq', backward)]
    ppermute x9 -> x6, waiting for transfers between devices: 7.21 us -> 6.44 us  [swap(): return lax.ppermute(value, 'seq', [(i, i ^ bits) for i in range(self.size)])]
  transfers between devices with their start and end apart: 16 -> 14, of which waited for: 10 -> 9; matrix products, arithmetic and copies ran while one was open for 1% -> 1% of each run, Pallas kernels for 30% -> 22%
where the time goes in v3:
time: 179 us; the launch traced here: 177 us
  waiting for transfers between devices  66.9 us (37%)
  Pallas kernels  45.2 us (25%)
  starting transfers between devices  38.4 us (21%)
  local copies, waits for them, and re-layouts  25.1 us (14%)
    all_to_all x5, waiting for transfers between devices, exchange(): return lax.all_to_all(value, 'seq', split_axis=0, concat_axis=0, tiled=True)  60.4 us
    all_to_all x5, starting transfers between devices, exchange(): return lax.all_to_all(value, 'seq', split_axis=0, concat_axis=0, tiled=True)  30.2 us
    unnamed x56, local copies, waits for them, and re-layouts  24.5 us
    pallas_call x9, Pallas kernels, position_call(): pl.pallas_call(kernel, grid=(channels // tile,), out_shape=[shapes[k] for...  22.3 us
    pallas_call x3, Pallas kernels, channel_call(): pl.pallas_call(kernel, out_shape=outs, in_specs=[whole] * len(operands),...  21.1 us
    ppermute x6, waiting for transfers between devices, swap(): return lax.ppermute(value, 'seq', [(i, i ^ bits) for i in range(self.size)])  6.44 us
    ppermute x6, starting transfers between devices, swap(): return lax.ppermute(value, 'seq', [(i, i ^ bits) for i in range(self.size)])  3.92 us
  transfers between devices with their start and end apart: 14, of which 9 were waited for; matrix products, arithmetic and copies ran while one was open for 1% of the time, Pallas kernels for 22%

profile of v3, /device:TPU:8, one launch (start us, length us, event | category | flops | bytes accessed | tf_op | source)
XLA Modules:
  0.0 177.4 jit_solution(15096244462693917864)
XLA Ops:
  0.6 1.7 edges.1
  2.3 1.7 collective-permute-start
  4.1 3.0 %outer.1.old_ref = bf16[32,128,128]{2,1,0:T(8,128)(2,1)} custom-call(bf16[128,4096]{1,0:T(8,128)(2,1)} %out_ref.9, bf16[128,4096]{1,0:T(8,128)(2,1)} %cot_ref.7, f32[3,3,4096]{2,1,0:T(4,128)} %taps_ref.13), custom_call_target="tpu_custom_call" | custom-call | bytes 12000000 | tf_op jit(solution)/shard_map/outer/pallas_call | solution.py:394
  7.7 1.9 %outer_head.1 = bf16[32,128,128]{2,1,0:T(8,128)(2,1)} custom-call(bf16[32,128,128]{2,1,0:T(8,128)(2,1)} %outer.1.old_ref, bf16[128,4096]{1,0:T(8,128)(2,1)} %out_ref.9, bf16[128,4096]{1,0:T(8,128)(2,1)} %cot_ref.7, bf16[8,4096]{1,0:T(8,128)(2,1)} %copy-done.16, f32[3,3,4096]{2,1,0:T(4,128)} %taps_ref.13), custom_call_target="tpu_custom_call", output_to_operand_aliasing={{}: (0, {})} | custom-call | bytes 3000000 | tf_op jit(solution)/shard_map/outer_head/pallas_call | solution.py:394
  9.6 12.1 %all-to-all-start.1 = ((bf16[32,128,128]{2,1,0:T(8,128)(2,1)}), bf16[32,128,128]{2,1,0:T(8,128)(2,1)}, u32[]{:S(2)}, u32[]{:S(2)}) async-start(bf16[32,128,128]{2,1,0:T(8,128)(2,1)} %outer_head.1), calls=%async_computation.1 | async-start | bytes 2097152 | tf_op jit(solution)/shard_map/all_to_all | solution.py:441
  21.8 2.2 %copy-done = bf16[33,256,256]{2,1,0:T(8,128)(2,1)S(1)} copy-done((bf16[33,256,256]{2,1,0:T(8,128)(2,1)S(1)}, bf16[33,256,256]{2,1,0:T(8,128)(2,1)}, u32[]{:S(2)}) %copy-start) | copy-done | bytes 4325400
  24.0 1.6 copy-done.15
  25.6 3.3 %filter_spec.1.filter_ref = bf16[33,256,128]{2,1,0:T(8,128)(2,1)S(1)} custom-call(f32[4096,128]{1,0:T(8,128)S(1)} %copy-done.15, bf16[72,64]{1,0:T(8,128)(2,1)S(1)} %copy-done.24, bf16[33,256,256]{2,1,0:T(8,128)(2,1)S(1)} %copy-done), custom_call_target="tpu_custom_call" | custom-call | bytes 24000000 | tf_op jit(solution)/shard_map/filter_spec/pallas_call | solution.py:180
  28.9 1.9 %signal.1 = bf16[32,128,128]{2,1,0:T(8,128)(2,1)S(1)} custom-call(bf16[128,4096]{1,0:T(8,128)(2,1)S(1)} %copy-done.8, bf16[128,4096]{1,0:T(8,128)(2,1)S(1)} %copy-done.10, bf16[8,4096]{1,0:T(8,128)(2,1)S(1)} %copy-done.17, f32[3,3,4096]{2,1,0:T(4,128)S(1)} %copy-done.7), custom_call_target="tpu_custom_call" | custom-call | bytes 12000000 | tf_op jit(solution)/shard_map/signal/pallas_call | solution.py:394
  30.9 1.0 copy-done.12
  31.9 18.3 %all-to-all-done.1.data_ref = bf16[32,128,128]{2,1,0:T(8,128)(2,1)} async-done(((bf16[32,128,128]{2,1,0:T(8,128)(2,1)}), bf16[32,128,128]{2,1,0:T(8,128)(2,1)}, u32[]{:S(2)}, u32[]{:S(2)}) %all-to-all-start.1) | async-done | bytes 1048608 | tf_op jit(solution)/shard_map/all_to_all | solution.py:441
  50.1 4.7 %all-to-all-start = ((bf16[32,128,128]{2,1,0:T(8,128)(2,1)}), bf16[32,128,128]{2,1,0:T(8,128)(2,1)}, u32[]{:S(2)}, u32[]{:S(2)}) async-start(bf16[32,128,128]{2,1,0:T(8,128)(2,1)} %copy-done.12), calls=%async_computation | async-start | bytes 2097152 | tf_op jit(solution)/shard_map/all_to_all | solution.py:441
  54.8 2.2 %copy-done.1 = bf16[33,256,256]{2,1,0:T(8,128)(2,1)S(1)} copy-done((bf16[33,256,256]{2,1,0:T(8,128)(2,1)S(1)}, bf16[33,256,256]{2,1,0:T(8,128)(2,1)}, u32[]{:S(2)}) %copy-start.1) | copy-done | bytes 4325400
  57.1 2.2 %copy-done.4 = bf16[33,256,256]{2,1,0:T(8,128)(2,1)S(1)} copy-done((bf16[33,256,256]{2,1,0:T(8,128)(2,1)S(1)}, bf16[33,256,256]{2,1,0:T(8,128)(2,1)}, u32[]{:S(2)}) %copy-start.4) | copy-done | bytes 4325400
  59.3 7.4 %signal_grad.1 = (bf16[33,256,128]{2,1,0:T(8,128)(2,1)S(1)}, bf16[32,128,128]{2,1,0:T(8,128)(2,1)S(1)}) custom-call(bf16[32,128,128]{2,1,0:T(8,128)(2,1)} %all-to-all-done.1.data_ref, bf16[33,256,128]{2,1,0:T(8,128)(2,1)S(1)} %filter_spec.1.filter_ref, bf16[72,32]{1,0:T(8,128)(2,1)S(1)} %copy-done.22, bf16[33,256,256]{2,1,0:T(8,128)(2,1)S(1)} %copy-done.1, ...), custom_call_target="tpu_custom_call" | custom-call | bytes 48000000 | tf_op jit(solution)/shard_map/signal_grad/pallas_call | solution.py:180
  66.7 1.4 copy-done.13
  68.0 1.0 copy-done.19
  69.0 14.1 %all-to-all-done.data_ref = bf16[32,128,128]{2,1,0:T(8,128)(2,1)} async-done(((bf16[32,128,128]{2,1,0:T(8,128)(2,1)}), bf16[32,128,128]{2,1,0:T(8,128)(2,1)}, u32[]{:S(2)}, u32[]{:S(2)}) %all-to-all-start) | async-done | bytes 1048608 | tf_op jit(solution)/shard_map/all_to_all | solution.py:441
  83.1 4.7 %all-to-all-start.3 = ((bf16[32,128,128]{2,1,0:T(8,128)(2,1)}), bf16[32,128,128]{2,1,0:T(8,128)(2,1)}, u32[]{:S(2)}, u32[]{:S(2)}) async-start(bf16[32,128,128]{2,1,0:T(8,128)(2,1)} %copy-done.19), calls=%async_computation.3 | async-start | bytes 2097152 | tf_op jit(solution)/shard_map/all_to_all | solution.py:441
  87.8 2.2 %copy-done.2 = bf16[33,256,256]{2,1,0:T(8,128)(2,1)S(1)} copy-done((bf16[33,256,256]{2,1,0:T(8,128)(2,1)S(1)}, bf16[33,256,256]{2,1,0:T(8,128)(2,1)}, u32[]{:S(2)}) %copy-start.2) | copy-done | bytes 4325400
  90.1 2.2 %copy-done.5 = bf16[33,256,256]{2,1,0:T(8,128)(2,1)S(1)} copy-done((bf16[33,256,256]{2,1,0:T(8,128)(2,1)S(1)}, bf16[33,256,256]{2,1,0:T(8,128)(2,1)}, u32[]{:S(2)}) %copy-start.5) | copy-done | bytes 4325400
  92.3 1.6 copy-done.14
  93.9 10.5 %conv_out.1 = (bf16[32,128,128]{2,1,0:T(8,128)(2,1)S(1)}, f32[4096,128]{1,0:T(8,128)}) custom-call(bf16[32,128,128]{2,1,0:T(8,128)(2,1)} %all-to-all-done.data_ref, bf16[33,256,128]{2,1,0:T(8,128)(2,1)S(1)} %filter_spec.1.filter_ref, bf16[33,256,128]{2,1,0:T(8,128)(2,1)S(1)} %copy-done.14, bf16[72,32]{1,0:T(8,128)(2,1)S(1)} %copy-done.22, ...), custom_call_target="tpu_custom_call" | custom-call | bytes 66000000 | tf_op jit(solution)/shard_map/conv_out/pallas_call | solution.py:180
  104.4 1.0 copy-done.18
  105.4 10.8 %all-to-all-done.3.sig_ref = bf16[32,128,128]{2,1,0:T(8,128)(2,1)} async-done(((bf16[32,128,128]{2,1,0:T(8,128)(2,1)}), bf16[32,128,128]{2,1,0:T(8,128)(2,1)}, u32[]{:S(2)}, u32[]{:S(2)}) %all-to-all-start.3) | async-done | bytes 1048608 | tf_op jit(solution)/shard_map/all_to_all | solution.py:441
  116.2 4.1 %all-to-all-start.2 = ((bf16[32,128,128]{2,1,0:T(8,128)(2,1)}), bf16[32,128,128]{2,1,0:T(8,128)(2,1)S(1)}, u32[]{:S(2)}, u32[]{:S(2)}) async-start(bf16[32,128,128]{2,1,0:T(8,128)(2,1)} %copy-done.18), calls=%async_computation.2 | async-start | bytes 2097152 | tf_op jit(solution)/shard_map/all_to_all | solution.py:441
  120.3 1.4 copy-done.9
  121.7 1.2 copy-done.11
  122.9 6.7 %input_grads.1 = (f32[4,6,1024]{2,1,0:T(8,128)S(1)}, bf16[8,4096]{1,0:T(8,128)(2,1)S(1)}, bf16[8,4096]{1,0:T(8,128)(2,1)S(1)}, bf16[128,4096]{1,0:T(8,128)(2,1)}, bf16[128,4096]{1,0:T(8,128)(2,1)}) custom-call(bf16[32,128,128]{2,1,0:T(8,128)(2,1)} %all-to-all-done.3.sig_ref, bf16[128,4096]{1,0:T(8,128)(2,1)S(1)} %copy-done.9, ...), custom_call_target="tpu_custom_call" | custom-call | bytes 18000000 | tf_op jit(solution)/shard_map/input_grads/pallas_call | solution.py:394
  131.1 1.7 collective-permute-start.2
  132.8 2.6 %collective-permute-done.2 = f32[6,1024]{1,0:T(8,128)S(1)} collective-permute-done((f32[6,1024]{1,0:T(8,128)}, f32[6,1024]{1,0:T(8,128)S(1)}, u32[]{:S(2)}, u32[]{:S(2)}) %collective-permute-start.2) | collective-permute-done | bytes 24608 | tf_op jit(solution)/shard_map/ppermute | solution.py:427
  136.0 0.7 collective-permute-done.3
  136.7 0.8 fusion.in_sums_ref
  137.5 11.1 %all-to-all-done.2.conv_ref = bf16[32,128,128]{2,1,0:T(8,128)(2,1)S(1)} async-done(((bf16[32,128,128]{2,1,0:T(8,128)(2,1)}), bf16[32,128,128]{2,1,0:T(8,128)(2,1)S(1)}, u32[]{:S(2)}, u32[]{:S(2)}) %all-to-all-start.2) | async-done | bytes 1048608 | tf_op jit(solution)/shard_map/all_to_all | solution.py:441
  148.6 1.3 output_sums.1
  150.0 0.7 copy-done.20
  151.4 4.6 %all-to-all-start.4 = ((bf16[32,40,128]{2,1,0:T(8,128)(2,1)}), bf16[32,40,128]{2,1,0:T(8,128)(2,1)}, u32[]{:S(2)}, u32[]{:S(2)}) async-start(bf16[32,40,128]{2,1,0:T(8,128)(2,1)} %copy-done.20), calls=%async_computation.4 | async-start | bytes 655360 | tf_op jit(solution)/shard_map/all_to_all | solution.py:441
  155.9 1.3 collective-permute-start.5
  157.2 1.3 collective-permute-start.4
  158.5 2.0 %mixed.1 = bf16[128,4096]{1,0:T(8,128)(2,1)} custom-call(bf16[32,128,128]{2,1,0:T(8,128)(2,1)S(1)} %all-to-all-done.2.conv_ref, bf16[128,4096]{1,0:T(8,128)(2,1)S(1)} %copy-done.3, bf16[8,4096]{1,0:T(8,128)(2,1)S(1)} %copy-done.17, f32[3,3,4096]{2,1,0:T(4,128)S(1)} %copy-done.7), custom_call_target="tpu_custom_call" | custom-call | bytes 9000000 | tf_op jit(solution)/shard_map/mixed/pallas_call | solution.py:394
  160.5 1.8 finish_input_grads.1
  162.3 2.1 %output_grad.1 = bf16[128,4096]{1,0:T(8,128)(2,1)} custom-call(bf16[32,128,128]{2,1,0:T(8,128)(2,1)S(1)} %all-to-all-done.2.conv_ref, bf16[128,4096]{1,0:T(8,128)(2,1)S(1)} %copy-done.6, bf16[8,4096]{1,0:T(8,128)(2,1)S(1)} %collective-permute-done.4.next_ref, f32[3,3,4096]{2,1,0:T(4,128)S(1)} %copy-done.7), custom_call_target="tpu_custom_call" | custom-call | bytes 9000000 | tf_op jit(solution)/shard_map/output_grad/pallas_call | solution.py:394
  164.4 6.1 %all-to-all-done.4.packet_ref = bf16[32,40,128]{2,1,0:T(8,128)(2,1)} async-done(((bf16[32,40,128]{2,1,0:T(8,128)(2,1)}), bf16[32,40,128]{2,1,0:T(8,128)(2,1)}, u32[]{:S(2)}, u32[]{:S(2)}) %all-to-all-start.4) | async-done | bytes 327712 | tf_op jit(solution)/shard_map/all_to_all | solution.py:441
  170.5 1.0 packet_sums.1
  171.5 1.2 collective-permute-start.8
  173.4 1.8 %collective-permute-done.8 = f32[72,128]{1,0:T(8,128)S(1)} collective-permute-done((f32[72,128]{1,0:T(8,128)S(1)}, f32[72,128]{1,0:T(8,128)S(1)}, u32[]{:S(2)}, u32[]{:S(2)}) %collective-permute-start.8) | collective-permute-done | bytes 36896 | tf_op jit(solution)/shard_map/ppermute | solution.py:427
  175.3 1.4 collective-permute-done.7
  176.7 0.7 grad_short.1
  (53 shorter events, 4.3 us)
Async XLA Ops:
  2.3 4.8 %collective-permute-start = (bf16[8,4096]{1,0:T(8,128)(2,1)}, bf16[8,4096]{1,0:T(8,128)(2,1)S(1)}, u32[]{:S(2)}, u32[]{:S(2)}) collective-permute-start(bf16[8,4096]{1,0:T(8,128)(2,1)} %edges.1), channel_id=1, source_target_pairs={{0,1},{1,2},{2,3},{3,4},{4,5},{5,6},{6,7},{7,8},{8,9},{9,10},{10,1... | collective-permute-start | bytes 196616 | tf_op jit(solution)/shard_map/ppermute | solution.py:457
  7.1 14.7 %copy-start.24 = (bf16[72,64]{1,0:T(8,128)(2,1)S(1)}, bf16[72,64]{1,0:T(8,128)(2,1)}, u32[]{:S(2)}) copy-start(bf16[72,64]{1,0:T(8,128)(2,1)} %constant.55.clone.twice_ref) | copy-start | bytes 27652
  7.1 0.6 copy-start.16
  9.6 40.5 %all-to-all-start.1 = ((bf16[32,128,128]{2,1,0:T(8,128)(2,1)}), bf16[32,128,128]{2,1,0:T(8,128)(2,1)}, u32[]{:S(2)}, u32[]{:S(2)}) async-start(bf16[32,128,128]{2,1,0:T(8,128)(2,1)} %outer_head.1), calls=%async_computation.1 | async-start | bytes 2097152 | tf_op jit(solution)/shard_map/all_to_all | solution.py:441
  21.8 2.2 %copy-start = (bf16[33,256,256]{2,1,0:T(8,128)(2,1)S(1)}, bf16[33,256,256]{2,1,0:T(8,128)(2,1)}, u32[]{:S(2)}) copy-start(bf16[33,256,256]{2,1,0:T(8,128)(2,1)} %constant.56.clone.fine_ref) | copy-start | bytes 12976132
  24.0 1.6 copy-start.15
  25.6 3.3 %copy-start.7 = (f32[3,3,4096]{2,1,0:T(4,128)S(1)}, f32[3,3,4096]{2,1,0:T(4,128)}, u32[]{:S(2)}) copy-start(f32[3,3,4096]{2,1,0:T(4,128)} %taps_ref.13) | copy-start | bytes 442372
  25.6 3.3 %copy-start.8 = (bf16[128,4096]{1,0:T(8,128)(2,1)S(1)}, bf16[128,4096]{1,0:T(8,128)(2,1)}, u32[]{:S(2)}) copy-start(bf16[128,4096]{1,0:T(8,128)(2,1)} %gate_ref.5) | copy-start | bytes 3145732
  25.6 3.3 %copy-start.10 = (bf16[128,4096]{1,0:T(8,128)(2,1)S(1)}, bf16[128,4096]{1,0:T(8,128)(2,1)}, u32[]{:S(2)}) copy-start(bf16[128,4096]{1,0:T(8,128)(2,1)} %value_ref.5) | copy-start | bytes 3145732
  25.6 3.3 %copy-start.17 = (bf16[8,4096]{1,0:T(8,128)(2,1)S(1)}, bf16[8,4096]{1,0:T(8,128)(2,1)}, u32[]{:S(2)}) copy-start(bf16[8,4096]{1,0:T(8,128)(2,1)} %copy-done.16) | copy-start | bytes 196612
  28.9 25.9 %copy-start.22 = (bf16[72,32]{1,0:T(8,128)(2,1)S(1)}, bf16[72,32]{1,0:T(8,128)(2,1)}, u32[]{:S(2)}) copy-start(bf16[72,32]{1,0:T(8,128)(2,1)} %constant.54.clone.coarse_ref) | copy-start | bytes 13828
  28.9 25.9 %copy-start.23 = (bf16[32,72]{1,0:T(8,128)(2,1)S(1)}, bf16[32,72]{1,0:T(8,128)(2,1)}, u32[]{:S(2)}) copy-start(bf16[32,72]{1,0:T(8,128)(2,1)} %constant.58.clone.back_ref) | copy-start | bytes 13828
  30.9 1.0 copy-start.12
  50.1 33.0 %all-to-all-start = ((bf16[32,128,128]{2,1,0:T(8,128)(2,1)}), bf16[32,128,128]{2,1,0:T(8,128)(2,1)}, u32[]{:S(2)}, u32[]{:S(2)}) async-start(bf16[32,128,128]{2,1,0:T(8,128)(2,1)} %copy-done.12), calls=%async_computation | async-start | bytes 2097152 | tf_op jit(solution)/shard_map/all_to_all | solution.py:441
  54.8 2.2 %copy-start.1 = (bf16[33,256,256]{2,1,0:T(8,128)(2,1)S(1)}, bf16[33,256,256]{2,1,0:T(8,128)(2,1)}, u32[]{:S(2)}) copy-start(bf16[33,256,256]{2,1,0:T(8,128)(2,1)} %constant.56.clone.fine_ref) | copy-start | bytes 12976132
  57.1 2.2 %copy-start.4 = (bf16[33,256,256]{2,1,0:T(8,128)(2,1)S(1)}, bf16[33,256,256]{2,1,0:T(8,128)(2,1)}, u32[]{:S(2)}) copy-start(bf16[33,256,256]{2,1,0:T(8,128)(2,1)} %constant.57.clone.inv_ref) | copy-start | bytes 12976132
  66.7 1.4 copy-start.13
  68.0 1.0 copy-start.19
  83.1 33.0 %all-to-all-start.3 = ((bf16[32,128,128]{2,1,0:T(8,128)(2,1)}), bf16[32,128,128]{2,1,0:T(8,128)(2,1)}, u32[]{:S(2)}, u32[]{:S(2)}) async-start(bf16[32,128,128]{2,1,0:T(8,128)(2,1)} %copy-done.19), calls=%async_computation.3 | async-start | bytes 2097152 | tf_op jit(solution)/shard_map/all_to_all | solution.py:441
  87.8 2.2 %copy-start.2 = (bf16[33,256,256]{2,1,0:T(8,128)(2,1)S(1)}, bf16[33,256,256]{2,1,0:T(8,128)(2,1)}, u32[]{:S(2)}) copy-start(bf16[33,256,256]{2,1,0:T(8,128)(2,1)} %constant.56.clone.fine_ref) | copy-start | bytes 12976132
  90.1 2.2 %copy-start.5 = (bf16[33,256,256]{2,1,0:T(8,128)(2,1)S(1)}, bf16[33,256,256]{2,1,0:T(8,128)(2,1)}, u32[]{:S(2)}) copy-start(bf16[33,256,256]{2,1,0:T(8,128)(2,1)} %constant.57.clone.inv_ref) | copy-start | bytes 12976132
  92.3 1.6 copy-start.14
  104.4 1.0 copy-start.18
  116.2 32.5 %all-to-all-start.2 = ((bf16[32,128,128]{2,1,0:T(8,128)(2,1)}), bf16[32,128,128]{2,1,0:T(8,128)(2,1)S(1)}, u32[]{:S(2)}, u32[]{:S(2)}) async-start(bf16[32,128,128]{2,1,0:T(8,128)(2,1)} %copy-done.18), calls=%async_computation.2 | async-start | bytes 2097152 | tf_op jit(solution)/shard_map/all_to_all | solution.py:441
  120.3 28.4 %copy-start.3 = (bf16[128,4096]{1,0:T(8,128)(2,1)S(1)}, bf16[128,4096]{1,0:T(8,128)(2,1)}, u32[]{:S(2)}) copy-start(bf16[128,4096]{1,0:T(8,128)(2,1)} %out_ref.9) | copy-start | bytes 3145732
  120.3 28.4 %copy-start.6 = (bf16[128,4096]{1,0:T(8,128)(2,1)S(1)}, bf16[128,4096]{1,0:T(8,128)(2,1)}, u32[]{:S(2)}) copy-start(bf16[128,4096]{1,0:T(8,128)(2,1)} %cot_ref.7) | copy-start | bytes 3145732
  120.3 1.4 copy-start.9
  121.7 1.2 copy-start.11
  129.6 0.7 copy-start.21
  129.6 1.3 copy-start.25
  130.9 2.0 %collective-permute-start.1 = (f32[6,1024]{1,0:T(8,128)}, f32[6,1024]{1,0:T(8,128)S(1)}, u32[]{:S(2)}, u32[]{:S(2)}) collective-permute-start(f32[6,1024]{1,0:T(8,128)} %get-tuple-element.48), channel_id=1, source_target_pairs={{0,1},{1,0},{2,3},{3,2},{4,5},{5,4},{6,7},{7,6},{8,9},{9,8},{10,11... | collective-permute-start | bytes 73736 | tf_op jit(solution)/shard_map/ppermute | solution.py:427
  131.1 4.3 %collective-permute-start.2 = (f32[6,1024]{1,0:T(8,128)}, f32[6,1024]{1,0:T(8,128)S(1)}, u32[]{:S(2)}, u32[]{:S(2)}) collective-permute-start(f32[6,1024]{1,0:T(8,128)} %get-tuple-element.47), channel_id=1, source_target_pairs={{0,16},{1,17},{2,18},{3,19},{4,20},{5,21},{6,22},{7,23},{8,24},{9,... | collective-permute-start | bytes 73736 | tf_op jit(solution)/shard_map/ppermute | solution.py:427
  132.8 3.9 %collective-permute-start.3 = (f32[6,1024]{1,0:T(8,128)}, f32[6,1024]{1,0:T(8,128)}, u32[]{:S(2)}, u32[]{:S(2)}) collective-permute-start(f32[6,1024]{1,0:T(8,128)} %get-tuple-element.46), channel_id=1, source_target_pairs={{0,17},{1,16},{2,19},{3,18},{4,21},{5,20},{6,23},{7,22},{8,25},{9,... | collective-permute-start | bytes 73736 | tf_op jit(solution)/shard_map/ppermute | solution.py:427
  135.4 0.6 copy-start.27
  150.0 0.8 copy-start.20
  150.7 0.6 copy-start.26
  151.4 19.1 %all-to-all-start.4 = ((bf16[32,40,128]{2,1,0:T(8,128)(2,1)}), bf16[32,40,128]{2,1,0:T(8,128)(2,1)}, u32[]{:S(2)}, u32[]{:S(2)}) async-start(bf16[32,40,128]{2,1,0:T(8,128)(2,1)} %copy-done.20), calls=%async_computation.4 | async-start | bytes 655360 | tf_op jit(solution)/shard_map/all_to_all | solution.py:441
  155.9 4.6 %collective-permute-start.5 = (bf16[8,4096]{1,0:T(8,128)(2,1)}, bf16[8,4096]{1,0:T(8,128)(2,1)S(1)}, u32[]{:S(2)}, u32[]{:S(2)}) collective-permute-start(bf16[8,4096]{1,0:T(8,128)(2,1)} %copy-done.25), channel_id=1, source_target_pairs={{1,0},{2,1},{3,2},{4,3},{5,4},{6,5},{7,6},{8,7},{9,8},{10,9},{11,1... | collective-permute-start | bytes 196616 | tf_op jit(solution)/shard_map/ppermute | solution.py:517
  157.2 5.1 %collective-permute-start.4 = (bf16[8,4096]{1,0:T(8,128)(2,1)}, bf16[8,4096]{1,0:T(8,128)(2,1)S(1)}, u32[]{:S(2)}, u32[]{:S(2)}) collective-permute-start(bf16[8,4096]{1,0:T(8,128)(2,1)} %copy-done.26), channel_id=1, source_target_pairs={{1,0},{2,1},{3,2},{4,3},{5,4},{6,5},{7,6},{8,7},{9,8},{10,9},{11,1... | collective-permute-start | bytes 196616 | tf_op jit(solution)/shard_map/ppermute | solution.py:527
  171.5 3.8 %collective-permute-start.8 = (f32[72,128]{1,0:T(8,128)S(1)}, f32[72,128]{1,0:T(8,128)S(1)}, u32[]{:S(2)}, u32[]{:S(2)}) collective-permute-start(f32[72,128]{1,0:T(8,128)S(1)} %packet_sums.1), channel_id=1, source_target_pairs={{0,17},{1,16},{2,19},{3,18},{4,21},{5,20},{6,23},{7,22},{8,25},{9,... | collective-permute-start | bytes 110600 | tf_op jit(solution)/shard_map/ppermute | solution.py:427
  172.7 4.0 %collective-permute-start.7 = (f32[72,128]{1,0:T(8,128)S(1)}, f32[72,128]{1,0:T(8,128)S(1)}, u32[]{:S(2)}, u32[]{:S(2)}) collective-permute-start(f32[72,128]{1,0:T(8,128)S(1)} %packet_sums.1), channel_id=1, source_target_pairs={{0,16},{1,17},{2,18},{3,19},{4,20},{5,21},{6,22},{7,23},{8,24},{9,... | collective-permute-start | bytes 110600 | tf_op jit(solution)/shard_map/ppermute | solution.py:427
  173.1 3.5 %collective-permute-start.6 = (f32[72,128]{1,0:T(8,128)S(1)}, f32[72,128]{1,0:T(8,128)S(1)}, u32[]{:S(2)}, u32[]{:S(2)}) collective-permute-start(f32[72,128]{1,0:T(8,128)S(1)} %packet_sums.1), channel_id=1, source_target_pairs={{0,1},{1,0},{2,3},{3,2},{4,5},{5,4},{6,7},{7,6},{8,9},{9,8},{10,11... | collective-permute-start | bytes 110600 | tf_op jit(solution)/shard_map/ppermute | solution.py:427

commit v4 on v3

--- a/solution.py
+++ b/solution.py
@@ -130,10 +130,38 @@
     return s_re * h_re - s_im * h_im, s_re * h_im + s_im * h_re
 
 
+def load_longer(z, data_ref, held):
+    def body(i, carry):
+        held[pl.ds(pl.multiple_of(i * z.pitch, 8), z.pitch), :] = data_ref[i].astype(f32)
+        return carry
+
+    lax.fori_loop(0, z.blocks, body, 0, unroll=4)
+
+
+def spare_rows(z, held, start, count):
+    return [held[pl.ds(z.rows + start + k, z.blocks, stride=z.pitch), :] for k in range(count)]
+
+
+def first_features(z, held, start, taps):
+    last, end, first, second = spare_rows(z, held, start, 4)
+    top = lax.broadcasted_iota(jnp.int32, last.shape, 0) == 0
+    two_before, before = [jnp.where(top, 0.0, pltpu.roll(rows, 1, 0)) for rows in (last, end)]
+    return [
+        (taps[0:1] * now + taps[1:2] * one + taps[2:3] * two).astype(bf16).astype(f32)
+        for now, one, two in ((first, before, two_before), (second, first, before))
+    ]
+
+
+def put_first_rows(z, held, products):
+    for k, (left, right) in enumerate(products):
+        held[pl.ds(k, z.blocks, stride=z.pitch), :] = (left * right).astype(bf16).astype(f32)
+
+
 def signal_grad_kernel(
-    z, data_ref, filter_ref, coarse_ref, fine_ref, inv_ref, back_ref, spec_ref, out_ref, held, parts
+    z, data_ref, taps_ref, filter_ref, coarse_ref, fine_ref, inv_ref, back_ref, spec_ref, out_ref, held, parts
 ):
-    load_blocks(z, lambda i: data_ref[i], held)
+    load_longer(z, data_ref, held)
+    put_first_rows(z, held, zip(first_features(z, held, 0, taps_ref[2]), spare_rows(z, held, 4, 2)))
     coarse_forward(z, held, coarse_ref, parts, False)
 
     def body(a, carry):
@@ -148,9 +176,25 @@
 
 
 def conv_out_kernel(
-    z, data_ref, filter_ref, grad_ref, coarse_ref, fine_ref, inv_ref, back_ref, out_ref, long_ref, held, parts, more
+    z,
+    data_ref,
+    taps_ref,
+    filter_ref,
+    grad_ref,
+    coarse_ref,
+    fine_ref,
+    inv_ref,
+    back_ref,
+    out_ref,
+    long_ref,
+    held,
+    parts,
+    more,
 ):
-    load_blocks(z, lambda i: data_ref[i], held)
+    load_longer(z, data_ref, held)
+    put_first_rows(
+        z, held, zip(first_features(z, held, 0, taps_ref[0]), first_features(z, held, 4, taps_ref[1]))
+    )
     coarse_forward(z, held, coarse_ref, parts, False)
     spare = (z.parts - 2 * z.half) * z.pitch
     if spare:
@@ -220,20 +264,19 @@
 
 
 def outer_kernel(out_ref, cot_ref, taps_ref, outer_ref):
-    feat_out, _ = feature(out_ref[...], jnp.zeros((8, out_ref.shape[1]), f32), 2, taps_ref)
-    outward(outer_ref, feat_out * cot_ref[...].astype(f32))
-
-
-def outer_head_kernel(old_ref, out_ref, cot_ref, halo_ref, taps_ref, outer_ref):
-    feat_out, _ = feature(out_ref[...], halo_ref[...].astype(f32), 2, taps_ref)
-    outward(outer_ref, feat_out * cot_ref[...].astype(f32))
-
-
-def signal_kernel(gate_ref, value_ref, halo_ref, taps_ref, signal_ref):
-    halo = halo_ref[...].astype(f32)
-    feat_gate, _ = feature(gate_ref[...], halo, 0, taps_ref)
-    feat_value, _ = feature(value_ref[...], halo, 1, taps_ref)
-    outward(signal_ref, feat_gate * feat_value)
+    rows, cot = out_ref[...].astype(f32), cot_ref[...].astype(f32)
+    feat_out, _ = feature(out_ref[...], jnp.zeros((8, rows.shape[1]), f32), 2, taps_ref)
+    more = collect([rows[rows.shape[0] - 2 :], rows[0:2], cot[0:2]], PAD, f32)
+    outward(outer_ref, jnp.concatenate([feat_out * cot, more], axis=0))
+
+
+def signal_kernel(gate_ref, value_ref, taps_ref, signal_ref):
+    none = jnp.zeros((8, gate_ref.shape[1]), f32)
+    feat_gate, (gate, _, _) = feature(gate_ref[...], none, 0, taps_ref)
+    feat_value, (value, _, _) = feature(value_ref[...], none, 1, taps_ref)
+    count = gate.shape[0]
+    more = collect([gate[count - 2 :], gate[0:2], value[count - 2 :], value[0:2]], PAD, f32)
+    outward(signal_ref, jnp.concatenate([feat_gate * feat_value, more], axis=0))
 
 
 def edges_kernel(gate_ref, value_ref, out_ref, edge_ref):
@@ -374,11 +417,8 @@
             "six": pl.BlockSpec((tile // quarter, 6, quarter), lambda i: (i, 0, 0)),
             "near": pl.BlockSpec((6, quarter), lambda i: (0, 0)),
             "taps": pl.BlockSpec((3, 3, tile), lambda i: (0, 0, i)),
-            "left": pl.BlockSpec(memory_space=pl.ANY),
-            "whole": pl.BlockSpec(memory_space=pltpu.VMEM),
             "packet": pl.BlockSpec((z.blocks, z.pack, z.width), lambda i: (0, 0, 0)),
-            "first": pl.BlockSpec((16, tile), lambda i: (0, i)),
-            "moved_first": pl.BlockSpec((tile // z.width, 16, z.width), lambda i: (i, 0, 0)),
+            "longer": pl.BlockSpec((tile // z.width, z.pitch, z.width), lambda i: (i, 0, 0)),
             "last": pl.BlockSpec((16, tile), lambda i: (z.rows // 16 - 1, i)),
         }[kind]
 
@@ -386,7 +426,7 @@
         "rows": jax.ShapeDtypeStruct((z.rows, channels), bf16),
         "last": jax.ShapeDtypeStruct((z.rows, channels), bf16),
         "moved": jax.ShapeDtypeStruct((channels // z.width, z.rows, z.width), bf16),
-        "moved_first": jax.ShapeDtypeStruct((channels // z.width, z.rows, z.width), bf16),
+        "longer": jax.ShapeDtypeStruct((channels // z.width, z.pitch, z.width), bf16),
         "packet": jax.ShapeDtypeStruct((z.blocks, z.pack, z.width), bf16),
         "edge": jax.ShapeDtypeStruct((8, channels), bf16),
         "six": jax.ShapeDtypeStruct((4, 6, quarter), f32),
@@ -453,42 +493,34 @@
     def position(kernel, operands, kinds, outs, name, cost_us, **more):
         return position_call(z, kernel, operands, kinds, outs, channels, name, cost_us, **more)
 
-    (edges,) = position(edges_kernel, (gate_in, value_in, gate_out), ("last",) * 3, ("edge",), "edges", 1, tile=channels, vmem=60)
-    halo = lax.ppermute(edges, "seq", onward)
-
     (outer,) = position(
         outer_kernel,
         (gate_out, cotangent, short_filters),
         ("rows", "rows", "taps"),
-        ("moved",),
+        ("longer",),
         "outer",
         4,
-        vmem=59.5,
-    )
-    (outer,) = position(
-        outer_head_kernel,
-        (outer, gate_out, cotangent, halo, short_filters),
-        ("left", "first", "first", "whole", "taps"),
-        ("moved_first",),
-        "outer_head",
-        1,
-        tile=channels,
-        aliases={0: 0},
-        vmem=59.5,
-    )
+        vmem=60,
+    )
+    outer, last_gate = lax.optimization_barrier((outer, gate_in))
+    (edges,) = position(
+        edges_kernel, (last_gate, value_in, gate_out), ("last",) * 3, ("edge",), "edges", 1, tile=channels
+    )
+    halo = lax.ppermute(edges, "seq", onward)
     (signal,) = position(
-        signal_kernel, (gate_in, value_in, halo, short_filters), ("rows", "rows", "edge", "taps"), ("moved",), "signal", 4
+        signal_kernel, (gate_in, value_in, short_filters), ("rows", "rows", "taps"), ("longer",), "signal", 4
     )
     outer_moved = exchange(outer)
+    taps_here = lax.dynamic_slice_in_dim(short_filters, lax.axis_index("seq") * z.width, z.width, 2)
     (filter_spec,) = channel_call(
         z, functools.partial(filter_kernel, z), (long_filter, twice, fine), (spec_shape,), "filter_spec", 8
     )
-    signal, filter_spec = lax.optimization_barrier((signal, filter_spec))
+    signal, filter_spec, halo = lax.optimization_barrier((signal, filter_spec, halo))
     signal_moved = exchange(signal)
     outer_spec, sig_grad = channel_call(
         z,
         functools.partial(signal_grad_kernel, z),
-        (outer_moved, filter_spec, coarse, fine, inv, back),
+        (outer_moved, taps_here, filter_spec, coarse, fine, inv, back),
         (spec_shape, moved_shape),
         "signal_grad",
         16,
@@ -497,7 +529,7 @@
     conv_out, grad_long = channel_call(
         z,
         functools.partial(conv_out_kernel, z),
-        (signal_moved, filter_spec, outer_spec, coarse, fine, inv, back),
+        (signal_moved, taps_here, filter_spec, outer_spec, coarse, fine, inv, back),
         (moved_shape, jax.ShapeDtypeStruct((z.blocks * z.rows, z.width), f32)),
         "conv_out",
         22,

time: 179 us -> 175 us (0.978)
  waiting for transfers between devices: 66.9 us -> 73 us
  local copies, waits for them, and re-layouts: 25.1 us -> 19.3 us
  Pallas kernels: 45.2 us -> 42 us
    unnamed x56 -> x50, local copies, waits for them, and re-layouts: 24.5 us -> 19.3 us
    all_to_all x5, waiting for transfers between devices: 60.4 us -> 65.6 us  [exchange(): return lax.all_to_all(value, 'seq', split_axis=0, concat_axis=0, tiled=True)]
    pallas_call x9 -> x8, Pallas kernels: 22.3 us -> 19 us  [position_call(): pl.pallas_call(kernel, grid=(channels // tile,), out_shape=[shapes[k] for...]
    all_to_all x5, starting transfers between devices: 30.2 us -> 28.2 us  [exchange(): return lax.all_to_all(value, 'seq', split_axis=0, concat_axis=0, tiled=True)]
  transfers between devices with their start and end apart: 14 -> 14, of which waited for: 9 -> 9; matrix products, arithmetic and copies ran while one was open for 1% -> 0% of each run, Pallas kernels for 22% -> 21%
where the time goes in v4:
time: 175 us; the launch traced here: 174 us
  waiting for transfers between devices  73 us (42%)
  Pallas kernels  42 us (24%)
  starting transfers between devices  37.5 us (21%)
  local copies, waits for them, and re-layouts  19.3 us (11%)
    all_to_all x5, waiting for transfers between devices, exchange(): return lax.all_to_all(value, 'seq', split_axis=0, concat_axis=0, tiled=True)  65.6 us
    all_to_all x5, starting transfers between devices, exchange(): return lax.all_to_all(value, 'seq', split_axis=0, concat_axis=0, tiled=True)  28.2 us
    pallas_call x3, Pallas kernels, channel_call(): pl.pallas_call(kernel, out_shape=outs, in_specs=[whole] * len(operands),...  21.2 us
    unnamed x50, local copies, waits for them, and re-layouts  19.3 us
    pallas_call x8, Pallas kernels, position_call(): pl.pallas_call(kernel, grid=(channels // tile,), out_shape=[shapes[k] for...  19 us
    ppermute x6, waiting for transfers between devices, swap(): return lax.ppermute(value, 'seq', [(i, i ^ bits) for i in range(self.size)])  7.44 us
    ppermute x6, starting transfers between devices, swap(): return lax.ppermute(value, 'seq', [(i, i ^ bits) for i in range(self.size)])  4.12 us
  transfers between devices with their start and end apart: 14, of which 9 were waited for; matrix products, arithmetic and copies ran while one was open for 0% of the time, Pallas kernels for 21%

profile of v4, /device:TPU:8, one launch (start us, length us, event | category | flops | bytes accessed | tf_op | source)
XLA Modules:
  0.0 173.5 jit_solution(17850490231372983147)
XLA Ops:
  0.7 3.2 %outer.1 = bf16[32,136,128]{2,1,0:T(8,128)(2,1)} custom-call(bf16[128,4096]{1,0:T(8,128)(2,1)} %out_ref.7, bf16[128,4096]{1,0:T(8,128)(2,1)} %cot_ref.5, f32[3,3,4096]{2,1,0:T(4,128)} %taps_ref.11), custom_call_target="tpu_custom_call" | custom-call | bytes 12000000 | tf_op jit(solution)/shard_map/outer/pallas_call | solution.py:434
  3.9 10.0 %all-to-all-start.1 = ((bf16[32,136,128]{2,1,0:T(8,128)(2,1)}), bf16[32,136,128]{2,1,0:T(8,128)(2,1)}, u32[]{:S(2)}, u32[]{:S(2)}) async-start(bf16[32,136,128]{2,1,0:T(8,128)(2,1)} %outer.1), calls=%async_computation.1 | async-start | bytes 2228224 | tf_op jit(solution)/shard_map/all_to_all | solution.py:481
  14.0 2.5 %collective-permute-start = (bf16[8,4096]{1,0:T(8,128)(2,1)S(1)}, bf16[8,4096]{1,0:T(8,128)(2,1)S(1)}, u32[]{:S(2)}, u32[]{:S(2)}) collective-permute-start(bf16[8,4096]{1,0:T(8,128)(2,1)S(1)} %edges.1), channel_id=1, source_target_pairs={{0,1},{1,2},{2,3},{3,4},{4,5},{5,6},{6,7},{7,8},{8,9},{9,10},{10,1... | collective-permute-start | bytes 196616 | tf_op jit(solution)/shard_map/ppermute | solution.py:509
  16.5 1.9 %signal.1 = bf16[32,136,128]{2,1,0:T(8,128)(2,1)S(1)} custom-call(bf16[128,4096]{1,0:T(8,128)(2,1)S(1)} %copy-done.6, bf16[128,4096]{1,0:T(8,128)(2,1)S(1)} %copy-done.8, f32[3,3,4096]{2,1,0:T(4,128)S(1)} %copy-done.11), custom_call_target="tpu_custom_call" | custom-call | bytes 12000000 | tf_op jit(solution)/shard_map/signal/pallas_call | solution.py:434
  18.5 1.0 copy-done.12
  19.5 3.3 %filter_spec.1.filter_ref = bf16[33,256,128]{2,1,0:T(8,128)(2,1)S(1)} custom-call(f32[4096,128]{1,0:T(8,128)S(1)} %copy-done.15, bf16[72,64]{1,0:T(8,128)(2,1)S(1)} %copy-done.22, bf16[33,256,256]{2,1,0:T(8,128)(2,1)S(1)} %copy-done), custom_call_target="tpu_custom_call" | custom-call | bytes 24000000 | tf_op jit(solution)/shard_map/filter_spec/pallas_call | solution.py:224
  22.8 20.8 %all-to-all-done.1.data_ref = bf16[32,136,128]{2,1,0:T(8,128)(2,1)} async-done(((bf16[32,136,128]{2,1,0:T(8,128)(2,1)}), bf16[32,136,128]{2,1,0:T(8,128)(2,1)}, u32[]{:S(2)}, u32[]{:S(2)}) %all-to-all-start.1) | async-done | bytes 1114144 | tf_op jit(solution)/shard_map/all_to_all | solution.py:481
  43.6 4.9 %all-to-all-start = ((bf16[32,136,128]{2,1,0:T(8,128)(2,1)}), bf16[32,136,128]{2,1,0:T(8,128)(2,1)}, u32[]{:S(2)}, u32[]{:S(2)}) async-start(bf16[32,136,128]{2,1,0:T(8,128)(2,1)} %copy-done.12), calls=%async_computation | async-start | bytes 2228224 | tf_op jit(solution)/shard_map/all_to_all | solution.py:481
  48.5 2.2 %copy-done.1 = bf16[33,256,256]{2,1,0:T(8,128)(2,1)S(1)} copy-done((bf16[33,256,256]{2,1,0:T(8,128)(2,1)S(1)}, bf16[33,256,256]{2,1,0:T(8,128)(2,1)}, u32[]{:S(2)}) %copy-start.1) | copy-done | bytes 4325400
  50.7 2.2 %copy-done.3 = bf16[33,256,256]{2,1,0:T(8,128)(2,1)S(1)} copy-done((bf16[33,256,256]{2,1,0:T(8,128)(2,1)S(1)}, bf16[33,256,256]{2,1,0:T(8,128)(2,1)}, u32[]{:S(2)}) %copy-start.3) | copy-done | bytes 4325400
  52.9 7.4 %signal_grad.1 = (bf16[33,256,128]{2,1,0:T(8,128)(2,1)S(1)}, bf16[32,128,128]{2,1,0:T(8,128)(2,1)S(1)}) custom-call(bf16[32,136,128]{2,1,0:T(8,128)(2,1)} %all-to-all-done.1.data_ref, f32[3,3,128]{2,1,0:T(4,128)S(1)} %constant_dynamic-slice_fusion.taps_ref, bf16[33,256,128]{2,1,0:T(8,128)(2,1)S(1)} %filter_spec.1.filter_ref, bf16[72,32]{1,0:T(8,128)(2,1)S(1)} %copy-done.20, ...), custom_call_target="tpu_custom_call" | custom-call | bytes 48000000 | tf_op jit(solution)/shard_map/signal_grad/pallas_call | solution.py:224
  60.4 1.3 copy-done.13
  61.7 1.0 copy-done.17
  62.7 15.4 %all-to-all-done.data_ref = bf16[32,136,128]{2,1,0:T(8,128)(2,1)} async-done(((bf16[32,136,128]{2,1,0:T(8,128)(2,1)}), bf16[32,136,128]{2,1,0:T(8,128)(2,1)}, u32[]{:S(2)}, u32[]{:S(2)}) %all-to-all-start) | async-done | bytes 1114144 | tf_op jit(solution)/shard_map/all_to_all | solution.py:481
  78.1 4.7 %all-to-all-start.3 = ((bf16[32,128,128]{2,1,0:T(8,128)(2,1)}), bf16[32,128,128]{2,1,0:T(8,128)(2,1)}, u32[]{:S(2)}, u32[]{:S(2)}) async-start(bf16[32,128,128]{2,1,0:T(8,128)(2,1)} %copy-done.17), calls=%async_computation.3 | async-start | bytes 2097152 | tf_op jit(solution)/shard_map/all_to_all | solution.py:481
  82.8 2.2 %copy-done.2 = bf16[33,256,256]{2,1,0:T(8,128)(2,1)S(1)} copy-done((bf16[33,256,256]{2,1,0:T(8,128)(2,1)S(1)}, bf16[33,256,256]{2,1,0:T(8,128)(2,1)}, u32[]{:S(2)}) %copy-start.2) | copy-done | bytes 4325400
  85.0 2.2 %copy-done.4 = bf16[33,256,256]{2,1,0:T(8,128)(2,1)S(1)} copy-done((bf16[33,256,256]{2,1,0:T(8,128)(2,1)S(1)}, bf16[33,256,256]{2,1,0:T(8,128)(2,1)}, u32[]{:S(2)}) %copy-start.4) | copy-done | bytes 4325400
  87.2 1.6 copy-done.14
  88.9 10.6 %conv_out.1 = (bf16[32,128,128]{2,1,0:T(8,128)(2,1)S(1)}, f32[4096,128]{1,0:T(8,128)}) custom-call(bf16[32,136,128]{2,1,0:T(8,128)(2,1)} %all-to-all-done.data_ref, f32[3,3,128]{2,1,0:T(4,128)S(1)} %constant_dynamic-slice_fusion.taps_ref, bf16[33,256,128]{2,1,0:T(8,128)(2,1)S(1)} %filter_spec.1.filter_ref, bf16[33,256,128]{2,1,0:T(8,128)(2,1)S(1)} %copy-done.14, ...), custom_call_target="tpu_custom_call" | custom-call | bytes 66000000 | tf_op jit(solution)/shard_map/conv_out/pallas_call | solution.py:224
  99.4 1.0 copy-done.16
  100.4 10.7 %all-to-all-done.3.sig_ref = bf16[32,128,128]{2,1,0:T(8,128)(2,1)} async-done(((bf16[32,128,128]{2,1,0:T(8,128)(2,1)}), bf16[32,128,128]{2,1,0:T(8,128)(2,1)}, u32[]{:S(2)}, u32[]{:S(2)}) %all-to-all-start.3) | async-done | bytes 1048608 | tf_op jit(solution)/shard_map/all_to_all | solution.py:481
  111.1 4.1 %all-to-all-start.2 = ((bf16[32,128,128]{2,1,0:T(8,128)(2,1)}), bf16[32,128,128]{2,1,0:T(8,128)(2,1)S(1)}, u32[]{:S(2)}, u32[]{:S(2)}) async-start(bf16[32,128,128]{2,1,0:T(8,128)(2,1)} %copy-done.16), calls=%async_computation.2 | async-start | bytes 2097152 | tf_op jit(solution)/shard_map/all_to_all | solution.py:481
  115.3 1.2 copy-done.9
  116.5 6.7 %input_grads.1 = (f32[4,6,1024]{2,1,0:T(8,128)S(1)}, bf16[8,4096]{1,0:T(8,128)(2,1)S(1)}, bf16[8,4096]{1,0:T(8,128)(2,1)S(1)}, bf16[128,4096]{1,0:T(8,128)(2,1)}, bf16[128,4096]{1,0:T(8,128)(2,1)}) custom-call(bf16[32,128,128]{2,1,0:T(8,128)(2,1)} %all-to-all-done.3.sig_ref, bf16[128,4096]{1,0:T(8,128)(2,1)S(1)} %copy-done.7, ...), custom_call_target="tpu_custom_call" | custom-call | bytes 18000000 | tf_op jit(solution)/shard_map/input_grads/pallas_call | solution.py:434
  123.2 0.7 copy-done.19
  123.8 0.4 collective-permute-start.1
  124.2 1.8 %collective-permute-start.2 = (f32[6,1024]{1,0:T(8,128)S(1)}, f32[6,1024]{1,0:T(8,128)S(1)}, u32[]{:S(2)}, u32[]{:S(2)}) collective-permute-start(f32[6,1024]{1,0:T(8,128)S(1)} %get-tuple-element.53), channel_id=1, source_target_pairs={{0,16},{1,17},{2,18},{3,19},{4,20},{5,21},{6,22},{7,23},{8,24},{9,... | collective-permute-start | bytes 73736 | tf_op jit(solution)/shard_map/ppermute | solution.py:467
  126.0 3.4 %collective-permute-done.2 = f32[6,1024]{1,0:T(8,128)S(1)} collective-permute-done((f32[6,1024]{1,0:T(8,128)S(1)}, f32[6,1024]{1,0:T(8,128)S(1)}, u32[]{:S(2)}, u32[]{:S(2)}) %collective-permute-start.2) | collective-permute-done | bytes 24608 | tf_op jit(solution)/shard_map/ppermute | solution.py:467
  129.4 0.8 collective-permute-done.3
  130.2 0.8 fusion.in_sums_ref
  131.0 12.6 %all-to-all-done.2.conv_ref = bf16[32,128,128]{2,1,0:T(8,128)(2,1)S(1)} async-done(((bf16[32,128,128]{2,1,0:T(8,128)(2,1)}), bf16[32,128,128]{2,1,0:T(8,128)(2,1)S(1)}, u32[]{:S(2)}, u32[]{:S(2)}) %all-to-all-start.2) | async-done | bytes 1048608 | tf_op jit(solution)/shard_map/all_to_all | solution.py:481
  143.6 1.2 copy-done.10
  144.8 1.3 output_sums.1
  146.2 0.7 copy-done.18
  146.9 0.6 copy-done.24
  147.5 4.6 %all-to-all-start.4 = ((bf16[32,40,128]{2,1,0:T(8,128)(2,1)}), bf16[32,40,128]{2,1,0:T(8,128)(2,1)}, u32[]{:S(2)}, u32[]{:S(2)}) async-start(bf16[32,40,128]{2,1,0:T(8,128)(2,1)} %copy-done.18), calls=%async_computation.4 | async-start | bytes 655360 | tf_op jit(solution)/shard_map/all_to_all | solution.py:481
  152.1 1.3 collective-permute-start.5
  153.4 1.3 collective-permute-start.4
  154.7 2.0 %mixed.1 = bf16[128,4096]{1,0:T(8,128)(2,1)} custom-call(bf16[32,128,128]{2,1,0:T(8,128)(2,1)S(1)} %all-to-all-done.2.conv_ref, bf16[128,4096]{1,0:T(8,128)(2,1)S(1)} %copy-done.5, bf16[8,4096]{1,0:T(8,128)(2,1)S(1)} %collective-permute-done.halo_ref, f32[3,3,4096]{2,1,0:T(4,128)S(1)} %copy-done.11), custom_call_target="tpu_custom_call" | custom-call | bytes 9000000 | tf_op jit(solution)/shard_map/mixed/pallas_call | solution.py:434
  156.7 1.8 %finish_input_grads.1 = (bf16[128,4096]{1,0:T(8,128)(2,1)}, bf16[128,4096]{1,0:T(8,128)(2,1)}) custom-call(bf16[128,4096]{1,0:T(8,128)(2,1)} %get-tuple-element.40.gate_ref, bf16[128,4096]{1,0:T(8,128)(2,1)} %get-tuple-element.41.value_ref, bf16[8,4096]{1,0:T(8,128)(2,1)S(1)} %collective-permute-done.5.next_ref, ...), custom_call_target="tpu_custom_call", output_to_operand_aliasing={{0}: (0, {}), {1}: (1, {})} | custom-call | bytes 6000000 | tf_op jit(solution)/shard_map/finish_input_grads/pallas_call | solution.py:434
  158.5 2.1 %output_grad.1 = bf16[128,4096]{1,0:T(8,128)(2,1)} custom-call(bf16[32,128,128]{2,1,0:T(8,128)(2,1)S(1)} %all-to-all-done.2.conv_ref, bf16[128,4096]{1,0:T(8,128)(2,1)S(1)} %copy-done.10, bf16[8,4096]{1,0:T(8,128)(2,1)S(1)} %collective-permute-done.4.next_ref, f32[3,3,4096]{2,1,0:T(4,128)S(1)} %copy-done.11), custom_call_target="tpu_custom_call" | custom-call | bytes 9000000 | tf_op jit(solution)/shard_map/output_grad/pallas_call | solution.py:434
  160.5 6.1 %all-to-all-done.4.packet_ref = bf16[32,40,128]{2,1,0:T(8,128)(2,1)} async-done(((bf16[32,40,128]{2,1,0:T(8,128)(2,1)}), bf16[32,40,128]{2,1,0:T(8,128)(2,1)}, u32[]{:S(2)}, u32[]{:S(2)}) %all-to-all-start.4) | async-done | bytes 327712 | tf_op jit(solution)/shard_map/all_to_all | solution.py:481
  166.6 1.0 packet_sums.1
  167.7 1.2 collective-permute-start.8
  168.8 0.5 collective-permute-start.7
  169.6 1.8 %collective-permute-done.8 = f32[72,128]{1,0:T(8,128)S(1)} collective-permute-done((f32[72,128]{1,0:T(8,128)S(1)}, f32[72,128]{1,0:T(8,128)S(1)}, u32[]{:S(2)}, u32[]{:S(2)}) %collective-permute-start.8) | collective-permute-done | bytes 36896 | tf_op jit(solution)/shard_map/ppermute | solution.py:467
  171.4 1.4 collective-permute-done.7
  172.8 0.7 grad_short.1
  (47 shorter events, 0.5 us)
Async XLA Ops:
  0.6 13.3 %copy-start.5 = (bf16[128,4096]{1,0:T(8,128)(2,1)S(1)}, bf16[128,4096]{1,0:T(8,128)(2,1)}, u32[]{:S(2)}) copy-start(bf16[128,4096]{1,0:T(8,128)(2,1)} %out_ref.7) | copy-start | bytes 3145732
  0.6 13.3 %copy-start.6 = (bf16[128,4096]{1,0:T(8,128)(2,1)S(1)}, bf16[128,4096]{1,0:T(8,128)(2,1)}, u32[]{:S(2)}) copy-start(bf16[128,4096]{1,0:T(8,128)(2,1)} %gate_ref.4) | copy-start | bytes 3145732
  0.7 13.3 %copy-start.8 = (bf16[128,4096]{1,0:T(8,128)(2,1)S(1)}, bf16[128,4096]{1,0:T(8,128)(2,1)}, u32[]{:S(2)}) copy-start(bf16[128,4096]{1,0:T(8,128)(2,1)} %value_ref.5) | copy-start | bytes 3145732
  3.9 12.7 %copy-start.11 = (f32[3,3,4096]{2,1,0:T(4,128)S(1)}, f32[3,3,4096]{2,1,0:T(4,128)}, u32[]{:S(2)}) copy-start(f32[3,3,4096]{2,1,0:T(4,128)} %taps_ref.11) | copy-start | bytes 442372
  3.9 39.7 %all-to-all-start.1 = ((bf16[32,136,128]{2,1,0:T(8,128)(2,1)}), bf16[32,136,128]{2,1,0:T(8,128)(2,1)}, u32[]{:S(2)}, u32[]{:S(2)}) async-start(bf16[32,136,128]{2,1,0:T(8,128)(2,1)} %outer.1), calls=%async_computation.1 | async-start | bytes 2228224 | tf_op jit(solution)/shard_map/all_to_all | solution.py:481
  13.9 5.6 %copy-start = (bf16[33,256,256]{2,1,0:T(8,128)(2,1)S(1)}, bf16[33,256,256]{2,1,0:T(8,128)(2,1)}, u32[]{:S(2)}) copy-start(bf16[33,256,256]{2,1,0:T(8,128)(2,1)} %constant.61.clone.fine_ref) | copy-start | bytes 12976132
  14.0 5.5 %copy-start.15 = (f32[4096,128]{1,0:T(8,128)S(1)}, f32[4096,128]{1,0:T(8,128)}, u32[]{:S(2)}) copy-start(f32[4096,128]{1,0:T(8,128)} %filter_ref.1) | copy-start | bytes 6291460
  14.0 5.5 %copy-start.22 = (bf16[72,64]{1,0:T(8,128)(2,1)S(1)}, bf16[72,64]{1,0:T(8,128)(2,1)}, u32[]{:S(2)}) copy-start(bf16[72,64]{1,0:T(8,128)(2,1)} %constant.60.clone.twice_ref) | copy-start | bytes 27652
  14.0 8.8 %collective-permute-start = (bf16[8,4096]{1,0:T(8,128)(2,1)S(1)}, bf16[8,4096]{1,0:T(8,128)(2,1)S(1)}, u32[]{:S(2)}, u32[]{:S(2)}) collective-permute-start(bf16[8,4096]{1,0:T(8,128)(2,1)S(1)} %edges.1), channel_id=1, source_target_pairs={{0,1},{1,2},{2,3},{3,4},{4,5},{5,6},{6,7},{7,8},{8,9},{9,10},{10,1... | collective-permute-start | bytes 196616 | tf_op jit(solution)/shard_map/ppermute | solution.py:509
  18.5 1.0 copy-start.12
  22.8 25.7 %copy-start.20 = (bf16[72,32]{1,0:T(8,128)(2,1)S(1)}, bf16[72,32]{1,0:T(8,128)(2,1)}, u32[]{:S(2)}) copy-start(bf16[72,32]{1,0:T(8,128)(2,1)} %constant.59.clone.coarse_ref) | copy-start | bytes 13828
  22.8 25.7 %copy-start.21 = (bf16[32,72]{1,0:T(8,128)(2,1)S(1)}, bf16[32,72]{1,0:T(8,128)(2,1)}, u32[]{:S(2)}) copy-start(bf16[32,72]{1,0:T(8,128)(2,1)} %constant.63.clone.back_ref) | copy-start | bytes 13828
  43.6 34.6 %all-to-all-start = ((bf16[32,136,128]{2,1,0:T(8,128)(2,1)}), bf16[32,136,128]{2,1,0:T(8,128)(2,1)}, u32[]{:S(2)}, u32[]{:S(2)}) async-start(bf16[32,136,128]{2,1,0:T(8,128)(2,1)} %copy-done.12), calls=%async_computation | async-start | bytes 2228224 | tf_op jit(solution)/shard_map/all_to_all | solution.py:481
  48.5 2.2 %copy-start.1 = (bf16[33,256,256]{2,1,0:T(8,128)(2,1)S(1)}, bf16[33,256,256]{2,1,0:T(8,128)(2,1)}, u32[]{:S(2)}) copy-start(bf16[33,256,256]{2,1,0:T(8,128)(2,1)} %constant.61.clone.fine_ref) | copy-start | bytes 12976132
  50.7 2.2 %copy-start.3 = (bf16[33,256,256]{2,1,0:T(8,128)(2,1)S(1)}, bf16[33,256,256]{2,1,0:T(8,128)(2,1)}, u32[]{:S(2)}) copy-start(bf16[33,256,256]{2,1,0:T(8,128)(2,1)} %constant.62.clone.inv_ref) | copy-start | bytes 12976132
  60.4 1.4 copy-start.13
  61.7 1.0 copy-start.17
  78.1 33.0 %all-to-all-start.3 = ((bf16[32,128,128]{2,1,0:T(8,128)(2,1)}), bf16[32,128,128]{2,1,0:T(8,128)(2,1)}, u32[]{:S(2)}, u32[]{:S(2)}) async-start(bf16[32,128,128]{2,1,0:T(8,128)(2,1)} %copy-done.17), calls=%async_computation.3 | async-start | bytes 2097152 | tf_op jit(solution)/shard_map/all_to_all | solution.py:481
  82.8 2.2 %copy-start.2 = (bf16[33,256,256]{2,1,0:T(8,128)(2,1)S(1)}, bf16[33,256,256]{2,1,0:T(8,128)(2,1)}, u32[]{:S(2)}) copy-start(bf16[33,256,256]{2,1,0:T(8,128)(2,1)} %constant.61.clone.fine_ref) | copy-start | bytes 12976132
  85.0 2.2 %copy-start.4 = (bf16[33,256,256]{2,1,0:T(8,128)(2,1)S(1)}, bf16[33,256,256]{2,1,0:T(8,128)(2,1)}, u32[]{:S(2)}) copy-start(bf16[33,256,256]{2,1,0:T(8,128)(2,1)} %constant.62.clone.inv_ref) | copy-start | bytes 12976132
  87.2 1.6 copy-start.14
  99.4 1.0 copy-start.16
  100.4 14.9 %copy-start.7 = (bf16[128,4096]{1,0:T(8,128)(2,1)S(1)}, bf16[128,4096]{1,0:T(8,128)(2,1)}, u32[]{:S(2)}) copy-start(bf16[128,4096]{1,0:T(8,128)(2,1)} %gate_ref.4) | copy-start | bytes 3145732
  111.1 32.5 %all-to-all-start.2 = ((bf16[32,128,128]{2,1,0:T(8,128)(2,1)}), bf16[32,128,128]{2,1,0:T(8,128)(2,1)S(1)}, u32[]{:S(2)}, u32[]{:S(2)}) async-start(bf16[32,128,128]{2,1,0:T(8,128)(2,1)} %copy-done.16), calls=%async_computation.2 | async-start | bytes 2097152 | tf_op jit(solution)/shard_map/all_to_all | solution.py:481
  115.3 1.2 copy-start.9
  123.2 0.7 copy-start.19
  123.2 6.2 %copy-start.23 = (bf16[8,4096]{1,0:T(8,128)(2,1)}, bf16[8,4096]{1,0:T(8,128)(2,1)S(1)}, u32[]{:S(2)}) copy-start(bf16[8,4096]{1,0:T(8,128)(2,1)S(1)} %get-tuple-element.42) | copy-start | bytes 196612
  123.8 2.2 %collective-permute-start.1 = (f32[6,1024]{1,0:T(8,128)S(1)}, f32[6,1024]{1,0:T(8,128)S(1)}, u32[]{:S(2)}, u32[]{:S(2)}) collective-permute-start(f32[6,1024]{1,0:T(8,128)S(1)} %get-tuple-element.54), channel_id=1, source_target_pairs={{0,1},{1,0},{2,3},{3,2},{4,5},{5,4},{6,7},{7,6},{8,9},{9,8},{10,11... | collective-permute-start | bytes 73736 | tf_op jit(solution)/shard_map/ppermute | solution.py:467
  124.2 5.2 %collective-permute-start.2 = (f32[6,1024]{1,0:T(8,128)S(1)}, f32[6,1024]{1,0:T(8,128)S(1)}, u32[]{:S(2)}, u32[]{:S(2)}) collective-permute-start(f32[6,1024]{1,0:T(8,128)S(1)} %get-tuple-element.53), channel_id=1, source_target_pairs={{0,16},{1,17},{2,18},{3,19},{4,20},{5,21},{6,22},{7,23},{8,24},{9,... | collective-permute-start | bytes 73736 | tf_op jit(solution)/shard_map/ppermute | solution.py:467
  126.0 4.3 %collective-permute-start.3 = (f32[6,1024]{1,0:T(8,128)S(1)}, f32[6,1024]{1,0:T(8,128)S(1)}, u32[]{:S(2)}, u32[]{:S(2)}) collective-permute-start(f32[6,1024]{1,0:T(8,128)S(1)} %get-tuple-element.52), channel_id=1, source_target_pairs={{0,17},{1,16},{2,19},{3,18},{4,21},{5,20},{6,23},{7,22},{8,25},{9,... | collective-permute-start | bytes 73736 | tf_op jit(solution)/shard_map/ppermute | solution.py:467
  143.6 1.2 copy-start.10
  146.2 0.7 copy-start.18
  146.9 0.6 copy-start.24
  147.5 19.1 %all-to-all-start.4 = ((bf16[32,40,128]{2,1,0:T(8,128)(2,1)}), bf16[32,40,128]{2,1,0:T(8,128)(2,1)}, u32[]{:S(2)}, u32[]{:S(2)}) async-start(bf16[32,40,128]{2,1,0:T(8,128)(2,1)} %copy-done.18), calls=%async_computation.4 | async-start | bytes 655360 | tf_op jit(solution)/shard_map/all_to_all | solution.py:481
  152.1 4.6 %collective-permute-start.5 = (bf16[8,4096]{1,0:T(8,128)(2,1)}, bf16[8,4096]{1,0:T(8,128)(2,1)S(1)}, u32[]{:S(2)}, u32[]{:S(2)}) collective-permute-start(bf16[8,4096]{1,0:T(8,128)(2,1)} %copy-done.23), channel_id=1, source_target_pairs={{1,0},{2,1},{3,2},{4,3},{5,4},{6,5},{7,6},{8,7},{9,8},{10,9},{11,1... | collective-permute-start | bytes 196616 | tf_op jit(solution)/shard_map/ppermute | solution.py:549
  153.4 5.1 %collective-permute-start.4 = (bf16[8,4096]{1,0:T(8,128)(2,1)}, bf16[8,4096]{1,0:T(8,128)(2,1)S(1)}, u32[]{:S(2)}, u32[]{:S(2)}) collective-permute-start(bf16[8,4096]{1,0:T(8,128)(2,1)} %copy-done.24), channel_id=1, source_target_pairs={{1,0},{2,1},{3,2},{4,3},{5,4},{6,5},{7,6},{8,7},{9,8},{10,9},{11,1... | collective-permute-start | bytes 196616 | tf_op jit(solution)/shard_map/ppermute | solution.py:559
  167.7 3.8 %collective-permute-start.8 = (f32[72,128]{1,0:T(8,128)S(1)}, f32[72,128]{1,0:T(8,128)S(1)}, u32[]{:S(2)}, u32[]{:S(2)}) collective-permute-start(f32[72,128]{1,0:T(8,128)S(1)} %packet_sums.1), channel_id=1, source_target_pairs={{0,17},{1,16},{2,19},{3,18},{4,21},{5,20},{6,23},{7,22},{8,25},{9,... | collective-permute-start | bytes 110600 | tf_op jit(solution)/shard_map/ppermute | solution.py:467
  168.8 4.0 %collective-permute-start.7 = (f32[72,128]{1,0:T(8,128)S(1)}, f32[72,128]{1,0:T(8,128)S(1)}, u32[]{:S(2)}, u32[]{:S(2)}) collective-permute-start(f32[72,128]{1,0:T(8,128)S(1)} %packet_sums.1), channel_id=1, source_target_pairs={{0,16},{1,17},{2,18},{3,19},{4,20},{5,21},{6,22},{7,23},{8,24},{9,... | collective-permute-start | bytes 110600 | tf_op jit(solution)/shard_map/ppermute | solution.py:467
  169.3 3.5 %collective-permute-start.6 = (f32[72,128]{1,0:T(8,128)S(1)}, f32[72,128]{1,0:T(8,128)S(1)}, u32[]{:S(2)}, u32[]{:S(2)}) collective-permute-start(f32[72,128]{1,0:T(8,128)S(1)} %packet_sums.1), channel_id=1, source_target_pairs={{0,1},{1,0},{2,3},{3,2},{4,5},{5,4},{6,7},{7,6},{8,9},{9,8},{10,11... | collective-permute-start | bytes 110600 | tf_op jit(solution)/shard_map/ppermute | solution.py:467

commit v5 on v4

--- a/solution.py
+++ b/solution.py
@@ -230,7 +230,7 @@
             pltpu.VMEM((z.blocks * z.pitch, z.width), f32),
         ]
         + [pltpu.VMEM((z.parts * z.pitch, z.width), f32)] * arrays,
-        compiler_params=pltpu.CompilerParams(vmem_limit_bytes=(20 + 8 * arrays) << 20),
+        compiler_params=pltpu.CompilerParams(vmem_limit_bytes=(16 + 7 * arrays) << 20),
         cost_estimate=pl.CostEstimate(flops=0, bytes_accessed=int(cost_us * 3e6), transcendentals=0),
         name=name,
     )(*operands)
@@ -238,6 +238,8 @@
 
 def delayed(rows, before, lag):
     moved = pltpu.roll(rows, lag, 0)
+    if before is None:
+        return moved
     index = lax.broadcasted_iota(jnp.int32, rows.shape, 0)
     for i in range(lag):
         moved = jnp.where(index == i, before[2 - lag + i : 3 - lag + i], moved)
@@ -246,7 +248,7 @@
 
 def feature(source, halo, which, taps_ref):
     rows = source.astype(f32)
-    before = halo[2 * which : 2 * which + 2]
+    before = None if halo is None else halo[2 * which : 2 * which + 2]
     one, two = delayed(rows, before, 1), delayed(rows, before, 2)
     taps = taps_ref[which]
     feat = taps[0:1] * rows + taps[1:2] * one + taps[2:3] * two
@@ -265,15 +267,14 @@
 
 def outer_kernel(out_ref, cot_ref, taps_ref, outer_ref):
     rows, cot = out_ref[...].astype(f32), cot_ref[...].astype(f32)
-    feat_out, _ = feature(out_ref[...], jnp.zeros((8, rows.shape[1]), f32), 2, taps_ref)
+    feat_out, _ = feature(out_ref[...], None, 2, taps_ref)
     more = collect([rows[rows.shape[0] - 2 :], rows[0:2], cot[0:2]], PAD, f32)
     outward(outer_ref, jnp.concatenate([feat_out * cot, more], axis=0))
 
 
 def signal_kernel(gate_ref, value_ref, taps_ref, signal_ref):
-    none = jnp.zeros((8, gate_ref.shape[1]), f32)
-    feat_gate, (gate, _, _) = feature(gate_ref[...], none, 0, taps_ref)
-    feat_value, (value, _, _) = feature(value_ref[...], none, 1, taps_ref)
+    feat_gate, (gate, _, _) = feature(gate_ref[...], None, 0, taps_ref)
+    feat_value, (value, _, _) = feature(value_ref[...], None, 1, taps_ref)
     count = gate.shape[0]
     more = collect([gate[count - 2 :], gate[0:2], value[count - 2 :], value[0:2]], PAD, f32)
     outward(signal_ref, jnp.concatenate([feat_gate * feat_value, more], axis=0))
@@ -312,7 +313,16 @@
 
 
 def input_grads_kernel(
-    sig_ref, gate_ref, value_ref, halo_ref, taps_ref, sums_ref, head_ref, tail_ref, grad_gate_ref, grad_value_ref
+    sig_ref,
+    gate_ref,
+    value_ref,
+    halo_ref,
+    taps_ref,
+    sums_ref,
+    head_ref,
+    tail_ref,
+    grad_gate_ref,
+    grad_value_ref,
 ):
     halo = halo_ref[...].astype(f32)
     sig = inward(sig_ref)

time: 175 us -> 175 us (level)
  no operation moved by 1% of the time
where the time goes in v5:
time: 175 us; the launch traced here: 174 us
  waiting for transfers between devices  73.1 us (42%)
  Pallas kernels  41.9 us (24%)
  starting transfers between devices  37.5 us (21%)
  local copies, waits for them, and re-layouts  19.3 us (11%)
    all_to_all x5, waiting for transfers between devices, exchange(): return lax.all_to_all(value, 'seq', split_axis=0, concat_axis=0, tiled=True)  65.6 us
    all_to_all x5, starting transfers between devices, exchange(): return lax.all_to_all(value, 'seq', split_axis=0, concat_axis=0, tiled=True)  28.2 us
    pallas_call x3, Pallas kernels, channel_call(): pl.pallas_call(kernel, out_shape=outs, in_specs=[whole] * len(operands),...  21.3 us
    unnamed x50, local copies, waits for them, and re-layouts  19.3 us
    pallas_call x8, Pallas kernels, position_call(): pl.pallas_call(kernel, grid=(channels // tile,), out_shape=[shapes[k] for...  18.9 us
    ppermute x6, waiting for transfers between devices, swap(): return lax.ppermute(value, 'seq', [(i, i ^ bits) for i in range(self.size)])  7.44 us
    ppermute x6, starting transfers between devices, swap(): return lax.ppermute(value, 'seq', [(i, i ^ bits) for i in range(self.size)])  4.12 us
  transfers between devices with their start and end apart: 14, of which 9 were waited for; matrix products, arithmetic and copies ran while one was open for 0% of the time, Pallas kernels for 21%

profile of v5, /device:TPU:8, one launch (start us, length us, event | category | flops | bytes accessed | tf_op | source)
XLA Modules:
  0.0 173.5 jit_solution(12071746983134273563)
XLA Ops:
  0.7 3.2 %outer.1 = bf16[32,136,128]{2,1,0:T(8,128)(2,1)} custom-call(bf16[128,4096]{1,0:T(8,128)(2,1)} %out_ref.7, bf16[128,4096]{1,0:T(8,128)(2,1)} %cot_ref.5, f32[3,3,4096]{2,1,0:T(4,128)} %taps_ref.11), custom_call_target="tpu_custom_call" | custom-call | bytes 12000000 | tf_op jit(solution)/shard_map/outer/pallas_call | solution.py:444
  3.8 10.0 %all-to-all-start.1 = ((bf16[32,136,128]{2,1,0:T(8,128)(2,1)}), bf16[32,136,128]{2,1,0:T(8,128)(2,1)}, u32[]{:S(2)}, u32[]{:S(2)}) async-start(bf16[32,136,128]{2,1,0:T(8,128)(2,1)} %outer.1), calls=%async_computation.1 | async-start | bytes 2228224 | tf_op jit(solution)/shard_map/all_to_all | solution.py:491
  14.0 2.5 %collective-permute-start = (bf16[8,4096]{1,0:T(8,128)(2,1)S(1)}, bf16[8,4096]{1,0:T(8,128)(2,1)S(1)}, u32[]{:S(2)}, u32[]{:S(2)}) collective-permute-start(bf16[8,4096]{1,0:T(8,128)(2,1)S(1)} %edges.1), channel_id=1, source_target_pairs={{0,1},{1,2},{2,3},{3,4},{4,5},{5,6},{6,7},{7,8},{8,9},{9,10},{10,1... | collective-permute-start | bytes 196616 | tf_op jit(solution)/shard_map/ppermute | solution.py:519
  16.5 1.9 %signal.1 = bf16[32,136,128]{2,1,0:T(8,128)(2,1)S(1)} custom-call(bf16[128,4096]{1,0:T(8,128)(2,1)S(1)} %copy-done.6, bf16[128,4096]{1,0:T(8,128)(2,1)S(1)} %copy-done.8, f32[3,3,4096]{2,1,0:T(4,128)S(1)} %copy-done.11), custom_call_target="tpu_custom_call" | custom-call | bytes 12000000 | tf_op jit(solution)/shard_map/signal/pallas_call | solution.py:444
  18.5 1.0 copy-done.12
  19.5 3.3 %filter_spec.1.filter_ref = bf16[33,256,128]{2,1,0:T(8,128)(2,1)S(1)} custom-call(f32[4096,128]{1,0:T(8,128)S(1)} %copy-done.15, bf16[72,64]{1,0:T(8,128)(2,1)S(1)} %copy-done.22, bf16[33,256,256]{2,1,0:T(8,128)(2,1)S(1)} %copy-done), custom_call_target="tpu_custom_call" | custom-call | bytes 24000000 | tf_op jit(solution)/shard_map/filter_spec/pallas_call | solution.py:224
  22.7 20.8 %all-to-all-done.1.data_ref = bf16[32,136,128]{2,1,0:T(8,128)(2,1)} async-done(((bf16[32,136,128]{2,1,0:T(8,128)(2,1)}), bf16[32,136,128]{2,1,0:T(8,128)(2,1)}, u32[]{:S(2)}, u32[]{:S(2)}) %all-to-all-start.1) | async-done | bytes 1114144 | tf_op jit(solution)/shard_map/all_to_all | solution.py:491
  43.5 4.9 %all-to-all-start = ((bf16[32,136,128]{2,1,0:T(8,128)(2,1)}), bf16[32,136,128]{2,1,0:T(8,128)(2,1)}, u32[]{:S(2)}, u32[]{:S(2)}) async-start(bf16[32,136,128]{2,1,0:T(8,128)(2,1)} %copy-done.12), calls=%async_computation | async-start | bytes 2228224 | tf_op jit(solution)/shard_map/all_to_all | solution.py:491
  48.5 2.2 %copy-done.1 = bf16[33,256,256]{2,1,0:T(8,128)(2,1)S(1)} copy-done((bf16[33,256,256]{2,1,0:T(8,128)(2,1)S(1)}, bf16[33,256,256]{2,1,0:T(8,128)(2,1)}, u32[]{:S(2)}) %copy-start.1) | copy-done | bytes 4325400
  50.7 2.2 %copy-done.3 = bf16[33,256,256]{2,1,0:T(8,128)(2,1)S(1)} copy-done((bf16[33,256,256]{2,1,0:T(8,128)(2,1)S(1)}, bf16[33,256,256]{2,1,0:T(8,128)(2,1)}, u32[]{:S(2)}) %copy-start.3) | copy-done | bytes 4325400
  52.9 7.4 %signal_grad.1 = (bf16[33,256,128]{2,1,0:T(8,128)(2,1)S(1)}, bf16[32,128,128]{2,1,0:T(8,128)(2,1)S(1)}) custom-call(bf16[32,136,128]{2,1,0:T(8,128)(2,1)} %all-to-all-done.1.data_ref, f32[3,3,128]{2,1,0:T(4,128)S(1)} %constant_dynamic-slice_fusion.taps_ref, bf16[33,256,128]{2,1,0:T(8,128)(2,1)S(1)} %filter_spec.1.filter_ref, bf16[72,32]{1,0:T(8,128)(2,1)S(1)} %copy-done.20, ...), custom_call_target="tpu_custom_call" | custom-call | bytes 48000000 | tf_op jit(solution)/shard_map/signal_grad/pallas_call | solution.py:224
  60.4 1.3 copy-done.13
  61.7 1.0 copy-done.17
  62.7 15.4 %all-to-all-done.data_ref = bf16[32,136,128]{2,1,0:T(8,128)(2,1)} async-done(((bf16[32,136,128]{2,1,0:T(8,128)(2,1)}), bf16[32,136,128]{2,1,0:T(8,128)(2,1)}, u32[]{:S(2)}, u32[]{:S(2)}) %all-to-all-start) | async-done | bytes 1114144 | tf_op jit(solution)/shard_map/all_to_all | solution.py:491
  78.1 4.7 %all-to-all-start.3 = ((bf16[32,128,128]{2,1,0:T(8,128)(2,1)}), bf16[32,128,128]{2,1,0:T(8,128)(2,1)}, u32[]{:S(2)}, u32[]{:S(2)}) async-start(bf16[32,128,128]{2,1,0:T(8,128)(2,1)} %copy-done.17), calls=%async_computation.3 | async-start | bytes 2097152 | tf_op jit(solution)/shard_map/all_to_all | solution.py:491
  82.8 2.2 %copy-done.2 = bf16[33,256,256]{2,1,0:T(8,128)(2,1)S(1)} copy-done((bf16[33,256,256]{2,1,0:T(8,128)(2,1)S(1)}, bf16[33,256,256]{2,1,0:T(8,128)(2,1)}, u32[]{:S(2)}) %copy-start.2) | copy-done | bytes 4325400
  85.0 2.2 %copy-done.4 = bf16[33,256,256]{2,1,0:T(8,128)(2,1)S(1)} copy-done((bf16[33,256,256]{2,1,0:T(8,128)(2,1)S(1)}, bf16[33,256,256]{2,1,0:T(8,128)(2,1)}, u32[]{:S(2)}) %copy-start.4) | copy-done | bytes 4325400
  87.2 1.6 copy-done.14
  88.8 10.6 %conv_out.1 = (bf16[32,128,128]{2,1,0:T(8,128)(2,1)S(1)}, f32[4096,128]{1,0:T(8,128)}) custom-call(bf16[32,136,128]{2,1,0:T(8,128)(2,1)} %all-to-all-done.data_ref, f32[3,3,128]{2,1,0:T(4,128)S(1)} %constant_dynamic-slice_fusion.taps_ref, bf16[33,256,128]{2,1,0:T(8,128)(2,1)S(1)} %filter_spec.1.filter_ref, bf16[33,256,128]{2,1,0:T(8,128)(2,1)S(1)} %copy-done.14, ...), custom_call_target="tpu_custom_call" | custom-call | bytes 66000000 | tf_op jit(solution)/shard_map/conv_out/pallas_call | solution.py:224
  99.4 1.0 copy-done.16
  100.4 10.7 %all-to-all-done.3.sig_ref = bf16[32,128,128]{2,1,0:T(8,128)(2,1)} async-done(((bf16[32,128,128]{2,1,0:T(8,128)(2,1)}), bf16[32,128,128]{2,1,0:T(8,128)(2,1)}, u32[]{:S(2)}, u32[]{:S(2)}) %all-to-all-start.3) | async-done | bytes 1048608 | tf_op jit(solution)/shard_map/all_to_all | solution.py:491
  111.1 4.1 %all-to-all-start.2 = ((bf16[32,128,128]{2,1,0:T(8,128)(2,1)}), bf16[32,128,128]{2,1,0:T(8,128)(2,1)S(1)}, u32[]{:S(2)}, u32[]{:S(2)}) async-start(bf16[32,128,128]{2,1,0:T(8,128)(2,1)} %copy-done.16), calls=%async_computation.2 | async-start | bytes 2097152 | tf_op jit(solution)/shard_map/all_to_all | solution.py:491
  115.3 1.2 copy-done.9
  116.5 6.7 %input_grads.1 = (f32[4,6,1024]{2,1,0:T(8,128)S(1)}, bf16[8,4096]{1,0:T(8,128)(2,1)S(1)}, bf16[8,4096]{1,0:T(8,128)(2,1)S(1)}, bf16[128,4096]{1,0:T(8,128)(2,1)}, bf16[128,4096]{1,0:T(8,128)(2,1)}) custom-call(bf16[32,128,128]{2,1,0:T(8,128)(2,1)} %all-to-all-done.3.sig_ref, bf16[128,4096]{1,0:T(8,128)(2,1)S(1)} %copy-done.7, ...), custom_call_target="tpu_custom_call" | custom-call | bytes 18000000 | tf_op jit(solution)/shard_map/input_grads/pallas_call | solution.py:444
  123.1 0.7 copy-done.19
  123.8 0.4 collective-permute-start.1
  124.2 1.8 %collective-permute-start.2 = (f32[6,1024]{1,0:T(8,128)S(1)}, f32[6,1024]{1,0:T(8,128)S(1)}, u32[]{:S(2)}, u32[]{:S(2)}) collective-permute-start(f32[6,1024]{1,0:T(8,128)S(1)} %get-tuple-element.53), channel_id=1, source_target_pairs={{0,16},{1,17},{2,18},{3,19},{4,20},{5,21},{6,22},{7,23},{8,24},{9,... | collective-permute-start | bytes 73736 | tf_op jit(solution)/shard_map/ppermute | solution.py:477
  126.0 3.4 %collective-permute-done.2 = f32[6,1024]{1,0:T(8,128)S(1)} collective-permute-done((f32[6,1024]{1,0:T(8,128)S(1)}, f32[6,1024]{1,0:T(8,128)S(1)}, u32[]{:S(2)}, u32[]{:S(2)}) %collective-permute-start.2) | collective-permute-done | bytes 24608 | tf_op jit(solution)/shard_map/ppermute | solution.py:477
  129.4 0.8 collective-permute-done.3
  130.2 0.8 fusion.in_sums_ref
  131.0 12.6 %all-to-all-done.2.conv_ref = bf16[32,128,128]{2,1,0:T(8,128)(2,1)S(1)} async-done(((bf16[32,128,128]{2,1,0:T(8,128)(2,1)}), bf16[32,128,128]{2,1,0:T(8,128)(2,1)S(1)}, u32[]{:S(2)}, u32[]{:S(2)}) %all-to-all-start.2) | async-done | bytes 1048608 | tf_op jit(solution)/shard_map/all_to_all | solution.py:491
  143.6 1.2 copy-done.10
  144.8 1.3 output_sums.1
  146.2 0.7 copy-done.18
  146.9 0.6 copy-done.24
  147.5 4.6 %all-to-all-start.4 = ((bf16[32,40,128]{2,1,0:T(8,128)(2,1)}), bf16[32,40,128]{2,1,0:T(8,128)(2,1)}, u32[]{:S(2)}, u32[]{:S(2)}) async-start(bf16[32,40,128]{2,1,0:T(8,128)(2,1)} %copy-done.18), calls=%async_computation.4 | async-start | bytes 655360 | tf_op jit(solution)/shard_map/all_to_all | solution.py:491
  152.1 1.3 collective-permute-start.5
  153.4 1.3 collective-permute-start.4
  154.7 2.0 %mixed.1 = bf16[128,4096]{1,0:T(8,128)(2,1)} custom-call(bf16[32,128,128]{2,1,0:T(8,128)(2,1)S(1)} %all-to-all-done.2.conv_ref, bf16[128,4096]{1,0:T(8,128)(2,1)S(1)} %copy-done.5, bf16[8,4096]{1,0:T(8,128)(2,1)S(1)} %collective-permute-done.halo_ref, f32[3,3,4096]{2,1,0:T(4,128)S(1)} %copy-done.11), custom_call_target="tpu_custom_call" | custom-call | bytes 9000000 | tf_op jit(solution)/shard_map/mixed/pallas_call | solution.py:444
  156.7 1.8 %finish_input_grads.1 = (bf16[128,4096]{1,0:T(8,128)(2,1)}, bf16[128,4096]{1,0:T(8,128)(2,1)}) custom-call(bf16[128,4096]{1,0:T(8,128)(2,1)} %get-tuple-element.40.gate_ref, bf16[128,4096]{1,0:T(8,128)(2,1)} %get-tuple-element.41.value_ref, bf16[8,4096]{1,0:T(8,128)(2,1)S(1)} %collective-permute-done.5.next_ref, ...), custom_call_target="tpu_custom_call", output_to_operand_aliasing={{0}: (0, {}), {1}: (1, {})} | custom-call | bytes 6000000 | tf_op jit(solution)/shard_map/finish_input_grads/pallas_call | solution.py:444
  158.4 2.1 %output_grad.1 = bf16[128,4096]{1,0:T(8,128)(2,1)} custom-call(bf16[32,128,128]{2,1,0:T(8,128)(2,1)S(1)} %all-to-all-done.2.conv_ref, bf16[128,4096]{1,0:T(8,128)(2,1)S(1)} %copy-done.10, bf16[8,4096]{1,0:T(8,128)(2,1)S(1)} %collective-permute-done.4.next_ref, f32[3,3,4096]{2,1,0:T(4,128)S(1)} %copy-done.11), custom_call_target="tpu_custom_call" | custom-call | bytes 9000000 | tf_op jit(solution)/shard_map/output_grad/pallas_call | solution.py:444
  160.5 6.1 %all-to-all-done.4.packet_ref = bf16[32,40,128]{2,1,0:T(8,128)(2,1)} async-done(((bf16[32,40,128]{2,1,0:T(8,128)(2,1)}), bf16[32,40,128]{2,1,0:T(8,128)(2,1)}, u32[]{:S(2)}, u32[]{:S(2)}) %all-to-all-start.4) | async-done | bytes 327712 | tf_op jit(solution)/shard_map/all_to_all | solution.py:491
  166.6 1.0 packet_sums.1
  167.6 1.2 collective-permute-start.8
  168.8 0.5 collective-permute-start.7
  169.6 1.8 %collective-permute-done.8 = f32[72,128]{1,0:T(8,128)S(1)} collective-permute-done((f32[72,128]{1,0:T(8,128)S(1)}, f32[72,128]{1,0:T(8,128)S(1)}, u32[]{:S(2)}, u32[]{:S(2)}) %collective-permute-start.8) | collective-permute-done | bytes 36896 | tf_op jit(solution)/shard_map/ppermute | solution.py:477
  171.4 1.4 collective-permute-done.7
  172.8 0.7 grad_short.1
  (47 shorter events, 0.5 us)
Async XLA Ops:
  0.6 13.3 %copy-start.5 = (bf16[128,4096]{1,0:T(8,128)(2,1)S(1)}, bf16[128,4096]{1,0:T(8,128)(2,1)}, u32[]{:S(2)}) copy-start(bf16[128,4096]{1,0:T(8,128)(2,1)} %out_ref.7) | copy-start | bytes 3145732
  0.6 13.3 %copy-start.6 = (bf16[128,4096]{1,0:T(8,128)(2,1)S(1)}, bf16[128,4096]{1,0:T(8,128)(2,1)}, u32[]{:S(2)}) copy-start(bf16[128,4096]{1,0:T(8,128)(2,1)} %gate_ref.4) | copy-start | bytes 3145732
  0.7 13.2 %copy-start.8 = (bf16[128,4096]{1,0:T(8,128)(2,1)S(1)}, bf16[128,4096]{1,0:T(8,128)(2,1)}, u32[]{:S(2)}) copy-start(bf16[128,4096]{1,0:T(8,128)(2,1)} %value_ref.5) | copy-start | bytes 3145732
  3.8 12.7 %copy-start.11 = (f32[3,3,4096]{2,1,0:T(4,128)S(1)}, f32[3,3,4096]{2,1,0:T(4,128)}, u32[]{:S(2)}) copy-start(f32[3,3,4096]{2,1,0:T(4,128)} %taps_ref.11) | copy-start | bytes 442372
  3.8 39.7 %all-to-all-start.1 = ((bf16[32,136,128]{2,1,0:T(8,128)(2,1)}), bf16[32,136,128]{2,1,0:T(8,128)(2,1)}, u32[]{:S(2)}, u32[]{:S(2)}) async-start(bf16[32,136,128]{2,1,0:T(8,128)(2,1)} %outer.1), calls=%async_computation.1 | async-start | bytes 2228224 | tf_op jit(solution)/shard_map/all_to_all | solution.py:491
  13.9 5.5 %copy-start = (bf16[33,256,256]{2,1,0:T(8,128)(2,1)S(1)}, bf16[33,256,256]{2,1,0:T(8,128)(2,1)}, u32[]{:S(2)}) copy-start(bf16[33,256,256]{2,1,0:T(8,128)(2,1)} %constant.61.clone.fine_ref) | copy-start | bytes 12976132
  14.0 5.5 %copy-start.15 = (f32[4096,128]{1,0:T(8,128)S(1)}, f32[4096,128]{1,0:T(8,128)}, u32[]{:S(2)}) copy-start(f32[4096,128]{1,0:T(8,128)} %filter_ref.1) | copy-start | bytes 6291460
  14.0 5.5 %copy-start.22 = (bf16[72,64]{1,0:T(8,128)(2,1)S(1)}, bf16[72,64]{1,0:T(8,128)(2,1)}, u32[]{:S(2)}) copy-start(bf16[72,64]{1,0:T(8,128)(2,1)} %constant.60.clone.twice_ref) | copy-start | bytes 27652
  14.0 8.7 %collective-permute-start = (bf16[8,4096]{1,0:T(8,128)(2,1)S(1)}, bf16[8,4096]{1,0:T(8,128)(2,1)S(1)}, u32[]{:S(2)}, u32[]{:S(2)}) collective-permute-start(bf16[8,4096]{1,0:T(8,128)(2,1)S(1)} %edges.1), channel_id=1, source_target_pairs={{0,1},{1,2},{2,3},{3,4},{4,5},{5,6},{6,7},{7,8},{8,9},{9,10},{10,1... | collective-permute-start | bytes 196616 | tf_op jit(solution)/shard_map/ppermute | solution.py:519
  18.5 1.0 copy-start.12
  22.7 25.7 %copy-start.20 = (bf16[72,32]{1,0:T(8,128)(2,1)S(1)}, bf16[72,32]{1,0:T(8,128)(2,1)}, u32[]{:S(2)}) copy-start(bf16[72,32]{1,0:T(8,128)(2,1)} %constant.59.clone.coarse_ref) | copy-start | bytes 13828
  22.7 25.7 %copy-start.21 = (bf16[32,72]{1,0:T(8,128)(2,1)S(1)}, bf16[32,72]{1,0:T(8,128)(2,1)}, u32[]{:S(2)}) copy-start(bf16[32,72]{1,0:T(8,128)(2,1)} %constant.63.clone.back_ref) | copy-start | bytes 13828
  43.5 34.6 %all-to-all-start = ((bf16[32,136,128]{2,1,0:T(8,128)(2,1)}), bf16[32,136,128]{2,1,0:T(8,128)(2,1)}, u32[]{:S(2)}, u32[]{:S(2)}) async-start(bf16[32,136,128]{2,1,0:T(8,128)(2,1)} %copy-done.12), calls=%async_computation | async-start | bytes 2228224 | tf_op jit(solution)/shard_map/all_to_all | solution.py:491
  48.5 2.2 %copy-start.1 = (bf16[33,256,256]{2,1,0:T(8,128)(2,1)S(1)}, bf16[33,256,256]{2,1,0:T(8,128)(2,1)}, u32[]{:S(2)}) copy-start(bf16[33,256,256]{2,1,0:T(8,128)(2,1)} %constant.61.clone.fine_ref) | copy-start | bytes 12976132
  50.7 2.2 %copy-start.3 = (bf16[33,256,256]{2,1,0:T(8,128)(2,1)S(1)}, bf16[33,256,256]{2,1,0:T(8,128)(2,1)}, u32[]{:S(2)}) copy-start(bf16[33,256,256]{2,1,0:T(8,128)(2,1)} %constant.62.clone.inv_ref) | copy-start | bytes 12976132
  60.4 1.4 copy-start.13
  61.7 1.0 copy-start.17
  78.1 33.0 %all-to-all-start.3 = ((bf16[32,128,128]{2,1,0:T(8,128)(2,1)}), bf16[32,128,128]{2,1,0:T(8,128)(2,1)}, u32[]{:S(2)}, u32[]{:S(2)}) async-start(bf16[32,128,128]{2,1,0:T(8,128)(2,1)} %copy-done.17), calls=%async_computation.3 | async-start | bytes 2097152 | tf_op jit(solution)/shard_map/all_to_all | solution.py:491
  82.8 2.2 %copy-start.2 = (bf16[33,256,256]{2,1,0:T(8,128)(2,1)S(1)}, bf16[33,256,256]{2,1,0:T(8,128)(2,1)}, u32[]{:S(2)}) copy-start(bf16[33,256,256]{2,1,0:T(8,128)(2,1)} %constant.61.clone.fine_ref) | copy-start | bytes 12976132
  85.0 2.2 %copy-start.4 = (bf16[33,256,256]{2,1,0:T(8,128)(2,1)S(1)}, bf16[33,256,256]{2,1,0:T(8,128)(2,1)}, u32[]{:S(2)}) copy-start(bf16[33,256,256]{2,1,0:T(8,128)(2,1)} %constant.62.clone.inv_ref) | copy-start | bytes 12976132
  87.2 1.6 copy-start.14
  99.4 1.0 copy-start.16
  100.4 14.9 %copy-start.7 = (bf16[128,4096]{1,0:T(8,128)(2,1)S(1)}, bf16[128,4096]{1,0:T(8,128)(2,1)}, u32[]{:S(2)}) copy-start(bf16[128,4096]{1,0:T(8,128)(2,1)} %gate_ref.4) | copy-start | bytes 3145732
  111.1 32.5 %all-to-all-start.2 = ((bf16[32,128,128]{2,1,0:T(8,128)(2,1)}), bf16[32,128,128]{2,1,0:T(8,128)(2,1)S(1)}, u32[]{:S(2)}, u32[]{:S(2)}) async-start(bf16[32,128,128]{2,1,0:T(8,128)(2,1)} %copy-done.16), calls=%async_computation.2 | async-start | bytes 2097152 | tf_op jit(solution)/shard_map/all_to_all | solution.py:491
  115.3 1.2 copy-start.9
  123.1 0.7 copy-start.19
  123.1 6.2 %copy-start.23 = (bf16[8,4096]{1,0:T(8,128)(2,1)}, bf16[8,4096]{1,0:T(8,128)(2,1)S(1)}, u32[]{:S(2)}) copy-start(bf16[8,4096]{1,0:T(8,128)(2,1)S(1)} %get-tuple-element.42) | copy-start | bytes 196612
  123.8 2.2 %collective-permute-start.1 = (f32[6,1024]{1,0:T(8,128)S(1)}, f32[6,1024]{1,0:T(8,128)S(1)}, u32[]{:S(2)}, u32[]{:S(2)}) collective-permute-start(f32[6,1024]{1,0:T(8,128)S(1)} %get-tuple-element.54), channel_id=1, source_target_pairs={{0,1},{1,0},{2,3},{3,2},{4,5},{5,4},{6,7},{7,6},{8,9},{9,8},{10,11... | collective-permute-start | bytes 73736 | tf_op jit(solution)/shard_map/ppermute | solution.py:477
  124.2 5.2 %collective-permute-start.2 = (f32[6,1024]{1,0:T(8,128)S(1)}, f32[6,1024]{1,0:T(8,128)S(1)}, u32[]{:S(2)}, u32[]{:S(2)}) collective-permute-start(f32[6,1024]{1,0:T(8,128)S(1)} %get-tuple-element.53), channel_id=1, source_target_pairs={{0,16},{1,17},{2,18},{3,19},{4,20},{5,21},{6,22},{7,23},{8,24},{9,... | collective-permute-start | bytes 73736 | tf_op jit(solution)/shard_map/ppermute | solution.py:477
  126.0 4.3 %collective-permute-start.3 = (f32[6,1024]{1,0:T(8,128)S(1)}, f32[6,1024]{1,0:T(8,128)S(1)}, u32[]{:S(2)}, u32[]{:S(2)}) collective-permute-start(f32[6,1024]{1,0:T(8,128)S(1)} %get-tuple-element.52), channel_id=1, source_target_pairs={{0,17},{1,16},{2,19},{3,18},{4,21},{5,20},{6,23},{7,22},{8,25},{9,... | collective-permute-start | bytes 73736 | tf_op jit(solution)/shard_map/ppermute | solution.py:477
  143.6 1.2 copy-start.10
  146.1 0.7 copy-start.18
  146.9 0.6 copy-start.24
  147.5 19.1 %all-to-all-start.4 = ((bf16[32,40,128]{2,1,0:T(8,128)(2,1)}), bf16[32,40,128]{2,1,0:T(8,128)(2,1)}, u32[]{:S(2)}, u32[]{:S(2)}) async-start(bf16[32,40,128]{2,1,0:T(8,128)(2,1)} %copy-done.18), calls=%async_computation.4 | async-start | bytes 655360 | tf_op jit(solution)/shard_map/all_to_all | solution.py:491
  152.1 4.6 %collective-permute-start.5 = (bf16[8,4096]{1,0:T(8,128)(2,1)}, bf16[8,4096]{1,0:T(8,128)(2,1)S(1)}, u32[]{:S(2)}, u32[]{:S(2)}) collective-permute-start(bf16[8,4096]{1,0:T(8,128)(2,1)} %copy-done.23), channel_id=1, source_target_pairs={{1,0},{2,1},{3,2},{4,3},{5,4},{6,5},{7,6},{8,7},{9,8},{10,9},{11,1... | collective-permute-start | bytes 196616 | tf_op jit(solution)/shard_map/ppermute | solution.py:559
  153.4 5.1 %collective-permute-start.4 = (bf16[8,4096]{1,0:T(8,128)(2,1)}, bf16[8,4096]{1,0:T(8,128)(2,1)S(1)}, u32[]{:S(2)}, u32[]{:S(2)}) collective-permute-start(bf16[8,4096]{1,0:T(8,128)(2,1)} %copy-done.24), channel_id=1, source_target_pairs={{1,0},{2,1},{3,2},{4,3},{5,4},{6,5},{7,6},{8,7},{9,8},{10,9},{11,1... | collective-permute-start | bytes 196616 | tf_op jit(solution)/shard_map/ppermute | solution.py:569
  167.6 3.8 %collective-permute-start.8 = (f32[72,128]{1,0:T(8,128)S(1)}, f32[72,128]{1,0:T(8,128)S(1)}, u32[]{:S(2)}, u32[]{:S(2)}) collective-permute-start(f32[72,128]{1,0:T(8,128)S(1)} %packet_sums.1), channel_id=1, source_target_pairs={{0,17},{1,16},{2,19},{3,18},{4,21},{5,20},{6,23},{7,22},{8,25},{9,... | collective-permute-start | bytes 110600 | tf_op jit(solution)/shard_map/ppermute | solution.py:477
  168.8 4.0 %collective-permute-start.7 = (f32[72,128]{1,0:T(8,128)S(1)}, f32[72,128]{1,0:T(8,128)S(1)}, u32[]{:S(2)}, u32[]{:S(2)}) collective-permute-start(f32[72,128]{1,0:T(8,128)S(1)} %packet_sums.1), channel_id=1, source_target_pairs={{0,16},{1,17},{2,18},{3,19},{4,20},{5,21},{6,22},{7,23},{8,24},{9,... | collective-permute-start | bytes 110600 | tf_op jit(solution)/shard_map/ppermute | solution.py:477
  169.3 3.5 %collective-permute-start.6 = (f32[72,128]{1,0:T(8,128)S(1)}, f32[72,128]{1,0:T(8,128)S(1)}, u32[]{:S(2)}, u32[]{:S(2)}) collective-permute-start(f32[72,128]{1,0:T(8,128)S(1)} %packet_sums.1), channel_id=1, source_target_pairs={{0,1},{1,0},{2,3},{3,2},{4,5},{5,4},{6,7},{7,6},{8,9},{9,8},{10,11... | collective-permute-start | bytes 110600 | tf_op jit(solution)/shard_map/ppermute | solution.py:477

commit v6 on v5

--- a/solution.py
+++ b/solution.py
@@ -353,13 +353,12 @@
         new_ref[...] = new.astype(bf16)
 
 
-def output_sums_kernel(conv_ref, out_ref, cot_ref, halo_ref, in_sums_ref, packet_ref, head_ref):
+def output_sums_kernel(conv_ref, out_ref, cot_ref, halo_ref, in_sums_ref, packet_ref):
     before = halo_ref[...].astype(f32)[4:6]
     out_grad = (cot_ref[...].astype(f32) * inward(conv_ref)).astype(bf16).astype(f32)
     rows = out_ref[...].astype(f32)
     lags = (rows, delayed(rows, before, 1), delayed(rows, before, 2))
     sums, ins = jnp.concatenate(lag_sums(out_grad, lags), axis=0), in_sums_ref[...]
-    head_ref[...] = collect([out_grad[0:2]], 8, bf16)
     count, pack, width = packet_ref.shape
     quarter = sums.shape[1] // 4
     part = quarter // 4
@@ -405,9 +404,11 @@
                 short_ref[2, :, start : start + width] = held[out_row : out_row + 3]
 
 
-def mixed_kernel(conv_ref, out_ref, halo_ref, taps_ref, mixed_ref):
+def mixed_kernel(conv_ref, out_ref, cot_first, halo_ref, taps_ref, mixed_ref, head_ref):
     feat_out, _ = feature(out_ref[...], halo_ref[...].astype(f32), 2, taps_ref)
-    mixed_ref[...] = (feat_out * inward(conv_ref)).astype(bf16)
+    conv = inward(conv_ref)
+    mixed_ref[...] = (feat_out * conv).astype(bf16)
+    head_ref[...] = collect([cot_first[...].astype(f32)[0:2] * conv[0:2]], 8, bf16)
 
 
 def output_grad_kernel(conv_ref, cot_ref, next_ref, taps_ref, grad_ref):
@@ -429,6 +430,7 @@
             "taps": pl.BlockSpec((3, 3, tile), lambda i: (0, 0, i)),
             "packet": pl.BlockSpec((z.blocks, z.pack, z.width), lambda i: (0, 0, 0)),
             "longer": pl.BlockSpec((tile // z.width, z.pitch, z.width), lambda i: (i, 0, 0)),
+            "first": pl.BlockSpec((16, tile), lambda i: (0, i)),
             "last": pl.BlockSpec((16, tile), lambda i: (z.rows // 16 - 1, i)),
         }[kind]
 
@@ -557,25 +559,25 @@
     near = Near(size)
     in_sums = near.scatter(in_sums)
     in_after = lax.ppermute(in_head, "seq", backward)
-    packets, out_head = position(
+    (packets,) = position(
         output_sums_kernel,
         (conv_rows, gate_out, cotangent, halo, in_sums),
         ("moved", "rows", "rows", "edge", "near"),
-        ("packet", "edge"),
+        ("packet",),
         "output_sums",
         3,
         tile=channels,
     )
-    after = lax.ppermute(out_head, "seq", backward)
     packets = exchange(packets)
-    (mixed,) = position(
+    mixed, out_head = position(
         mixed_kernel,
-        (conv_rows, gate_out, halo, short_filters),
-        ("moved", "rows", "edge", "taps"),
-        ("rows",),
+        (conv_rows, gate_out, cotangent, halo, short_filters),
+        ("moved", "rows", "first", "edge", "taps"),
+        ("rows", "edge"),
         "mixed",
         3,
     )
+    after = lax.ppermute(out_head, "seq", backward)
     (grad_out,) = position(
         output_grad_kernel,
         (conv_rows, cotangent, after, short_filters),

time: 175 us -> 173 us (0.989)
    all_to_all x5, waiting for transfers between devices: 65.6 us -> 63.6 us  [exchange(): return lax.all_to_all(value, 'seq', split_axis=0, concat_axis=0, tiled=True)]
    unnamed x50 -> x48, local copies, waits for them, and re-layouts: 19.3 us -> 18.7 us
  transfers between devices with their start and end apart: 14 -> 14, of which waited for: 9 -> 10; matrix products, arithmetic and copies ran while one was open for 0% -> 1% of each run, Pallas kernels for 21% -> 21%
where the time goes in v6:
time: 173 us; the launch traced here: 172 us
  waiting for transfers between devices  71.4 us (41%)
  Pallas kernels  42.1 us (24%)
  starting transfers between devices  37.3 us (22%)
  local copies, waits for them, and re-layouts  19.4 us (11%)
    all_to_all x5, waiting for transfers between devices, exchange(): return lax.all_to_all(value, 'seq', split_axis=0, concat_axis=0, tiled=True)  63.6 us
    all_to_all x5, starting transfers between devices, exchange(): return lax.all_to_all(value, 'seq', split_axis=0, concat_axis=0, tiled=True)  28.3 us
    pallas_call x3, Pallas kernels, channel_call(): pl.pallas_call(kernel, out_shape=outs, in_specs=[whole] * len(operands),...  21.2 us
    pallas_call x8, Pallas kernels, position_call(): pl.pallas_call(kernel, grid=(channels // tile,), out_shape=[shapes[k] for...  19.2 us
    unnamed x48, local copies, waits for them, and re-layouts  18.7 us
    ppermute x6, waiting for transfers between devices, swap(): return lax.ppermute(value, 'seq', [(i, i ^ bits) for i in range(self.size)])  7.05 us
    ppermute x6, starting transfers between devices, swap(): return lax.ppermute(value, 'seq', [(i, i ^ bits) for i in range(self.size)])  3.92 us
  transfers between devices with their start and end apart: 14, of which 10 were waited for; matrix products, arithmetic and copies ran while one was open for 1% of the time, Pallas kernels for 21%

profile of v6, /device:TPU:8, one launch (start us, length us, event | category | flops | bytes accessed | tf_op | source)
XLA Modules:
  0.0 172.0 jit_solution(15608718272839679450)
XLA Ops:
  0.7 3.2 %outer.1 = bf16[32,136,128]{2,1,0:T(8,128)(2,1)} custom-call(bf16[128,4096]{1,0:T(8,128)(2,1)} %out_ref.7, bf16[128,4096]{1,0:T(8,128)(2,1)} %cot_ref.5, f32[3,3,4096]{2,1,0:T(4,128)} %taps_ref.11), custom_call_target="tpu_custom_call" | custom-call | bytes 12000000 | tf_op jit(solution)/shard_map/outer/pallas_call | solution.py:446
  3.9 10.0 %all-to-all-start.1 = ((bf16[32,136,128]{2,1,0:T(8,128)(2,1)}), bf16[32,136,128]{2,1,0:T(8,128)(2,1)}, u32[]{:S(2)}, u32[]{:S(2)}) async-start(bf16[32,136,128]{2,1,0:T(8,128)(2,1)} %outer.1), calls=%async_computation.1 | async-start | bytes 2228224 | tf_op jit(solution)/shard_map/all_to_all | solution.py:493
  14.0 2.5 %collective-permute-start = (bf16[8,4096]{1,0:T(8,128)(2,1)S(1)}, bf16[8,4096]{1,0:T(8,128)(2,1)S(1)}, u32[]{:S(2)}, u32[]{:S(2)}) collective-permute-start(bf16[8,4096]{1,0:T(8,128)(2,1)S(1)} %edges.1), channel_id=1, source_target_pairs={{0,1},{1,2},{2,3},{3,4},{4,5},{5,6},{6,7},{7,8},{8,9},{9,10},{10,1... | collective-permute-start | bytes 196616 | tf_op jit(solution)/shard_map/ppermute | solution.py:521
  16.5 1.9 %signal.1 = bf16[32,136,128]{2,1,0:T(8,128)(2,1)S(1)} custom-call(bf16[128,4096]{1,0:T(8,128)(2,1)S(1)} %copy-done.7, bf16[128,4096]{1,0:T(8,128)(2,1)S(1)} %copy-done.9, f32[3,3,4096]{2,1,0:T(4,128)S(1)} %copy-done.11), custom_call_target="tpu_custom_call" | custom-call | bytes 12000000 | tf_op jit(solution)/shard_map/signal/pallas_call | solution.py:446
  18.5 1.0 copy-done.12
  19.5 3.2 %filter_spec.1.filter_ref = bf16[33,256,128]{2,1,0:T(8,128)(2,1)S(1)} custom-call(f32[4096,128]{1,0:T(8,128)S(1)} %copy-done.15, bf16[72,64]{1,0:T(8,128)(2,1)S(1)} %copy-done.22, bf16[33,256,256]{2,1,0:T(8,128)(2,1)S(1)} %copy-done), custom_call_target="tpu_custom_call" | custom-call | bytes 24000000 | tf_op jit(solution)/shard_map/filter_spec/pallas_call | solution.py:224
  22.7 20.8 %all-to-all-done.1.data_ref = bf16[32,136,128]{2,1,0:T(8,128)(2,1)} async-done(((bf16[32,136,128]{2,1,0:T(8,128)(2,1)}), bf16[32,136,128]{2,1,0:T(8,128)(2,1)}, u32[]{:S(2)}, u32[]{:S(2)}) %all-to-all-start.1) | async-done | bytes 1114144 | tf_op jit(solution)/shard_map/all_to_all | solution.py:493
  43.5 4.9 %all-to-all-start = ((bf16[32,136,128]{2,1,0:T(8,128)(2,1)}), bf16[32,136,128]{2,1,0:T(8,128)(2,1)}, u32[]{:S(2)}, u32[]{:S(2)}) async-start(bf16[32,136,128]{2,1,0:T(8,128)(2,1)} %copy-done.12), calls=%async_computation | async-start | bytes 2228224 | tf_op jit(solution)/shard_map/all_to_all | solution.py:493
  48.5 2.2 %copy-done.1 = bf16[33,256,256]{2,1,0:T(8,128)(2,1)S(1)} copy-done((bf16[33,256,256]{2,1,0:T(8,128)(2,1)S(1)}, bf16[33,256,256]{2,1,0:T(8,128)(2,1)}, u32[]{:S(2)}) %copy-start.1) | copy-done | bytes 4325400
  50.7 2.2 %copy-done.3 = bf16[33,256,256]{2,1,0:T(8,128)(2,1)S(1)} copy-done((bf16[33,256,256]{2,1,0:T(8,128)(2,1)S(1)}, bf16[33,256,256]{2,1,0:T(8,128)(2,1)}, u32[]{:S(2)}) %copy-start.3) | copy-done | bytes 4325400
  52.9 7.4 %signal_grad.1 = (bf16[33,256,128]{2,1,0:T(8,128)(2,1)S(1)}, bf16[32,128,128]{2,1,0:T(8,128)(2,1)S(1)}) custom-call(bf16[32,136,128]{2,1,0:T(8,128)(2,1)} %all-to-all-done.1.data_ref, f32[3,3,128]{2,1,0:T(4,128)S(1)} %constant_dynamic-slice_fusion.taps_ref, bf16[33,256,128]{2,1,0:T(8,128)(2,1)S(1)} %filter_spec.1.filter_ref, bf16[72,32]{1,0:T(8,128)(2,1)S(1)} %copy-done.20, ...), custom_call_target="tpu_custom_call" | custom-call | bytes 48000000 | tf_op jit(solution)/shard_map/signal_grad/pallas_call | solution.py:224
  60.4 1.3 copy-done.13
  61.7 1.0 copy-done.18
  62.7 15.4 %all-to-all-done.data_ref = bf16[32,136,128]{2,1,0:T(8,128)(2,1)} async-done(((bf16[32,136,128]{2,1,0:T(8,128)(2,1)}), bf16[32,136,128]{2,1,0:T(8,128)(2,1)}, u32[]{:S(2)}, u32[]{:S(2)}) %all-to-all-start) | async-done | bytes 1114144 | tf_op jit(solution)/shard_map/all_to_all | solution.py:493
  78.1 4.7 %all-to-all-start.3 = ((bf16[32,128,128]{2,1,0:T(8,128)(2,1)}), bf16[32,128,128]{2,1,0:T(8,128)(2,1)}, u32[]{:S(2)}, u32[]{:S(2)}) async-start(bf16[32,128,128]{2,1,0:T(8,128)(2,1)} %copy-done.18), calls=%async_computation.3 | async-start | bytes 2097152 | tf_op jit(solution)/shard_map/all_to_all | solution.py:493
  82.8 2.2 %copy-done.2 = bf16[33,256,256]{2,1,0:T(8,128)(2,1)S(1)} copy-done((bf16[33,256,256]{2,1,0:T(8,128)(2,1)S(1)}, bf16[33,256,256]{2,1,0:T(8,128)(2,1)}, u32[]{:S(2)}) %copy-start.2) | copy-done | bytes 4325400
  85.0 2.2 %copy-done.4 = bf16[33,256,256]{2,1,0:T(8,128)(2,1)S(1)} copy-done((bf16[33,256,256]{2,1,0:T(8,128)(2,1)S(1)}, bf16[33,256,256]{2,1,0:T(8,128)(2,1)}, u32[]{:S(2)}) %copy-start.4) | copy-done | bytes 4325400
  87.3 1.6 copy-done.14
  88.9 10.5 %conv_out.1 = (bf16[32,128,128]{2,1,0:T(8,128)(2,1)S(1)}, f32[4096,128]{1,0:T(8,128)}) custom-call(bf16[32,136,128]{2,1,0:T(8,128)(2,1)} %all-to-all-done.data_ref, f32[3,3,128]{2,1,0:T(4,128)S(1)} %constant_dynamic-slice_fusion.taps_ref, bf16[33,256,128]{2,1,0:T(8,128)(2,1)S(1)} %filter_spec.1.filter_ref, bf16[33,256,128]{2,1,0:T(8,128)(2,1)S(1)} %copy-done.14, ...), custom_call_target="tpu_custom_call" | custom-call | bytes 66000000 | tf_op jit(solution)/shard_map/conv_out/pallas_call | solution.py:224
  99.4 1.0 copy-done.17
  100.3 10.8 %all-to-all-done.3.sig_ref = bf16[32,128,128]{2,1,0:T(8,128)(2,1)} async-done(((bf16[32,128,128]{2,1,0:T(8,128)(2,1)}), bf16[32,128,128]{2,1,0:T(8,128)(2,1)}, u32[]{:S(2)}, u32[]{:S(2)}) %all-to-all-start.3) | async-done | bytes 1048608 | tf_op jit(solution)/shard_map/all_to_all | solution.py:493
  111.1 4.1 %all-to-all-start.2 = ((bf16[32,128,128]{2,1,0:T(8,128)(2,1)}), bf16[32,128,128]{2,1,0:T(8,128)(2,1)S(1)}, u32[]{:S(2)}, u32[]{:S(2)}) async-start(bf16[32,128,128]{2,1,0:T(8,128)(2,1)} %copy-done.17), calls=%async_computation.2 | async-start | bytes 2097152 | tf_op jit(solution)/shard_map/all_to_all | solution.py:493
  115.3 1.3 copy-done.8
  116.6 1.2 copy-done.10
  117.8 6.7 %input_grads.1 = (f32[4,6,1024]{2,1,0:T(8,128)S(1)}, bf16[8,4096]{1,0:T(8,128)(2,1)S(1)}, bf16[8,4096]{1,0:T(8,128)(2,1)S(1)}, bf16[128,4096]{1,0:T(8,128)(2,1)}, bf16[128,4096]{1,0:T(8,128)(2,1)}) custom-call(bf16[32,128,128]{2,1,0:T(8,128)(2,1)} %all-to-all-done.3.sig_ref, bf16[128,4096]{1,0:T(8,128)(2,1)S(1)} %copy-done.8, ...), custom_call_target="tpu_custom_call" | custom-call | bytes 18000000 | tf_op jit(solution)/shard_map/input_grads/pallas_call | solution.py:446
  124.5 0.7 copy-done.19
  125.1 0.6 dynamic-slice_bitcast_fusion
  126.0 1.7 collective-permute-start.2
  127.7 2.6 %collective-permute-done.2 = f32[6,1024]{1,0:T(8,128)} collective-permute-done((f32[6,1024]{1,0:T(8,128)}, f32[6,1024]{1,0:T(8,128)}, u32[]{:S(2)}, u32[]{:S(2)}) %collective-permute-start.2) | collective-permute-done | bytes 24608 | tf_op jit(solution)/shard_map/ppermute | solution.py:479
  130.3 1.3 collective-permute-done.3
  131.6 0.8 fusion.in_sums_ref
  132.4 11.2 %all-to-all-done.2.conv_ref = bf16[32,128,128]{2,1,0:T(8,128)(2,1)S(1)} async-done(((bf16[32,128,128]{2,1,0:T(8,128)(2,1)}), bf16[32,128,128]{2,1,0:T(8,128)(2,1)S(1)}, u32[]{:S(2)}, u32[]{:S(2)}) %all-to-all-start.2) | async-done | bytes 1048608 | tf_op jit(solution)/shard_map/all_to_all | solution.py:493
  143.6 1.6 output_sums.1
  145.2 0.7 copy-done.16
  145.9 4.6 %all-to-all-start.4 = ((bf16[32,40,128]{2,1,0:T(8,128)(2,1)}), bf16[32,40,128]{2,1,0:T(8,128)(2,1)}, u32[]{:S(2)}, u32[]{:S(2)}) async-start(bf16[32,40,128]{2,1,0:T(8,128)(2,1)} %copy-done.16), calls=%async_computation.4 | async-start | bytes 655360 | tf_op jit(solution)/shard_map/all_to_all | solution.py:493
  150.5 1.3 collective-permute-start.5
  151.8 2.0 %mixed.1 = (bf16[128,4096]{1,0:T(8,128)(2,1)}, bf16[8,4096]{1,0:T(8,128)(2,1)S(1)}) custom-call(bf16[32,128,128]{2,1,0:T(8,128)(2,1)S(1)} %all-to-all-done.2.conv_ref, bf16[128,4096]{1,0:T(8,128)(2,1)S(1)} %copy-done.5, bf16[128,4096]{1,0:T(8,128)(2,1)S(1)} %copy-done.6, bf16[8,4096]{1,0:T(8,128)(2,1)S(1)} %collective-permute-done.halo_ref, ...), custom_call_target="tpu_custom_call" | custom-call | bytes 9000000 | tf_op jit(solution)/shard_map/mixed/pallas_call | solution.py:446
  153.8 1.3 collective-permute-start.4
  155.1 1.8 %finish_input_grads.1 = (bf16[128,4096]{1,0:T(8,128)(2,1)}, bf16[128,4096]{1,0:T(8,128)(2,1)}) custom-call(bf16[128,4096]{1,0:T(8,128)(2,1)} %get-tuple-element.40.gate_ref, bf16[128,4096]{1,0:T(8,128)(2,1)} %get-tuple-element.41.value_ref, bf16[8,4096]{1,0:T(8,128)(2,1)S(1)} %collective-permute-done.5.next_ref, ...), custom_call_target="tpu_custom_call", output_to_operand_aliasing={{0}: (0, {}), {1}: (1, {})} | custom-call | bytes 6000000 | tf_op jit(solution)/shard_map/finish_input_grads/pallas_call | solution.py:446
  156.9 0.7 collective-permute-done.4.next_ref
  157.6 2.1 %output_grad.1 = bf16[128,4096]{1,0:T(8,128)(2,1)} custom-call(bf16[32,128,128]{2,1,0:T(8,128)(2,1)S(1)} %all-to-all-done.2.conv_ref, bf16[128,4096]{1,0:T(8,128)(2,1)S(1)} %copy-done.6, bf16[8,4096]{1,0:T(8,128)(2,1)S(1)} %collective-permute-done.4.next_ref, f32[3,3,4096]{2,1,0:T(4,128)S(1)} %copy-done.11), custom_call_target="tpu_custom_call" | custom-call | bytes 9000000 | tf_op jit(solution)/shard_map/output_grad/pallas_call | solution.py:446
  159.6 5.4 %all-to-all-done.4.packet_ref = bf16[32,40,128]{2,1,0:T(8,128)(2,1)} async-done(((bf16[32,40,128]{2,1,0:T(8,128)(2,1)}), bf16[32,40,128]{2,1,0:T(8,128)(2,1)}, u32[]{:S(2)}, u32[]{:S(2)}) %all-to-all-start.4) | async-done | bytes 327712 | tf_op jit(solution)/shard_map/all_to_all | solution.py:493
  165.0 1.0 packet_sums.1
  166.1 1.2 collective-permute-start.8
  167.2 0.5 collective-permute-start.7
  168.0 1.8 %collective-permute-done.8 = f32[72,128]{1,0:T(8,128)S(1)} collective-permute-done((f32[72,128]{1,0:T(8,128)S(1)}, f32[72,128]{1,0:T(8,128)S(1)}, u32[]{:S(2)}, u32[]{:S(2)}) %collective-permute-start.8) | collective-permute-done | bytes 36896 | tf_op jit(solution)/shard_map/ppermute | solution.py:479
  169.8 1.4 collective-permute-done.7
  171.2 0.7 grad_short.1
  (45 shorter events, 0.8 us)
Async XLA Ops:
  0.6 13.3 %copy-start.5 = (bf16[128,4096]{1,0:T(8,128)(2,1)S(1)}, bf16[128,4096]{1,0:T(8,128)(2,1)}, u32[]{:S(2)}) copy-start(bf16[128,4096]{1,0:T(8,128)(2,1)} %out_ref.7) | copy-start | bytes 3145732
  0.6 13.3 %copy-start.7 = (bf16[128,4096]{1,0:T(8,128)(2,1)S(1)}, bf16[128,4096]{1,0:T(8,128)(2,1)}, u32[]{:S(2)}) copy-start(bf16[128,4096]{1,0:T(8,128)(2,1)} %gate_ref.4) | copy-start | bytes 3145732
  0.7 13.3 %copy-start.9 = (bf16[128,4096]{1,0:T(8,128)(2,1)S(1)}, bf16[128,4096]{1,0:T(8,128)(2,1)}, u32[]{:S(2)}) copy-start(bf16[128,4096]{1,0:T(8,128)(2,1)} %value_ref.5) | copy-start | bytes 3145732
  3.8 12.7 %copy-start.11 = (f32[3,3,4096]{2,1,0:T(4,128)S(1)}, f32[3,3,4096]{2,1,0:T(4,128)}, u32[]{:S(2)}) copy-start(f32[3,3,4096]{2,1,0:T(4,128)} %taps_ref.11) | copy-start | bytes 442372
  3.9 39.7 %all-to-all-start.1 = ((bf16[32,136,128]{2,1,0:T(8,128)(2,1)}), bf16[32,136,128]{2,1,0:T(8,128)(2,1)}, u32[]{:S(2)}, u32[]{:S(2)}) async-start(bf16[32,136,128]{2,1,0:T(8,128)(2,1)} %outer.1), calls=%async_computation.1 | async-start | bytes 2228224 | tf_op jit(solution)/shard_map/all_to_all | solution.py:493
  13.9 5.5 %copy-start = (bf16[33,256,256]{2,1,0:T(8,128)(2,1)S(1)}, bf16[33,256,256]{2,1,0:T(8,128)(2,1)}, u32[]{:S(2)}) copy-start(bf16[33,256,256]{2,1,0:T(8,128)(2,1)} %constant.61.clone.fine_ref) | copy-start | bytes 12976132
  14.0 5.5 %copy-start.15 = (f32[4096,128]{1,0:T(8,128)S(1)}, f32[4096,128]{1,0:T(8,128)}, u32[]{:S(2)}) copy-start(f32[4096,128]{1,0:T(8,128)} %filter_ref.1) | copy-start | bytes 6291460
  14.0 5.5 %copy-start.22 = (bf16[72,64]{1,0:T(8,128)(2,1)S(1)}, bf16[72,64]{1,0:T(8,128)(2,1)}, u32[]{:S(2)}) copy-start(bf16[72,64]{1,0:T(8,128)(2,1)} %constant.60.clone.twice_ref) | copy-start | bytes 27652
  14.0 8.7 %collective-permute-start = (bf16[8,4096]{1,0:T(8,128)(2,1)S(1)}, bf16[8,4096]{1,0:T(8,128)(2,1)S(1)}, u32[]{:S(2)}, u32[]{:S(2)}) collective-permute-start(bf16[8,4096]{1,0:T(8,128)(2,1)S(1)} %edges.1), channel_id=1, source_target_pairs={{0,1},{1,2},{2,3},{3,4},{4,5},{5,6},{6,7},{7,8},{8,9},{9,10},{10,1... | collective-permute-start | bytes 196616 | tf_op jit(solution)/shard_map/ppermute | solution.py:521
  18.5 1.0 copy-start.12
  22.7 25.8 %copy-start.20 = (bf16[72,32]{1,0:T(8,128)(2,1)S(1)}, bf16[72,32]{1,0:T(8,128)(2,1)}, u32[]{:S(2)}) copy-start(bf16[72,32]{1,0:T(8,128)(2,1)} %constant.59.clone.coarse_ref) | copy-start | bytes 13828
  22.7 25.8 %copy-start.21 = (bf16[32,72]{1,0:T(8,128)(2,1)S(1)}, bf16[32,72]{1,0:T(8,128)(2,1)}, u32[]{:S(2)}) copy-start(bf16[32,72]{1,0:T(8,128)(2,1)} %constant.63.clone.back_ref) | copy-start | bytes 13828
  43.5 34.6 %all-to-all-start = ((bf16[32,136,128]{2,1,0:T(8,128)(2,1)}), bf16[32,136,128]{2,1,0:T(8,128)(2,1)}, u32[]{:S(2)}, u32[]{:S(2)}) async-start(bf16[32,136,128]{2,1,0:T(8,128)(2,1)} %copy-done.12), calls=%async_computation | async-start | bytes 2228224 | tf_op jit(solution)/shard_map/all_to_all | solution.py:493
  48.5 2.2 %copy-start.1 = (bf16[33,256,256]{2,1,0:T(8,128)(2,1)S(1)}, bf16[33,256,256]{2,1,0:T(8,128)(2,1)}, u32[]{:S(2)}) copy-start(bf16[33,256,256]{2,1,0:T(8,128)(2,1)} %constant.61.clone.fine_ref) | copy-start | bytes 12976132
  50.7 2.2 %copy-start.3 = (bf16[33,256,256]{2,1,0:T(8,128)(2,1)S(1)}, bf16[33,256,256]{2,1,0:T(8,128)(2,1)}, u32[]{:S(2)}) copy-start(bf16[33,256,256]{2,1,0:T(8,128)(2,1)} %constant.62.clone.inv_ref) | copy-start | bytes 12976132
  60.4 1.4 copy-start.13
  61.7 1.0 copy-start.18
  78.1 33.0 %all-to-all-start.3 = ((bf16[32,128,128]{2,1,0:T(8,128)(2,1)}), bf16[32,128,128]{2,1,0:T(8,128)(2,1)}, u32[]{:S(2)}, u32[]{:S(2)}) async-start(bf16[32,128,128]{2,1,0:T(8,128)(2,1)} %copy-done.18), calls=%async_computation.3 | async-start | bytes 2097152 | tf_op jit(solution)/shard_map/all_to_all | solution.py:493
  82.8 2.2 %copy-start.2 = (bf16[33,256,256]{2,1,0:T(8,128)(2,1)S(1)}, bf16[33,256,256]{2,1,0:T(8,128)(2,1)}, u32[]{:S(2)}) copy-start(bf16[33,256,256]{2,1,0:T(8,128)(2,1)} %constant.61.clone.fine_ref) | copy-start | bytes 12976132
  85.0 2.2 %copy-start.4 = (bf16[33,256,256]{2,1,0:T(8,128)(2,1)S(1)}, bf16[33,256,256]{2,1,0:T(8,128)(2,1)}, u32[]{:S(2)}) copy-start(bf16[33,256,256]{2,1,0:T(8,128)(2,1)} %constant.62.clone.inv_ref) | copy-start | bytes 12976132
  87.2 1.6 copy-start.14
  99.4 1.0 copy-start.17
  111.1 32.5 %all-to-all-start.2 = ((bf16[32,128,128]{2,1,0:T(8,128)(2,1)}), bf16[32,128,128]{2,1,0:T(8,128)(2,1)S(1)}, u32[]{:S(2)}, u32[]{:S(2)}) async-start(bf16[32,128,128]{2,1,0:T(8,128)(2,1)} %copy-done.17), calls=%async_computation.2 | async-start | bytes 2097152 | tf_op jit(solution)/shard_map/all_to_all | solution.py:493
  115.2 28.4 %copy-start.6 = (bf16[128,4096]{1,0:T(8,128)(2,1)S(1)}, bf16[128,4096]{1,0:T(8,128)(2,1)}, u32[]{:S(2)}) copy-start(bf16[128,4096]{1,0:T(8,128)(2,1)} %cot_ref.5) | copy-start | bytes 3145732
  115.3 1.3 copy-start.8
  116.6 1.2 copy-start.10
  124.5 0.7 copy-start.19
  124.5 5.9 %copy-start.23 = (bf16[8,4096]{1,0:T(8,128)(2,1)}, bf16[8,4096]{1,0:T(8,128)(2,1)S(1)}, u32[]{:S(2)}) copy-start(bf16[8,4096]{1,0:T(8,128)(2,1)S(1)} %get-tuple-element.42) | copy-start | bytes 196612
  125.8 2.0 %collective-permute-start.1 = (f32[6,1024]{1,0:T(8,128)}, f32[6,1024]{1,0:T(8,128)}, u32[]{:S(2)}, u32[]{:S(2)}) collective-permute-start(f32[6,1024]{1,0:T(8,128)} %get-tuple-element.54), channel_id=1, source_target_pairs={{0,1},{1,0},{2,3},{3,2},{4,5},{5,4},{6,7},{7,6},{8,9},{9,8},{10,11... | collective-permute-start | bytes 73736 | tf_op jit(solution)/shard_map/ppermute | solution.py:479
  126.0 4.3 %collective-permute-start.2 = (f32[6,1024]{1,0:T(8,128)}, f32[6,1024]{1,0:T(8,128)}, u32[]{:S(2)}, u32[]{:S(2)}) collective-permute-start(f32[6,1024]{1,0:T(8,128)} %get-tuple-element.53), channel_id=1, source_target_pairs={{0,16},{1,17},{2,18},{3,19},{4,20},{5,21},{6,22},{7,23},{8,24},{9,... | collective-permute-start | bytes 73736 | tf_op jit(solution)/shard_map/ppermute | solution.py:479
  127.7 3.9 %collective-permute-start.3 = (f32[6,1024]{1,0:T(8,128)}, f32[6,1024]{1,0:T(8,128)}, u32[]{:S(2)}, u32[]{:S(2)}) collective-permute-start(f32[6,1024]{1,0:T(8,128)} %get-tuple-element.52), channel_id=1, source_target_pairs={{0,17},{1,16},{2,19},{3,18},{4,21},{5,20},{6,23},{7,22},{8,25},{9,... | collective-permute-start | bytes 73736 | tf_op jit(solution)/shard_map/ppermute | solution.py:479
  145.2 0.7 copy-start.16
  145.9 19.1 %all-to-all-start.4 = ((bf16[32,40,128]{2,1,0:T(8,128)(2,1)}), bf16[32,40,128]{2,1,0:T(8,128)(2,1)}, u32[]{:S(2)}, u32[]{:S(2)}) async-start(bf16[32,40,128]{2,1,0:T(8,128)(2,1)} %copy-done.16), calls=%async_computation.4 | async-start | bytes 655360 | tf_op jit(solution)/shard_map/all_to_all | solution.py:493
  150.5 4.6 %collective-permute-start.5 = (bf16[8,4096]{1,0:T(8,128)(2,1)}, bf16[8,4096]{1,0:T(8,128)(2,1)S(1)}, u32[]{:S(2)}, u32[]{:S(2)}) collective-permute-start(bf16[8,4096]{1,0:T(8,128)(2,1)} %copy-done.23), channel_id=1, source_target_pairs={{1,0},{2,1},{3,2},{4,3},{5,4},{6,5},{7,6},{8,7},{9,8},{10,9},{11,1... | collective-permute-start | bytes 196616 | tf_op jit(solution)/shard_map/ppermute | solution.py:561
  153.8 3.8 %collective-permute-start.4 = (bf16[8,4096]{1,0:T(8,128)(2,1)S(1)}, bf16[8,4096]{1,0:T(8,128)(2,1)S(1)}, u32[]{:S(2)}, u32[]{:S(2)}) collective-permute-start(bf16[8,4096]{1,0:T(8,128)(2,1)S(1)} %get-tuple-element.39), channel_id=1, source_target_pairs={{1,0},{2,1},{3,2},{4,3},{5,4},{6,5},{7,6},{8,7},{9,8},{10,9},{11,1... | collective-permute-start | bytes 196616 | tf_op jit(solution)/shard_map/ppermute | solution.py:580
  166.1 3.8 %collective-permute-start.8 = (f32[72,128]{1,0:T(8,128)S(1)}, f32[72,128]{1,0:T(8,128)S(1)}, u32[]{:S(2)}, u32[]{:S(2)}) collective-permute-start(f32[72,128]{1,0:T(8,128)S(1)} %packet_sums.1), channel_id=1, source_target_pairs={{0,17},{1,16},{2,19},{3,18},{4,21},{5,20},{6,23},{7,22},{8,25},{9,... | collective-permute-start | bytes 110600 | tf_op jit(solution)/shard_map/ppermute | solution.py:479
  167.2 4.0 %collective-permute-start.7 = (f32[72,128]{1,0:T(8,128)S(1)}, f32[72,128]{1,0:T(8,128)S(1)}, u32[]{:S(2)}, u32[]{:S(2)}) collective-permute-start(f32[72,128]{1,0:T(8,128)S(1)} %packet_sums.1), channel_id=1, source_target_pairs={{0,16},{1,17},{2,18},{3,19},{4,20},{5,21},{6,22},{7,23},{8,24},{9,... | collective-permute-start | bytes 110600 | tf_op jit(solution)/shard_map/ppermute | solution.py:479
  167.7 3.5 %collective-permute-start.6 = (f32[72,128]{1,0:T(8,128)S(1)}, f32[72,128]{1,0:T(8,128)S(1)}, u32[]{:S(2)}, u32[]{:S(2)}) collective-permute-start(f32[72,128]{1,0:T(8,128)S(1)} %packet_sums.1), channel_id=1, source_target_pairs={{0,1},{1,0},{2,3},{3,2},{4,5},{5,4},{6,7},{7,6},{8,9},{9,8},{10,11... | collective-permute-start | bytes 110600 | tf_op jit(solution)/shard_map/ppermute | solution.py:479
